TPU v7x, 512 devices: a whole 4x4x16 slice. The times are simulated.
512 devices in a mesh: ctx: 64 (over x, z), tp: 8 (over y, core).
Axes of the slice: x: 4, y: 4, z: 16, core: 2. Of those that a mesh axis runs over, the one named last changes fastest.
Arguments:
- queries: bfloat16 [12288, 8192], P('ctx', 'tp'), may hold values from -16 to 16
- keys: bfloat16 [12288, 1024], P('ctx', 'tp'), may hold values from -4 to 4
- values: bfloat16 [12288, 1024], P('ctx', 'tp'), may hold values from -5 to 5
- lengths: int32 [64], replicated, may hold values from 1 to 192, 9216 in all
- page_owner: int32 [6144, 1], P('ctx'), may hold values from 0 to 63; in each aligned block of 96 rows (0 to 95, 96 to 191, ...) at most 2 rows name the same one
Outputs:
- attended: bfloat16 [12288, 8192], P('ctx', 'tp')
- decode_cache: bfloat16 [64, 128, 2, 8, 256], P('ctx', 'tp')
Inputs may be any that keep to these rules, and one draw needn't show every extreme that they name: The lengths sum to 9216; the largest is exactly 192. `page_owner`: among the pages of one index of ctx no owner is named more than 2 times.
All inputs are finite; a program needn't handle non-finite values.
Results may differ from a plain program's by a relative error of at most 0.0065.
Values may be sent and summed in bfloat16 or wider, within the bound.
No kernel may reach another device: no remote copies, remote signals or barrier semaphores. Data moves between devices by JAX's collectives and lax.ppermute only.
A program may use at most 64 MiB of HBM per device.

v0:
```python
import math

import jax
import jax.numpy as jnp
from jax import lax
from jax.sharding import PartitionSpec as P

HD = 128
PAGE = 2


def table_lookup(source, table):
    match = source[:, None] == jnp.arange(table.shape[0], dtype=jnp.int32)[None, :]
    return jnp.sum(jnp.where(match, table[None, :], 0), axis=1)


def attend(block_q, q_pos, q_ok, keys, values, offsets, lengths):
    cap = keys.shape[0]
    kv_heads = keys.shape[1] // HD
    group = block_q.shape[1] // HD // kv_heads
    count_rows = block_q.shape[0]
    scale = 1.0 / math.sqrt(HD)
    q_view = block_q.reshape(count_rows, kv_heads, group, HD)
    last_pos = jnp.max(jnp.where(q_ok, q_pos, -1))
    start_state = (
        jnp.full((count_rows, kv_heads, group), -1e30, jnp.float32),
        jnp.zeros((count_rows, kv_heads, group), jnp.float32),
        jnp.zeros((count_rows, kv_heads, group, HD), jnp.float32),
    )

    def update(state, key_block, value_block, k_pos, k_ok):
        width = key_block.shape[0]
        running, total, accum = state
        scores = (
            jnp.einsum(
                "rhgd,khd->rhgk",
                q_view,
                key_block.reshape(width, kv_heads, HD),
                preferred_element_type=jnp.float32,
            )
            * scale
        )
        allowed = ((k_pos[None, :] <= q_pos[:, None]) & k_ok[None, :])[:, None, None, :]
        newest = jnp.maximum(running, jnp.max(jnp.where(allowed, scores, -1e30), axis=-1))
        weights = jnp.where(allowed, jnp.exp(scores - newest[..., None]), 0.0)
        factor = jnp.exp(running - newest)
        total = total * factor + jnp.sum(weights, axis=-1)
        accum = accum * factor[..., None] + jnp.einsum(
            "rhgk,khd->rhgd",
            weights.astype(jnp.bfloat16),
            value_block.reshape(width, kv_heads, HD),
            preferred_element_type=jnp.float32,
        )
        return (newest, total, accum)

    state = start_state
    key_piece = lax.all_gather(keys, "ctx", axis=0, tiled=True)
    value_piece = lax.all_gather(values, "ctx", axis=0, tiled=True)
    count = key_piece.shape[0]
    width = math.gcd(count, 768)
    steps_count = count // width
    key_blocks = key_piece.reshape(steps_count, width, key_piece.shape[1])
    value_blocks = value_piece.reshape(steps_count, width, value_piece.shape[1])

    def one_block(carry, items):
        key_block, value_block, block_number = items
        global_rows = block_number * width + jnp.arange(width, dtype=jnp.int32)
        source = global_rows // cap
        local = global_rows - source * cap
        k_pos = table_lookup(source, offsets) + local
        k_ok = local < table_lookup(source, lengths)
        carry = lax.cond(
            jnp.min(k_pos) <= last_pos,
            lambda inner: update(inner, key_block, value_block, k_pos, k_ok),
            lambda inner: inner,
            carry,
        )
        return (carry, None)

    state, unused = lax.scan(
        one_block, state, (key_blocks, value_blocks, jnp.arange(steps_count, dtype=jnp.int32))
    )
    running, total, accum = state
    safe = jnp.where(q_ok[:, None, None], total, 1.0)
    result = jnp.where(q_ok[:, None, None, None], accum / safe[..., None], 0.0)
    return result.reshape(count_rows, block_q.shape[1]).astype(jnp.bfloat16)


def body(queries, keys, values, lengths, page_owner):
    cap = queries.shape[0]
    kv_heads = keys.shape[1] // HD
    ctx_count = lax.axis_size("ctx")
    myself = lax.axis_index("ctx")
    offsets = jnp.cumsum(lengths) - lengths
    rows = jnp.arange(cap, dtype=jnp.int32)
    my_offset = offsets[myself]
    my_length = lengths[myself]
    attended = attend(queries, my_offset + rows, rows < my_length, keys, values, offsets, lengths)
    page_count = cap // PAGE
    slot_count = max(2, (page_count + ctx_count - 1) // ctx_count)
    page_index = jnp.arange(page_count, dtype=jnp.int32)
    finished = (page_index + 1) * PAGE <= my_length
    paged = jnp.concatenate(
        [
            keys.reshape(page_count, PAGE, kv_heads, HD),
            values.reshape(page_count, PAGE, kv_heads, HD),
        ],
        axis=-1,
    )
    paged = jnp.where(finished[:, None, None, None], paged, jnp.zeros_like(paged))
    owner = page_owner[:, 0]
    same = owner[:, None] == owner[None, :]
    earlier = page_index[None, :] < page_index[:, None]
    rank = jnp.sum((same & earlier).astype(jnp.int32), axis=1)
    slot = owner * slot_count + rank
    select = (slot[None, :] == jnp.arange(ctx_count * slot_count, dtype=jnp.int32)[:, None]).astype(
        jnp.bfloat16
    )
    outgoing = jnp.dot(
        select,
        paged.reshape(page_count, PAGE * kv_heads * 2 * HD),
        preferred_element_type=jnp.float32,
    )
    outgoing = outgoing.astype(jnp.bfloat16).reshape(ctx_count * slot_count, PAGE, kv_heads, 2 * HD)
    decode_cache = lax.all_to_all(
        lax.all_to_all(outgoing, "ctx", split_axis=0, concat_axis=0, tiled=True),
        "tp",
        split_axis=0,
        concat_axis=2,
        tiled=True,
    )
    return (attended, decode_cache.reshape((1,) + decode_cache.shape))


def solution(mesh):
    in_specs = (P("ctx", "tp"), P("ctx", "tp"), P("ctx", "tp"), P(), P("ctx", None))
    out_specs = (P("ctx", "tp"), P("ctx", "tp", None, None, None))
    return jax.shard_map(body, mesh=mesh, in_specs=in_specs, out_specs=out_specs, check_vma=False)
```

profile of v0, /device:TPU:502, one launch (start us, length us, event | category | flops | bytes accessed | tf_op | source)
XLA Modules:
  0.0 476.1 jit_solution(4822909542297005606)
XLA Ops:
  13.4 25.0 %all_to_all.20 = bf16[128,2,1,256]{3,1,2,0:T(2,128)(2,1)} all-to-all(bf16[128,2,1,256]{3,1,2,0:T(2,128)(2,1)S(1)} %bitcast.96), channel_id=1, replica_groups=mesh['ctx'=64,'tp'=8] {'ctx'}, dimensions={0} | all-to-all | bytes 262144 | tf_op jit(solution)/shard_map/all_to_all | solution.py:126
  38.3 4.8 %all-to-all-start.1 = ((bf16[128,2,1,256]{3,1,2,0:T(2,128)(2,1)}), bf16[128,2,1,256]{3,1,2,0:T(2,128)(2,1)S(1)}, u32[]{:S(2)}, u32[]{:S(2)}) async-start(bf16[128,2,1,256]{3,1,2,0:T(2,128)(2,1)} %all_to_all.20), calls=%async_computation.1 | async-start | bytes 262144 | tf_op jit(solution)/shard_map/all_to_all | solution.py:125
  49.7 100.1 %all-gather.3.cloned.1.call-done = bf16[12288,128]{1,0:T(8,128)(2,1)} async-done(((bf16[192,128]{1,0:T(8,128)(2,1)}), bf16[12288,128]{1,0:T(8,128)(2,1)}) %all-gather.3.cloned.1.call-update) | async-done | bytes 3145744 | tf_op jit(solution)/shard_map/all_gather | solution.py:57
  149.8 141.4 %all-gather.5.cloned.1.call-done = bf16[12288,128]{1,0:T(8,128)(2,1)} async-done(((bf16[192,128]{1,0:T(8,128)(2,1)}), bf16[12288,128]{1,0:T(8,128)(2,1)}) %all-gather.5.cloned.1.call-update) | async-done | bytes 3145744 | tf_op jit(solution)/shard_map/all_gather | solution.py:58
  291.2 176.6 %while.17 = (s32[]{:T(128)}, f32[192,1,8]{0,2,1:T(8,128)S(1)}, f32[192,1,8]{0,2,1:T(8,128)S(1)}, f32[192,1,8,128]{3,0,2,1:T(8,128)S(1)}, s32[16]{0:T(128)S(1)}, ...) while((s32[]{:T(128)}, f32[192,1,8]{0,2,1:T(8,128)S(1)}, ...), condition=%wide.region_10.11_spmd.clone, body=%wide.region_2.10_spmd.clone.sunk | while | flops 617961408 | bytes 17735024 | solution.py:80
  294.9 7.4 %conditional.3 = ((f32[192,1,8]{0,2,1:T(8,128)S(1)}, f32[192,1,8]{0,2,1:T(8,128)S(1)}, f32[192,1,8,128]{3,0,2,1:T(8,128)S(1)})) conditional(s32[]{:T(128)} %convert_element_type.40, (f32[192,1,8]{0,2,1:T(8,128)S(1)}, f32[192,1,8]{0,2,1:T(8,128)S(1)}, f32[192,1,8,128]{3,0,2,1:T(8,128)S(1)}) %tuple.62, (s32[768]{0:T(1024)S(1)}, s32[]{:T(128)}, ...), branch_computations={%region_5.5_spmd, %region_6.9_spmd} | conditional | flops 617747136 | bytes 17466404 | solution.py:72
  299.9 2.4 fusion.14
  305.9 7.4 %conditional.3 = ((f32[192,1,8]{0,2,1:T(8,128)S(1)}, f32[192,1,8]{0,2,1:T(8,128)S(1)}, f32[192,1,8,128]{3,0,2,1:T(8,128)S(1)})) conditional(s32[]{:T(128)} %convert_element_type.40, (f32[192,1,8]{0,2,1:T(8,128)S(1)}, f32[192,1,8]{0,2,1:T(8,128)S(1)}, f32[192,1,8,128]{3,0,2,1:T(8,128)S(1)}) %tuple.62, (s32[768]{0:T(1024)S(1)}, s32[]{:T(128)}, ...), branch_computations={%region_5.5_spmd, %region_6.9_spmd} | conditional | flops 617747136 | bytes 17466404 | solution.py:72
  310.9 2.4 fusion.14
  317.0 7.4 %conditional.3 = ((f32[192,1,8]{0,2,1:T(8,128)S(1)}, f32[192,1,8]{0,2,1:T(8,128)S(1)}, f32[192,1,8,128]{3,0,2,1:T(8,128)S(1)})) conditional(s32[]{:T(128)} %convert_element_type.40, (f32[192,1,8]{0,2,1:T(8,128)S(1)}, f32[192,1,8]{0,2,1:T(8,128)S(1)}, f32[192,1,8,128]{3,0,2,1:T(8,128)S(1)}) %tuple.62, (s32[768]{0:T(1024)S(1)}, s32[]{:T(128)}, ...), branch_computations={%region_5.5_spmd, %region_6.9_spmd} | conditional | flops 617747136 | bytes 17466404 | solution.py:72
  321.9 2.4 fusion.14
  328.0 7.4 %conditional.3 = ((f32[192,1,8]{0,2,1:T(8,128)S(1)}, f32[192,1,8]{0,2,1:T(8,128)S(1)}, f32[192,1,8,128]{3,0,2,1:T(8,128)S(1)})) conditional(s32[]{:T(128)} %convert_element_type.40, (f32[192,1,8]{0,2,1:T(8,128)S(1)}, f32[192,1,8]{0,2,1:T(8,128)S(1)}, f32[192,1,8,128]{3,0,2,1:T(8,128)S(1)}) %tuple.62, (s32[768]{0:T(1024)S(1)}, s32[]{:T(128)}, ...), branch_computations={%region_5.5_spmd, %region_6.9_spmd} | conditional | flops 617747136 | bytes 17466404 | solution.py:72
  333.0 2.4 fusion.14
  339.1 7.4 %conditional.3 = ((f32[192,1,8]{0,2,1:T(8,128)S(1)}, f32[192,1,8]{0,2,1:T(8,128)S(1)}, f32[192,1,8,128]{3,0,2,1:T(8,128)S(1)})) conditional(s32[]{:T(128)} %convert_element_type.40, (f32[192,1,8]{0,2,1:T(8,128)S(1)}, f32[192,1,8]{0,2,1:T(8,128)S(1)}, f32[192,1,8,128]{3,0,2,1:T(8,128)S(1)}) %tuple.62, (s32[768]{0:T(1024)S(1)}, s32[]{:T(128)}, ...), branch_computations={%region_5.5_spmd, %region_6.9_spmd} | conditional | flops 617747136 | bytes 17466404 | solution.py:72
  344.0 2.4 fusion.14
  350.1 7.4 %conditional.3 = ((f32[192,1,8]{0,2,1:T(8,128)S(1)}, f32[192,1,8]{0,2,1:T(8,128)S(1)}, f32[192,1,8,128]{3,0,2,1:T(8,128)S(1)})) conditional(s32[]{:T(128)} %convert_element_type.40, (f32[192,1,8]{0,2,1:T(8,128)S(1)}, f32[192,1,8]{0,2,1:T(8,128)S(1)}, f32[192,1,8,128]{3,0,2,1:T(8,128)S(1)}) %tuple.62, (s32[768]{0:T(1024)S(1)}, s32[]{:T(128)}, ...), branch_computations={%region_5.5_spmd, %region_6.9_spmd} | conditional | flops 617747136 | bytes 17466404 | solution.py:72
  355.1 2.4 fusion.14
  361.1 7.4 %conditional.3 = ((f32[192,1,8]{0,2,1:T(8,128)S(1)}, f32[192,1,8]{0,2,1:T(8,128)S(1)}, f32[192,1,8,128]{3,0,2,1:T(8,128)S(1)})) conditional(s32[]{:T(128)} %convert_element_type.40, (f32[192,1,8]{0,2,1:T(8,128)S(1)}, f32[192,1,8]{0,2,1:T(8,128)S(1)}, f32[192,1,8,128]{3,0,2,1:T(8,128)S(1)}) %tuple.62, (s32[768]{0:T(1024)S(1)}, s32[]{:T(128)}, ...), branch_computations={%region_5.5_spmd, %region_6.9_spmd} | conditional | flops 617747136 | bytes 17466404 | solution.py:72
  372.2 7.4 %conditional.3 = ((f32[192,1,8]{0,2,1:T(8,128)S(1)}, f32[192,1,8]{0,2,1:T(8,128)S(1)}, f32[192,1,8,128]{3,0,2,1:T(8,128)S(1)})) conditional(s32[]{:T(128)} %convert_element_type.40, (f32[192,1,8]{0,2,1:T(8,128)S(1)}, f32[192,1,8]{0,2,1:T(8,128)S(1)}, f32[192,1,8,128]{3,0,2,1:T(8,128)S(1)}) %tuple.62, (s32[768]{0:T(1024)S(1)}, s32[]{:T(128)}, ...), branch_computations={%region_5.5_spmd, %region_6.9_spmd} | conditional | flops 617747136 | bytes 17466404 | solution.py:72
  377.1 2.4 fusion.14
  383.2 7.4 %conditional.3 = ((f32[192,1,8]{0,2,1:T(8,128)S(1)}, f32[192,1,8]{0,2,1:T(8,128)S(1)}, f32[192,1,8,128]{3,0,2,1:T(8,128)S(1)})) conditional(s32[]{:T(128)} %convert_element_type.40, (f32[192,1,8]{0,2,1:T(8,128)S(1)}, f32[192,1,8]{0,2,1:T(8,128)S(1)}, f32[192,1,8,128]{3,0,2,1:T(8,128)S(1)}) %tuple.62, (s32[768]{0:T(1024)S(1)}, s32[]{:T(128)}, ...), branch_computations={%region_5.5_spmd, %region_6.9_spmd} | conditional | flops 617747136 | bytes 17466404 | solution.py:72
  394.3 7.4 %conditional.3 = ((f32[192,1,8]{0,2,1:T(8,128)S(1)}, f32[192,1,8]{0,2,1:T(8,128)S(1)}, f32[192,1,8,128]{3,0,2,1:T(8,128)S(1)})) conditional(s32[]{:T(128)} %convert_element_type.40, (f32[192,1,8]{0,2,1:T(8,128)S(1)}, f32[192,1,8]{0,2,1:T(8,128)S(1)}, f32[192,1,8,128]{3,0,2,1:T(8,128)S(1)}) %tuple.62, (s32[768]{0:T(1024)S(1)}, s32[]{:T(128)}, ...), branch_computations={%region_5.5_spmd, %region_6.9_spmd} | conditional | flops 617747136 | bytes 17466404 | solution.py:72
  399.2 2.4 fusion.14
  405.3 7.4 %conditional.3 = ((f32[192,1,8]{0,2,1:T(8,128)S(1)}, f32[192,1,8]{0,2,1:T(8,128)S(1)}, f32[192,1,8,128]{3,0,2,1:T(8,128)S(1)})) conditional(s32[]{:T(128)} %convert_element_type.40, (f32[192,1,8]{0,2,1:T(8,128)S(1)}, f32[192,1,8]{0,2,1:T(8,128)S(1)}, f32[192,1,8,128]{3,0,2,1:T(8,128)S(1)}) %tuple.62, (s32[768]{0:T(1024)S(1)}, s32[]{:T(128)}, ...), branch_computations={%region_5.5_spmd, %region_6.9_spmd} | conditional | flops 617747136 | bytes 17466404 | solution.py:72
  416.3 7.4 %conditional.3 = ((f32[192,1,8]{0,2,1:T(8,128)S(1)}, f32[192,1,8]{0,2,1:T(8,128)S(1)}, f32[192,1,8,128]{3,0,2,1:T(8,128)S(1)})) conditional(s32[]{:T(128)} %convert_element_type.40, (f32[192,1,8]{0,2,1:T(8,128)S(1)}, f32[192,1,8]{0,2,1:T(8,128)S(1)}, f32[192,1,8,128]{3,0,2,1:T(8,128)S(1)}) %tuple.62, (s32[768]{0:T(1024)S(1)}, s32[]{:T(128)}, ...), branch_computations={%region_5.5_spmd, %region_6.9_spmd} | conditional | flops 617747136 | bytes 17466404 | solution.py:72
  421.3 2.4 fusion.14
  427.4 7.4 %conditional.3 = ((f32[192,1,8]{0,2,1:T(8,128)S(1)}, f32[192,1,8]{0,2,1:T(8,128)S(1)}, f32[192,1,8,128]{3,0,2,1:T(8,128)S(1)})) conditional(s32[]{:T(128)} %convert_element_type.40, (f32[192,1,8]{0,2,1:T(8,128)S(1)}, f32[192,1,8]{0,2,1:T(8,128)S(1)}, f32[192,1,8,128]{3,0,2,1:T(8,128)S(1)}) %tuple.62, (s32[768]{0:T(1024)S(1)}, s32[]{:T(128)}, ...), branch_computations={%region_5.5_spmd, %region_6.9_spmd} | conditional | flops 617747136 | bytes 17466404 | solution.py:72
  438.4 7.4 %conditional.3 = ((f32[192,1,8]{0,2,1:T(8,128)S(1)}, f32[192,1,8]{0,2,1:T(8,128)S(1)}, f32[192,1,8,128]{3,0,2,1:T(8,128)S(1)})) conditional(s32[]{:T(128)} %convert_element_type.40, (f32[192,1,8]{0,2,1:T(8,128)S(1)}, f32[192,1,8]{0,2,1:T(8,128)S(1)}, f32[192,1,8,128]{3,0,2,1:T(8,128)S(1)}) %tuple.62, (s32[768]{0:T(1024)S(1)}, s32[]{:T(128)}, ...), branch_computations={%region_5.5_spmd, %region_6.9_spmd} | conditional | flops 617747136 | bytes 17466404 | solution.py:72
  443.4 2.4 fusion.14
  449.5 7.4 %conditional.3 = ((f32[192,1,8]{0,2,1:T(8,128)S(1)}, f32[192,1,8]{0,2,1:T(8,128)S(1)}, f32[192,1,8,128]{3,0,2,1:T(8,128)S(1)})) conditional(s32[]{:T(128)} %convert_element_type.40, (f32[192,1,8]{0,2,1:T(8,128)S(1)}, f32[192,1,8]{0,2,1:T(8,128)S(1)}, f32[192,1,8,128]{3,0,2,1:T(8,128)S(1)}) %tuple.62, (s32[768]{0:T(1024)S(1)}, s32[]{:T(128)}, ...), branch_computations={%region_5.5_spmd, %region_6.9_spmd} | conditional | flops 617747136 | bytes 17466404 | solution.py:72
  460.5 7.4 %conditional.3 = ((f32[192,1,8]{0,2,1:T(8,128)S(1)}, f32[192,1,8]{0,2,1:T(8,128)S(1)}, f32[192,1,8,128]{3,0,2,1:T(8,128)S(1)})) conditional(s32[]{:T(128)} %convert_element_type.40, (f32[192,1,8]{0,2,1:T(8,128)S(1)}, f32[192,1,8]{0,2,1:T(8,128)S(1)}, f32[192,1,8,128]{3,0,2,1:T(8,128)S(1)}) %tuple.62, (s32[768]{0:T(1024)S(1)}, s32[]{:T(128)}, ...), branch_computations={%region_5.5_spmd, %region_6.9_spmd} | conditional | flops 617747136 | bytes 17466404 | solution.py:72
  465.5 2.4 fusion.14
  (293 shorter events, 133.2 us)
Async XLA Ops:
  7.2 142.6 %all-gather.3.cloned.1.call-start = ((), (), s32[]{:S(2)}) async-start(), calls=%async_computation.2 | async-start | bytes 3194880 | tf_op jit(solution)/shard_map/all_gather | solution.py:57
  7.9 283.3 %all-gather.5.cloned.1.call-start = ((), (), s32[]{:S(2)}) async-start(), calls=%async_computation.3 | async-start | bytes 3194880 | tf_op jit(solution)/shard_map/all_gather | solution.py:58
  38.3 10.6 %all-to-all-start.1 = ((bf16[128,2,1,256]{3,1,2,0:T(2,128)(2,1)}), bf16[128,2,1,256]{3,1,2,0:T(2,128)(2,1)S(1)}, u32[]{:S(2)}, u32[]{:S(2)}) async-start(bf16[128,2,1,256]{3,1,2,0:T(2,128)(2,1)} %all_to_all.20), calls=%async_computation.1 | async-start | bytes 262144 | tf_op jit(solution)/shard_map/all_to_all | solution.py:125
Sparse Core Ops, SparseCore 0:
  10.9 138.7 all-gather.2
  152.7 138.3 all-gather.4
where the time goes:
time: 479 us; the launch traced here: 476 us
  waiting for transfers between devices  243 us (51%)
  other arithmetic  71.6 us (15%)
  matrix products  70.5 us (15%)
  loops' own time  31.3 us (7%)
  blocking collectives  25 us (5%)
  local copies, waits for them, and re-layouts  15.9 us (3%)
  between operations  14.2 us (3%)
  starting transfers between devices  4.88 us (1%)
    all_gather x1, waiting for transfers between devices, attend(): value_piece = lax.all_gather(values, 'ctx', axis=0, tiled=True)  141 us
    all_gather x1, waiting for transfers between devices, attend(): key_piece = lax.all_gather(keys, 'ctx', axis=0, tiled=True)  100 us
    dot_general x16, matrix products, update(): jnp.einsum('rhgk,khd->rhgd', weights.astype(jnp.bfloat16), value_block.re...  38.2 us
    dot_general x16, matrix products, update(): jnp.einsum('rhgd,khd->rhgk', q_view, key_block.reshape(width, kv_heads, H...  32 us
    another operation x1, loops' own time, attend(): lax.scan(one_block, state, (key_blocks, value_blocks, jnp.arange(steps_co...  30.2 us
    all_to_all x1, blocking collectives, body(): lax.all_to_all(outgoing, 'ctx', split_axis=0, concat_axis=0, tiled=True)  25 us
    reduce_sum x16, other arithmetic, update(): total = total * factor + jnp.sum(weights, axis=-1)  21.5 us
    reduce_sum x32, other arithmetic, table_lookup(): return jnp.sum(jnp.where(match, table[None, :], 0), axis=1)  18.1 us
  transfers between devices with their start and end apart: 3, of which 2 were waited for; matrix products, arithmetic and copies ran while one was open for 2% of the time, Pallas kernels for 0%

commit v1 on v0

v1 whole, which is shorter than its diff:
```python
import functools
import math

import jax
import jax.numpy as jnp
from jax import lax
from jax.experimental import pallas as pl
from jax.experimental.pallas import tpu as pltpu
from jax.sharding import PartitionSpec as P

HD = 128
PAGE = 2
NX = 4
NZ = 16
N = NX * NZ
CAP = 192
HALF = CAP // 2
PAGES = CAP // PAGE
HALF_PAGES = PAGES // 2
ROWS_A = 2 * HALF
ROWS_B = 2 * HALF + 16
GROUP = 8
BLOCK = 8
WIDTH = BLOCK * HALF
BLOCKS = 2 * N // BLOCK
NEG = -1e30

X_GROUPS = [[x * NZ + z for x in range(NX)] for z in range(NZ)]
Z_GROUPS = [[x * NZ + z for z in range(NZ)] for x in range(NX)]


def shift(value, dx, dz):
    pairs = [
        (x * NZ + z, ((x + dx) % NX) * NZ + (z + dz) % NZ) for x in range(NX) for z in range(NZ)
    ]
    return lax.ppermute(value, "ctx", pairs)


def attention_kernel(n_ref, q_ref, k_ref, v_ref, bias_ref, *refs):
    sources, (out_ref, qs, kv, m, l, acc, sems) = refs[:6], refs[6:]
    copies = []
    start = 0
    for i, source in enumerate(sources):
        count, rows = source.shape[0], source.shape[1]
        copies.append(
            pltpu.make_async_copy(
                source, kv.at[pl.ds(start, count), pl.ds(0, rows)], sems.at[i]
            )
        )
        start += count
    for copy in copies:
        copy.start()
    scale = math.log2(math.e) / math.sqrt(HD)
    live = n_ref[0]

    for h in range(GROUP):
        qs[h] = q_ref[:, h * HD : (h + 1) * HD]

    row = lax.broadcasted_iota(jnp.int32, (CAP, CAP), 0)
    col = lax.broadcasted_iota(jnp.int32, (CAP, CAP), 1)
    own_bias = jnp.where((col <= row) & (col < live), 0.0, NEG).astype(jnp.float32)
    keys = k_ref[...]
    values = v_ref[...]

    def scores(h, keys, bias):
        s = lax.dot_general(
            qs[h], keys, (((1,), (1,)), ((), ())), preferred_element_type=jnp.float32
        )
        return s * scale + bias

    def own(h, carry):
        s = scores(h, keys, own_bias)
        top = jnp.max(s, axis=1, keepdims=True)
        p = jnp.exp2(s - top)
        m[h] = jnp.broadcast_to(top, (CAP, HD))
        l[h] = jnp.broadcast_to(jnp.sum(p, axis=1, keepdims=True), (CAP, HD))
        acc[h] = jnp.dot(p.astype(jnp.bfloat16), values, preferred_element_type=jnp.float32)
        return carry

    lax.fori_loop(0, GROUP, own, 0)

    for copy in copies:
        copy.wait()

    def block(b, carry):
        def head(h, inner):
            first = pl.multiple_of(b * BLOCK, BLOCK)
            k = kv[pl.ds(first, BLOCK), 0:HALF, :].reshape(WIDTH, HD)
            v = kv[pl.ds(first, BLOCK), HALF : 2 * HALF, :].reshape(WIDTH, HD)
            s = scores(h, k, bias_ref[b])
            old = m[h][:, :1]
            top = jnp.maximum(old, jnp.max(s, axis=1, keepdims=True))
            p = jnp.exp2(s - top)
            factor = jnp.exp2(old - top)
            m[h] = jnp.broadcast_to(top, (CAP, HD))
            l[h] = l[h] * factor + jnp.sum(p, axis=1, keepdims=True)
            acc[h] = acc[h] * factor + jnp.dot(
                p.astype(jnp.bfloat16), v, preferred_element_type=jnp.float32
            )
            return inner

        return lax.fori_loop(0, GROUP, head, carry, unroll=2)

    lax.fori_loop(0, BLOCKS, block, 0)

    ok = lax.broadcasted_iota(jnp.int32, (CAP, HD), 0) < live
    for h in range(GROUP):
        result = jnp.where(ok, acc[h] / l[h], 0.0)
        out_ref[:, h * HD : (h + 1) * HD] = result.astype(jnp.bfloat16)


def attention(live, queries, keys, values, bias, sources):
    vmem = pl.BlockSpec(memory_space=pltpu.VMEM)
    return pl.pallas_call(
        attention_kernel,
        out_shape=jax.ShapeDtypeStruct(queries.shape, jnp.bfloat16),
        in_specs=[pl.BlockSpec(memory_space=pltpu.SMEM)]
        + [vmem] * 4
        + [pl.BlockSpec(memory_space=pl.ANY)] * len(sources),
        out_specs=vmem,
        scratch_shapes=[
            pltpu.VMEM((GROUP, CAP, HD), jnp.bfloat16),
            pltpu.VMEM((2 * N, ROWS_B, HD), jnp.bfloat16),
            pltpu.VMEM((GROUP, CAP, HD), jnp.float32),
            pltpu.VMEM((GROUP, CAP, HD), jnp.float32),
            pltpu.VMEM((GROUP, CAP, HD), jnp.float32),
            pltpu.SemaphoreType.DMA((len(sources),)),
        ],
        compiler_params=pltpu.CompilerParams(vmem_limit_bytes=40 * 1024 * 1024),
        cost_estimate=pl.CostEstimate(
            flops=4 * GROUP * CAP * N * CAP * HD, bytes_accessed=8 << 20, transcendentals=0
        ),
    )(live, queries, keys, values, bias, *sources)


def select_kernel(sel_ref, *refs):
    sources, (out_ref, pages, sems) = refs[:6], refs[6:]
    copies = []
    start = 0
    for i, source in enumerate(sources):
        count = source.shape[0]
        copies.append(
            pltpu.make_async_copy(source, pages.at[pl.ds(start, count)], sems.at[i])
        )
        start += count
    for copy in copies:
        copy.start()
    for copy in copies:
        copy.wait()

    def one(s, carry):
        place = sel_ref[s]
        found = jnp.maximum(place, 0)
        keep = jnp.where(place >= 0, 1.0, 0.0).astype(jnp.bfloat16)
        out_ref[s, :, 0:HD] = pages[found] * keep
        out_ref[s, :, HD : 2 * HD] = pages[found + HALF_PAGES] * keep
        return carry

    lax.fori_loop(0, 2 * N, one, 0, unroll=4)


def select_pages(sel, sources):
    total = sum(s.shape[0] for s in sources)
    return pl.pallas_call(
        select_kernel,
        out_shape=jax.ShapeDtypeStruct((2 * N, PAGE, 2 * HD), jnp.bfloat16),
        in_specs=[pl.BlockSpec(memory_space=pltpu.SMEM)]
        + [pl.BlockSpec(memory_space=pl.ANY)] * len(sources),
        out_specs=pl.BlockSpec(memory_space=pltpu.VMEM),
        scratch_shapes=[
            pltpu.VMEM((total, PAGE, HD), jnp.bfloat16),
            pltpu.SemaphoreType.DMA((len(sources),)),
        ],
        compiler_params=pltpu.CompilerParams(vmem_limit_bytes=40 * 1024 * 1024),
        cost_estimate=pl.CostEstimate(flops=0, bytes_accessed=8 << 20, transcendentals=0),
    )(sel, *sources)


def body(queries, keys, values, lengths, page_owner):
    me = lax.axis_index("ctx")
    mx, mz = me // NZ, me % NZ
    my_length = jnp.sum(jnp.where(jnp.arange(N, dtype=jnp.int32) == me, lengths, 0))

    page_index = jnp.arange(PAGES, dtype=jnp.int32)
    owner = page_owner[:, 0]
    same = owner[:, None] == owner[None, :]
    earlier = page_index[None, :] < page_index[:, None]
    rank = jnp.sum((same & earlier).astype(jnp.int32), axis=1)
    finished = (page_index + 1) * PAGE <= my_length
    slot = jnp.where(finished, owner * 2 + rank, -1)
    table = jnp.sum(
        jnp.where(
            slot[:, None] == jnp.arange(2 * N, dtype=jnp.int32)[None, :],
            page_index[:, None] + 1,
            0,
        ),
        axis=0,
    ).astype(jnp.bfloat16)

    a = jnp.concatenate([keys[:HALF], values[:HALF]], axis=0)
    b = jnp.concatenate(
        [keys[HALF:], values[HALF:], jnp.broadcast_to(table[None, :], (16, 2 * N))], axis=0
    )

    a = lax.all_gather(a, "ctx", axis=0, tiled=False, axis_index_groups=X_GROUPS)
    a = lax.all_gather(a, "ctx", axis=0, tiled=False, axis_index_groups=Z_GROUPS)
    a = a.reshape(N, ROWS_A, HD)

    up, down = [b], [b]
    for k in range(8):
        up.append(shift(up[-1], 0, 1))
        if k < 7:
            down.append(shift(down[-1], 0, -1))
    b0 = jnp.stack(up + down[1:])
    from_left = shift(b0, 1, 0)
    from_right = shift(b0, -1, 0)
    far_left = shift(from_left[:8], 1, 0)
    far_right = shift(from_right[8:], -1, 0)
    sources = [a, b0, from_left, from_right, far_left, far_right]

    order_z = [-k for k in range(9)] + list(range(1, 8))
    delta_z = jnp.array(order_z * NX, jnp.int32)
    delta_x = jnp.array([0] * NZ + [-1] * NZ + [1] * NZ + [2] * NZ, jnp.int32)
    piece_b = ((mx + delta_x) % NX) * NZ + (mz + delta_z) % NZ
    place = jnp.arange(N, dtype=jnp.int32)
    piece_a = (place % NX) * NZ + place // NX
    piece = jnp.concatenate([piece_a, piece_b])
    base = jnp.concatenate([jnp.zeros((N,), jnp.int32), jnp.full((N,), HALF, jnp.int32)])
    sizes = jnp.sum(jnp.where(piece[:, None] == place[None, :], lengths[None, :], 0), axis=1)
    count = jnp.where(piece < me, sizes - base, 0)
    bias = jnp.where(
        jnp.arange(HALF, dtype=jnp.int32)[None, :] < count[:, None], 0.0, NEG
    ).astype(jnp.float32)
    bias = bias.reshape(BLOCKS, 1, WIDTH)

    tables = jnp.concatenate([s[:, ROWS_A, :] for s in sources[1:]], axis=0)
    codes = lax.dynamic_slice(tables, (0, me * 2), (N, 2)).astype(jnp.int32)
    hit = piece_b[:, None] == place[None, :]
    code = jnp.sum(jnp.where(hit[:, :, None], codes[:, None, :], 0), axis=0)
    place_b = jnp.sum(jnp.where(hit, place[:, None], 0), axis=0)
    place_a = (place % NZ) * NX + place // NZ
    page = code - 1
    pages_a, pages_b = ROWS_A // PAGE, ROWS_B // PAGE
    at_a = place_a[:, None] * pages_a + page
    at_b = N * pages_a + place_b[:, None] * pages_b + page - HALF_PAGES
    sel = jnp.where(page < 0, -1, jnp.where(page < HALF_PAGES, at_a, at_b)).reshape(2 * N)

    outgoing = select_pages(
        sel, [s.reshape(s.shape[0] * s.shape[1] // PAGE, PAGE, HD) for s in sources]
    )
    decode_cache = lax.all_to_all(
        outgoing.reshape(2 * N, PAGE, 1, 2 * HD), "tp", split_axis=0, concat_axis=2, tiled=True
    )
    attended = attention(my_length.reshape(1), queries, keys, values, bias, sources)
    return (attended, decode_cache.reshape((1,) + decode_cache.shape))


def solution(mesh):
    in_specs = (P("ctx", "tp"), P("ctx", "tp"), P("ctx", "tp"), P(), P("ctx", None))
    out_specs = (P("ctx", "tp"), P("ctx", "tp", None, None, None))
    return jax.shard_map(body, mesh=mesh, in_specs=in_specs, out_specs=out_specs, check_vma=False)
```

time: 479 us -> 242 us (0.51)
  the two profiles are of different devices: /device:TPU:502 before, /device:TPU:1 now
where the time goes in v1:
time: 242 us; the launch traced here: 241 us
  starting transfers between devices  83.8 us (35%)
  Pallas kernels  83.3 us (34%)
  local copies, waits for them, and re-layouts  22.9 us (9%)
  waiting for transfers between devices  15.7 us (6%)
  between operations  14.6 us (6%)
  blocking collectives  11.2 us (5%)
  other arithmetic  9.3 us (4%)
    pallas_call x1, Pallas kernels, attention(): pl.pallas_call(attention_kernel, out_shape=jax.ShapeDtypeStruct(queries.s...  80.1 us
    ppermute x19, starting transfers between devices, shift(): return lax.ppermute(value, 'ctx', pairs)  68.3 us
    ppermute x19, waiting for transfers between devices, shift(): return lax.ppermute(value, 'ctx', pairs)  15.7 us
    unnamed x54, local copies, waits for them, and re-layouts  15.6 us
    all_to_all x1, starting transfers between devices, body(): lax.all_to_all(outgoing.reshape(2 * N, PAGE, 1, 2 * HD), 'tp', split_axis...  15.5 us
    all_gather x1, blocking collectives, body(): lax.all_gather(a, 'ctx', axis=0, tiled=False, axis_index_groups=X_GROUPS)  11.2 us
  transfers between devices with their start and end apart: 21, of which 8 were waited for; matrix products, arithmetic and copies ran while one was open for 6% of the time, Pallas kernels for 33%

profile of v1, /device:TPU:1, one launch (start us, length us, event | category | flops | bytes accessed | tf_op | source)
XLA Modules:
  0.0 240.8 jit_solution(13049074705312771336)
XLA Ops:
  8.0 11.2 %all-gather = bf16[768,128]{1,0:T(8,128)(2,1)} all-gather(bf16[192,128]{1,0:T(8,128)(2,1)S(1)} %pad_maximum_fusion.1), channel_id=2, replica_groups={{0,128,256,384},{8,136,264,392},{16,144,272,400},{24,152,280,408},{32,1..., dimensions={0}, use_global_device_ids=true | all-gather | bytes 245760 | tf_op jit(solution)/shard_map/all_gather | solution.py:205
  20.1 1.3 fusion.12
  21.5 1.3 fusion.13
  22.9 4.0 %collective-permute-start = (bf16[208,128]{1,0:T(8,128)(2,1)S(1)}, bf16[208,128]{1,0:T(8,128)(2,1)S(1)}, u32[]{:S(2)}, u32[]{:S(2)}) collective-permute-start(bf16[208,128]{1,0:T(8,128)(2,1)S(1)} %pad_maximum_fusion), channel_id=1, source_target_pairs={{0,8},{8,16},{16,24},{24,32},{32,40},{40,48},{48,56},{56,64},{64,7... | collective-permute-start | bytes 159752 | tf_op jit(solution)/shard_map/ppermute | solution.py:36
  26.9 9.5 %collective-permute-start.8 = (bf16[208,128]{1,0:T(8,128)(2,1)S(1)}, bf16[208,128]{1,0:T(8,128)(2,1)S(1)}, u32[]{:S(2)}, u32[]{:S(2)}) collective-permute-start(bf16[208,128]{1,0:T(8,128)(2,1)S(1)} %pad_maximum_fusion), channel_id=1, source_target_pairs={{0,120},{8,0},{16,8},{24,16},{32,24},{40,32},{48,40},{56,48},{64,5... | collective-permute-start | bytes 159752 | tf_op jit(solution)/shard_map/ppermute | solution.py:36
  37.2 1.9 collective-permute-start.1
  39.1 4.6 %collective-permute-start.9 = (bf16[208,128]{1,0:T(8,128)(2,1)S(1)}, bf16[208,128]{1,0:T(8,128)(2,1)S(1)}, u32[]{:S(2)}, u32[]{:S(2)}) collective-permute-start(bf16[208,128]{1,0:T(8,128)(2,1)S(1)} %collective-permute-done.8), channel_id=1, source_target_pairs={{0,120},{8,0},{16,8},{24,16},{32,24},{40,32},{48,40},{56,48},{64,5... | collective-permute-start | bytes 159752 | tf_op jit(solution)/shard_map/ppermute | solution.py:36
  43.7 1.9 collective-permute-start.2
  45.7 5.1 %collective-permute-start.10 = (bf16[208,128]{1,0:T(8,128)(2,1)S(1)}, bf16[208,128]{1,0:T(8,128)(2,1)S(1)}, u32[]{:S(2)}, u32[]{:S(2)}) collective-permute-start(bf16[208,128]{1,0:T(8,128)(2,1)S(1)} %collective-permute-done.9), channel_id=1, source_target_pairs={{0,120},{8,0},{16,8},{24,16},{32,24},{40,32},{48,40},{56,48},{64,5... | collective-permute-start | bytes 159752 | tf_op jit(solution)/shard_map/ppermute | solution.py:36
  50.7 1.9 collective-permute-start.3
  52.7 4.6 %collective-permute-start.11 = (bf16[208,128]{1,0:T(8,128)(2,1)S(1)}, bf16[208,128]{1,0:T(8,128)(2,1)S(1)}, u32[]{:S(2)}, u32[]{:S(2)}) collective-permute-start(bf16[208,128]{1,0:T(8,128)(2,1)S(1)} %collective-permute-done.10), channel_id=1, source_target_pairs={{0,120},{8,0},{16,8},{24,16},{32,24},{40,32},{48,40},{56,48},{64,5... | collective-permute-start | bytes 159752 | tf_op jit(solution)/shard_map/ppermute | solution.py:36
  58.0 1.9 collective-permute-start.4
  59.9 4.6 %collective-permute-start.12 = (bf16[208,128]{1,0:T(8,128)(2,1)S(1)}, bf16[208,128]{1,0:T(8,128)(2,1)S(1)}, u32[]{:S(2)}, u32[]{:S(2)}) collective-permute-start(bf16[208,128]{1,0:T(8,128)(2,1)S(1)} %collective-permute-done.11), channel_id=1, source_target_pairs={{0,120},{8,0},{16,8},{24,16},{32,24},{40,32},{48,40},{56,48},{64,5... | collective-permute-start | bytes 159752 | tf_op jit(solution)/shard_map/ppermute | solution.py:36
  64.9 1.9 collective-permute-start.5
  66.9 4.6 %collective-permute-start.13 = (bf16[208,128]{1,0:T(8,128)(2,1)S(1)}, bf16[208,128]{1,0:T(8,128)(2,1)S(1)}, u32[]{:S(2)}, u32[]{:S(2)}) collective-permute-start(bf16[208,128]{1,0:T(8,128)(2,1)S(1)} %collective-permute-done.12), channel_id=1, source_target_pairs={{0,120},{8,0},{16,8},{24,16},{32,24},{40,32},{48,40},{56,48},{64,5... | collective-permute-start | bytes 159752 | tf_op jit(solution)/shard_map/ppermute | solution.py:36
  71.8 1.9 collective-permute-start.6
  73.8 4.6 %collective-permute-start.14 = (bf16[208,128]{1,0:T(8,128)(2,1)S(1)}, bf16[208,128]{1,0:T(8,128)(2,1)S(1)}, u32[]{:S(2)}, u32[]{:S(2)}) collective-permute-start(bf16[208,128]{1,0:T(8,128)(2,1)S(1)} %collective-permute-done.13), channel_id=1, source_target_pairs={{0,120},{8,0},{16,8},{24,16},{32,24},{40,32},{48,40},{56,48},{64,5... | collective-permute-start | bytes 159752 | tf_op jit(solution)/shard_map/ppermute | solution.py:36
  78.9 1.9 collective-permute-start.7
  80.8 5.0 %collective-permute-done.7 = bf16[208,128]{1,0:T(8,128)(2,1)S(1)} collective-permute-done((bf16[208,128]{1,0:T(8,128)(2,1)S(1)}, bf16[208,128]{1,0:T(8,128)(2,1)S(1)}, u32[]{:S(2)}, u32[]{:S(2)}) %collective-permute-start.7) | collective-permute-done | bytes 53280 | tf_op jit(solution)/shard_map/ppermute | solution.py:36
  86.0 4.5 %collective-permute-start.15 = (bf16[16,208,128]{2,1,0:T(8,128)(2,1)S(1)}, bf16[16,208,128]{2,1,0:T(8,128)(2,1)S(1)}, u32[]{:S(2)}, u32[]{:S(2)}) collective-permute-start(bf16[16,208,128]{2,1,0:T(8,128)(2,1)S(1)} %bitcast_dynamic-update-slice_fusion.refs_1_), channel_id=1, source_target_pairs={{0,128},{8,136},{16,144},{24,152},{32,160},{40,168},{48,176},{56,1... | collective-permute-start | bytes 2555912 | tf_op jit(solution)/shard_map/ppermute | solution.py:36
  90.5 2.5 %collective-permute-start.16 = (bf16[16,208,128]{2,1,0:T(8,128)(2,1)S(1)}, bf16[16,208,128]{2,1,0:T(8,128)(2,1)S(1)}, u32[]{:S(2)}, u32[]{:S(2)}) collective-permute-start(bf16[16,208,128]{2,1,0:T(8,128)(2,1)S(1)} %bitcast_dynamic-update-slice_fusion.refs_1_), channel_id=1, source_target_pairs={{0,384},{8,392},{16,400},{24,408},{32,416},{40,424},{48,432},{56,4... | collective-permute-start | bytes 2555912 | tf_op jit(solution)/shard_map/ppermute | solution.py:36
  96.4 5.8 %collective-permute-done.15.refs_2_ = bf16[16,208,128]{2,1,0:T(8,128)(2,1)S(1)} collective-permute-done((bf16[16,208,128]{2,1,0:T(8,128)(2,1)S(1)}, bf16[16,208,128]{2,1,0:T(8,128)(2,1)S(1)}, u32[]{:S(2)}, u32[]{:S(2)}) %collective-permute-start.15) | collective-permute-done | bytes 852000 | tf_op jit(solution)/shard_map/ppermute | solution.py:36
  103.0 2.7 %collective-permute-start.17 = (bf16[8,208,128]{2,1,0:T(8,128)(2,1)}, bf16[8,208,128]{2,1,0:T(8,128)(2,1)S(1)}, u32[]{:S(2)}, u32[]{:S(2)}) collective-permute-start(bf16[8,208,128]{2,1,0:T(8,128)(2,1)} %slice.44), channel_id=1, source_target_pairs={{0,128},{8,136},{16,144},{24,152},{32,160},{40,168},{48,176},{56,1... | collective-permute-start | bytes 1277960 | tf_op jit(solution)/shard_map/ppermute | solution.py:36
  106.7 3.7 %collective-permute-start.18 = (bf16[8,208,128]{2,1,0:T(8,128)(2,1)}, bf16[8,208,128]{2,1,0:T(8,128)(2,1)S(1)}, u32[]{:S(2)}, u32[]{:S(2)}) collective-permute-start(bf16[8,208,128]{2,1,0:T(8,128)(2,1)} %slice.45), channel_id=1, source_target_pairs={{0,384},{8,392},{16,400},{24,408},{32,416},{40,424},{48,432},{56,4... | collective-permute-start | bytes 1277960 | tf_op jit(solution)/shard_map/ppermute | solution.py:36
  112.7 2.2 collective-permute-done.17.refs_4_
  120.5 1.9 copy-done
  122.4 1.2 copy-done.3
  123.5 1.2 copy-done.6
  127.9 3.2 %shard_map.87 = bf16[128,2,256]{2,1,0:T(2,128)(2,1)} custom-call(s32[128]{0:T(128)S(1)} %reshape.213.sel_ref, bf16[6144,2,128]{2,1,0:T(2,128)(2,1)S(1)} %bitcast.62, bf16[1664,2,128]{2,1,0:T(2,128)(2,1)S(1)} %bitcast.65, bf16[1664,2,128]{2,1,0:T(2,128)(2,1)S(1)} %bitcast.63, bf16[1664,2,128]{2,1,0:T(2,128)(2,1)S(1)} %bitcast.64, ...), custom_call_target="tpu_custom_call" | custom-call | bytes 8388608 | tf_op jit(solution)/shard_map/pallas_call | solution.py:164
  131.1 15.5 %all-to-all-start = ((bf16[128,2,1,256]{3,1,2,0:T(2,128)(2,1)}), bf16[128,2,1,256]{3,1,2,0:T(2,128)(2,1)S(1)}, u32[]{:S(2)}, u32[]{:S(2)}) async-start(bf16[128,2,1,256]{3,1,2,0:T(2,128)(2,1)} %bitcast.34), calls=%async_computation | async-start | bytes 262144 | tf_op jit(solution)/shard_map/all_to_all | solution.py:251
  147.8 1.2 copy-done.7
  153.1 80.1 %shard_map.86 = bf16[192,1024]{1,0:T(8,128)(2,1)} custom-call(s32[1]{0:T(128)} %bitcast.n_ref, bf16[192,1024]{1,0:T(8,128)(2,1)S(1)} %copy-done.19, bf16[192,128]{1,0:T(8,128)(2,1)S(1)} %copy-done.17, bf16[192,128]{1,0:T(8,128)(2,1)S(1)} %copy-done.18, f32[16,1,768]{2,1,0:T(1,128)S(1)} %compare_select_fusion.bias_ref, bf16[64,192,128]{2,1,0:T(8,128)(2,1)S(1)} %copy-done.1, ...), custom_call_target="tpu_custom_call" | custom-call | flops 9663676416 | bytes 8388608 | tf_op jit(solution)/shard_map/pallas_call | solution.py:114
  (117 shorter events, 27.0 us)
Async XLA Ops:
  7.2 113.3 %all-gather.4.cloned.1.call-start = ((), (), s32[]{:S(2)}) async-start(), calls=%async_computation.1 | async-start | bytes 3342336 | tf_op jit(solution)/shard_map/all_gather | solution.py:206
  22.9 14.3 %collective-permute-start = (bf16[208,128]{1,0:T(8,128)(2,1)S(1)}, bf16[208,128]{1,0:T(8,128)(2,1)S(1)}, u32[]{:S(2)}, u32[]{:S(2)}) collective-permute-start(bf16[208,128]{1,0:T(8,128)(2,1)S(1)} %pad_maximum_fusion), channel_id=1, source_target_pairs={{0,8},{8,16},{16,24},{24,32},{32,40},{40,48},{48,56},{56,64},{64,7... | collective-permute-start | bytes 159752 | tf_op jit(solution)/shard_map/ppermute | solution.py:36
  26.9 12.2 %collective-permute-start.8 = (bf16[208,128]{1,0:T(8,128)(2,1)S(1)}, bf16[208,128]{1,0:T(8,128)(2,1)S(1)}, u32[]{:S(2)}, u32[]{:S(2)}) collective-permute-start(bf16[208,128]{1,0:T(8,128)(2,1)S(1)} %pad_maximum_fusion), channel_id=1, source_target_pairs={{0,120},{8,0},{16,8},{24,16},{32,24},{40,32},{48,40},{56,48},{64,5... | collective-permute-start | bytes 159752 | tf_op jit(solution)/shard_map/ppermute | solution.py:36
  37.2 6.5 %collective-permute-start.1 = (bf16[208,128]{1,0:T(8,128)(2,1)S(1)}, bf16[208,128]{1,0:T(8,128)(2,1)S(1)}, u32[]{:S(2)}, u32[]{:S(2)}) collective-permute-start(bf16[208,128]{1,0:T(8,128)(2,1)S(1)} %collective-permute-done), channel_id=1, source_target_pairs={{0,8},{8,16},{16,24},{24,32},{32,40},{40,48},{48,56},{56,64},{64,7... | collective-permute-start | bytes 159752 | tf_op jit(solution)/shard_map/ppermute | solution.py:36
  39.1 6.5 %collective-permute-start.9 = (bf16[208,128]{1,0:T(8,128)(2,1)S(1)}, bf16[208,128]{1,0:T(8,128)(2,1)S(1)}, u32[]{:S(2)}, u32[]{:S(2)}) collective-permute-start(bf16[208,128]{1,0:T(8,128)(2,1)S(1)} %collective-permute-done.8), channel_id=1, source_target_pairs={{0,120},{8,0},{16,8},{24,16},{32,24},{40,32},{48,40},{56,48},{64,5... | collective-permute-start | bytes 159752 | tf_op jit(solution)/shard_map/ppermute | solution.py:36
  43.7 7.0 %collective-permute-start.2 = (bf16[208,128]{1,0:T(8,128)(2,1)S(1)}, bf16[208,128]{1,0:T(8,128)(2,1)S(1)}, u32[]{:S(2)}, u32[]{:S(2)}) collective-permute-start(bf16[208,128]{1,0:T(8,128)(2,1)S(1)} %collective-permute-done.1), channel_id=1, source_target_pairs={{0,8},{8,16},{16,24},{24,32},{32,40},{40,48},{48,56},{56,64},{64,7... | collective-permute-start | bytes 159752 | tf_op jit(solution)/shard_map/ppermute | solution.py:36
  45.7 7.0 %collective-permute-start.10 = (bf16[208,128]{1,0:T(8,128)(2,1)S(1)}, bf16[208,128]{1,0:T(8,128)(2,1)S(1)}, u32[]{:S(2)}, u32[]{:S(2)}) collective-permute-start(bf16[208,128]{1,0:T(8,128)(2,1)S(1)} %collective-permute-done.9), channel_id=1, source_target_pairs={{0,120},{8,0},{16,8},{24,16},{32,24},{40,32},{48,40},{56,48},{64,5... | collective-permute-start | bytes 159752 | tf_op jit(solution)/shard_map/ppermute | solution.py:36
  50.7 7.2 %collective-permute-start.3 = (bf16[208,128]{1,0:T(8,128)(2,1)S(1)}, bf16[208,128]{1,0:T(8,128)(2,1)S(1)}, u32[]{:S(2)}, u32[]{:S(2)}) collective-permute-start(bf16[208,128]{1,0:T(8,128)(2,1)S(1)} %collective-permute-done.2), channel_id=1, source_target_pairs={{0,8},{8,16},{16,24},{24,32},{32,40},{40,48},{48,56},{56,64},{64,7... | collective-permute-start | bytes 159752 | tf_op jit(solution)/shard_map/ppermute | solution.py:36
  52.7 7.2 %collective-permute-start.11 = (bf16[208,128]{1,0:T(8,128)(2,1)S(1)}, bf16[208,128]{1,0:T(8,128)(2,1)S(1)}, u32[]{:S(2)}, u32[]{:S(2)}) collective-permute-start(bf16[208,128]{1,0:T(8,128)(2,1)S(1)} %collective-permute-done.10), channel_id=1, source_target_pairs={{0,120},{8,0},{16,8},{24,16},{32,24},{40,32},{48,40},{56,48},{64,5... | collective-permute-start | bytes 159752 | tf_op jit(solution)/shard_map/ppermute | solution.py:36
  58.0 7.0 %collective-permute-start.4 = (bf16[208,128]{1,0:T(8,128)(2,1)S(1)}, bf16[208,128]{1,0:T(8,128)(2,1)S(1)}, u32[]{:S(2)}, u32[]{:S(2)}) collective-permute-start(bf16[208,128]{1,0:T(8,128)(2,1)S(1)} %collective-permute-done.3), channel_id=1, source_target_pairs={{0,8},{8,16},{16,24},{24,32},{32,40},{40,48},{48,56},{56,64},{64,7... | collective-permute-start | bytes 159752 | tf_op jit(solution)/shard_map/ppermute | solution.py:36
  59.9 7.0 %collective-permute-start.12 = (bf16[208,128]{1,0:T(8,128)(2,1)S(1)}, bf16[208,128]{1,0:T(8,128)(2,1)S(1)}, u32[]{:S(2)}, u32[]{:S(2)}) collective-permute-start(bf16[208,128]{1,0:T(8,128)(2,1)S(1)} %collective-permute-done.11), channel_id=1, source_target_pairs={{0,120},{8,0},{16,8},{24,16},{32,24},{40,32},{48,40},{56,48},{64,5... | collective-permute-start | bytes 159752 | tf_op jit(solution)/shard_map/ppermute | solution.py:36
  64.9 6.9 %collective-permute-start.5 = (bf16[208,128]{1,0:T(8,128)(2,1)S(1)}, bf16[208,128]{1,0:T(8,128)(2,1)S(1)}, u32[]{:S(2)}, u32[]{:S(2)}) collective-permute-start(bf16[208,128]{1,0:T(8,128)(2,1)S(1)} %collective-permute-done.4), channel_id=1, source_target_pairs={{0,8},{8,16},{16,24},{24,32},{32,40},{40,48},{48,56},{56,64},{64,7... | collective-permute-start | bytes 159752 | tf_op jit(solution)/shard_map/ppermute | solution.py:36
  66.9 6.9 %collective-permute-start.13 = (bf16[208,128]{1,0:T(8,128)(2,1)S(1)}, bf16[208,128]{1,0:T(8,128)(2,1)S(1)}, u32[]{:S(2)}, u32[]{:S(2)}) collective-permute-start(bf16[208,128]{1,0:T(8,128)(2,1)S(1)} %collective-permute-done.12), channel_id=1, source_target_pairs={{0,120},{8,0},{16,8},{24,16},{32,24},{40,32},{48,40},{56,48},{64,5... | collective-permute-start | bytes 159752 | tf_op jit(solution)/shard_map/ppermute | solution.py:36
  71.8 7.1 %collective-permute-start.6 = (bf16[208,128]{1,0:T(8,128)(2,1)S(1)}, bf16[208,128]{1,0:T(8,128)(2,1)S(1)}, u32[]{:S(2)}, u32[]{:S(2)}) collective-permute-start(bf16[208,128]{1,0:T(8,128)(2,1)S(1)} %collective-permute-done.5), channel_id=1, source_target_pairs={{0,8},{8,16},{16,24},{24,32},{32,40},{40,48},{48,56},{56,64},{64,7... | collective-permute-start | bytes 159752 | tf_op jit(solution)/shard_map/ppermute | solution.py:36
  73.8 12.2 %collective-permute-start.14 = (bf16[208,128]{1,0:T(8,128)(2,1)S(1)}, bf16[208,128]{1,0:T(8,128)(2,1)S(1)}, u32[]{:S(2)}, u32[]{:S(2)}) collective-permute-start(bf16[208,128]{1,0:T(8,128)(2,1)S(1)} %collective-permute-done.13), channel_id=1, source_target_pairs={{0,120},{8,0},{16,8},{24,16},{32,24},{40,32},{48,40},{56,48},{64,5... | collective-permute-start | bytes 159752 | tf_op jit(solution)/shard_map/ppermute | solution.py:36
  78.9 6.9 %collective-permute-start.7 = (bf16[208,128]{1,0:T(8,128)(2,1)S(1)}, bf16[208,128]{1,0:T(8,128)(2,1)S(1)}, u32[]{:S(2)}, u32[]{:S(2)}) collective-permute-start(bf16[208,128]{1,0:T(8,128)(2,1)S(1)} %collective-permute-done.6), channel_id=1, source_target_pairs={{0,8},{8,16},{16,24},{24,32},{32,40},{40,48},{48,56},{56,64},{64,7... | collective-permute-start | bytes 159752 | tf_op jit(solution)/shard_map/ppermute | solution.py:36
  86.0 34.5 %copy-start.8 = (bf16[16,208,128]{2,1,0:T(8,128)(2,1)}, bf16[16,208,128]{2,1,0:T(8,128)(2,1)S(1)}, u32[]{:S(2)}) copy-start(bf16[16,208,128]{2,1,0:T(8,128)(2,1)S(1)} %bitcast_dynamic-update-slice_fusion.refs_1_) | copy-start | bytes 2555908
  86.0 16.2 %collective-permute-start.15 = (bf16[16,208,128]{2,1,0:T(8,128)(2,1)S(1)}, bf16[16,208,128]{2,1,0:T(8,128)(2,1)S(1)}, u32[]{:S(2)}, u32[]{:S(2)}) collective-permute-start(bf16[16,208,128]{2,1,0:T(8,128)(2,1)S(1)} %bitcast_dynamic-update-slice_fusion.refs_1_), channel_id=1, source_target_pairs={{0,128},{8,136},{16,144},{24,152},{32,160},{40,168},{48,176},{56,1... | collective-permute-start | bytes 2555912 | tf_op jit(solution)/shard_map/ppermute | solution.py:36
  90.5 15.3 %collective-permute-start.16 = (bf16[16,208,128]{2,1,0:T(8,128)(2,1)S(1)}, bf16[16,208,128]{2,1,0:T(8,128)(2,1)S(1)}, u32[]{:S(2)}, u32[]{:S(2)}) collective-permute-start(bf16[16,208,128]{2,1,0:T(8,128)(2,1)S(1)} %bitcast_dynamic-update-slice_fusion.refs_1_), channel_id=1, source_target_pairs={{0,384},{8,392},{16,400},{24,408},{32,416},{40,424},{48,432},{56,4... | collective-permute-start | bytes 2555912 | tf_op jit(solution)/shard_map/ppermute | solution.py:36
  102.2 18.3 %copy-start.2 = (bf16[16,208,128]{2,1,0:T(8,128)(2,1)}, bf16[16,208,128]{2,1,0:T(8,128)(2,1)S(1)}, u32[]{:S(2)}) copy-start(bf16[16,208,128]{2,1,0:T(8,128)(2,1)S(1)} %collective-permute-done.15.refs_2_) | copy-start | bytes 2555908
  103.0 11.8 %collective-permute-start.17 = (bf16[8,208,128]{2,1,0:T(8,128)(2,1)}, bf16[8,208,128]{2,1,0:T(8,128)(2,1)S(1)}, u32[]{:S(2)}, u32[]{:S(2)}) collective-permute-start(bf16[8,208,128]{2,1,0:T(8,128)(2,1)} %slice.44), channel_id=1, source_target_pairs={{0,128},{8,136},{16,144},{24,152},{32,160},{40,168},{48,176},{56,1... | collective-permute-start | bytes 1277960 | tf_op jit(solution)/shard_map/ppermute | solution.py:36
  105.8 14.7 %copy-start.5 = (bf16[16,208,128]{2,1,0:T(8,128)(2,1)}, bf16[16,208,128]{2,1,0:T(8,128)(2,1)S(1)}, u32[]{:S(2)}) copy-start(bf16[16,208,128]{2,1,0:T(8,128)(2,1)S(1)} %collective-permute-done.16.refs_3_) | copy-start | bytes 2555908
  106.7 11.0 %collective-permute-start.18 = (bf16[8,208,128]{2,1,0:T(8,128)(2,1)}, bf16[8,208,128]{2,1,0:T(8,128)(2,1)S(1)}, u32[]{:S(2)}, u32[]{:S(2)}) collective-permute-start(bf16[8,208,128]{2,1,0:T(8,128)(2,1)} %slice.45), channel_id=1, source_target_pairs={{0,384},{8,392},{16,400},{24,408},{32,416},{40,424},{48,432},{56,4... | collective-permute-start | bytes 1277960 | tf_op jit(solution)/shard_map/ppermute | solution.py:36
  120.5 1.9 copy-start
  122.4 1.2 copy-start.3
  123.5 1.2 copy-start.6
  127.9 18.8 %copy-start.1 = (bf16[64,192,128]{2,1,0:T(8,128)(2,1)S(1)}, bf16[64,192,128]{2,1,0:T(8,128)(2,1)}, u32[]{:S(2)}) copy-start(bf16[64,192,128]{2,1,0:T(8,128)(2,1)} %all-gather.4.cloned.1.call-done.refs_0_) | copy-start | bytes 9437188
  127.9 18.8 %copy-start.17 = (bf16[192,128]{1,0:T(8,128)(2,1)S(1)}, bf16[192,128]{1,0:T(8,128)(2,1)}, u32[]{:S(2)}) copy-start(bf16[192,128]{1,0:T(8,128)(2,1)} %k_ref.1) | copy-start | bytes 147460
  127.9 18.8 %copy-start.18 = (bf16[192,128]{1,0:T(8,128)(2,1)S(1)}, bf16[192,128]{1,0:T(8,128)(2,1)}, u32[]{:S(2)}) copy-start(bf16[192,128]{1,0:T(8,128)(2,1)} %v_ref.1) | copy-start | bytes 147460
  131.1 102.1 %all-to-all-start = ((bf16[128,2,1,256]{3,1,2,0:T(2,128)(2,1)}), bf16[128,2,1,256]{3,1,2,0:T(2,128)(2,1)S(1)}, u32[]{:S(2)}, u32[]{:S(2)}) async-start(bf16[128,2,1,256]{3,1,2,0:T(2,128)(2,1)} %bitcast.34), calls=%async_computation | async-start | bytes 262144 | tf_op jit(solution)/shard_map/all_to_all | solution.py:251
  146.6 1.2 copy-start.4
  147.8 1.2 copy-start.7
  (9 other events, 8.9 us)
Sparse Core Ops, SparseCore 0:
  19.3 77.1 all-gather.3

commit v2 on v0

v2 whole, which is shorter than its diff:
```python
import math

import jax
import jax.numpy as jnp
from jax import lax
from jax.experimental import pallas as pl
from jax.experimental.pallas import tpu as pltpu
from jax.sharding import PartitionSpec as P

HD = 128
PAGE = 2
NX = 4
NZ = 16
N = NX * NZ
CAP = 192
ROWS_A = 64
ROWS_B = CAP - ROWS_A
PAGES = CAP // PAGE
PAGES_A = ROWS_A // PAGE
PAGES_B = ROWS_B // PAGE
PAD = 16
TALL_A = 2 * ROWS_A + PAD
TALL_B = 2 * ROWS_B
GROUP = 8
ROWS = GROUP * CAP
TILES = 4
TILE = ROWS // TILES
WIDTH = 512
DEAD = -1e30
SCALE = math.log2(math.e) / math.sqrt(HD)
LIMIT = 64.0 / SCALE
VMEM_LIMIT = 56 * 1024 * 1024

Z_GROUPS = [[x * NZ + z for z in range(NZ)] for x in range(NX)]
Z_FIRST = [4, 0, -4, 8]
Z_REST = [3, -1, -5, 7, 5, 1, -3, 9, -2, -6, 6, 2]
X_A = [0, -1, 1, 2]
X_B = [0] * 16 + [-1] * 4 + [1] * 4 + [-1] * 12 + [1] * 12 + [2] * 16
Z_B = (Z_FIRST + Z_REST) + Z_FIRST * 2 + Z_REST * 2 + (Z_FIRST + Z_REST)


def shift(value, dx, dz):
    pairs = [
        (x * NZ + z, ((x + dx) % NX) * NZ + (z + dz) % NZ) for x in range(NX) for z in range(NZ)
    ]
    return lax.ppermute(value, "ctx", pairs)


def gather_z(value):
    return lax.all_gather(value, "ctx", axis=0, tiled=False, axis_index_groups=Z_GROUPS)


def exchange(a, b):
    left4, right4 = shift(b, 0, 4), shift(b, 0, -4)
    near = [shift(a, dx, 0) for dx in (1, -1, 2)]
    far4 = jnp.concatenate(
        [shift(left4[:ROWS_B], 0, 4), shift(right4[ROWS_B:], 0, -4)], axis=0
    )
    first = jnp.stack([right4, b, left4, far4])
    gathered = gather_z(jnp.stack([a] + near)).reshape(N, TALL_A, HD)
    rest = jnp.concatenate(
        [shift(first, 0, 1), shift(first, 0, -1), shift(first[1:3], 0, 2), shift(first[0:2], 0, -2)],
        axis=0,
    )
    first_left, first_right = shift(first, 1, 0), shift(first, -1, 0)
    first_far = shift(first_left, 1, 0)
    rest_left, rest_right = shift(rest, 1, 0), shift(rest, -1, 0)
    far_left, far_right = shift(rest_left[:4], 1, 0), shift(rest_right[4:], -1, 0)
    own = [first, rest]
    beside = [first_left, first_right, rest_left, rest_right]
    across = [first_far, far_left, far_right]
    return gathered, own, beside, across


def lanes(rows):
    return lax.broadcasted_iota(jnp.int32, (rows, HD), 1)


def reference_columns(m):
    rows = m.shape[0]
    m = jnp.broadcast_to(m, (rows, HD))
    high = m.astype(jnp.bfloat16).astype(jnp.float32)
    rest = m - high
    middle = rest.astype(jnp.bfloat16).astype(jnp.float32)
    low = rest - middle
    lane = lanes(rows)
    out = jnp.where(lane == 0, 1.0, 0.0)
    out = jnp.where(lane == 1, -high, out)
    out = jnp.where(lane == 2, -middle, out)
    out = jnp.where(lane == 3, -low, out)
    return out.astype(jnp.bfloat16)


def dot_t(a, b):
    return lax.dot_general(a, b, (((1,), (1,)), ((), ())), preferred_element_type=jnp.float32)


def by_lanes(op, s):
    out = s[:, :HD]
    for i in range(1, s.shape[1] // HD):
        out = op(out, s[:, i * HD : (i + 1) * HD])
    return out


def attention_kernel(first, last, talls, counts, *refs):
    n_src = len(talls)
    count_ref, live_ref = refs[0], refs[1]
    sources = refs[2 : 2 + n_src]
    refs = refs[2 + n_src :]
    if first:
        (q_ref, k_ref, v_ref), refs = refs[:3], refs[3:]
    else:
        (q0, l0, acc0), refs = refs[:3], refs[3:]
    if last:
        out_ref, refs = refs[0], refs[1:]
    q1, l1, acc1, kbuf, vbuf, sems = refs[:6]
    stages, refs = refs[6 : 6 + n_src], refs[6 + n_src :]
    if first:
        q0, l0, acc0 = refs
    live = live_ref[0]

    copies = [
        pltpu.make_async_copy(sources[i], stages[i], sems.at[i]) for i in range(n_src)
    ]
    for copy in copies:
        copy.start()

    if first:
        row = lax.broadcasted_iota(jnp.int32, (CAP, CAP), 0)
        col = lax.broadcasted_iota(jnp.int32, (CAP, CAP), 1)
        bias = jnp.where((col <= row) & (col < live), 0.0, DEAD).astype(jnp.float32)
        for h in range(GROUP):
            at = slice(h * CAP, (h + 1) * CAP)
            q = q_ref[:, h * HD : (h + 1) * HD]
            s = dot_t(q, k_ref[...]) + bias
            top = jnp.max(s, axis=1, keepdims=True)
            p = jnp.exp2((s - top) * SCALE)
            q0[at, 0:HD] = q
            q0[at, HD : 2 * HD] = reference_columns(top)
            l0[at, :] = jnp.where(lanes(CAP) == 0, jnp.sum(p, axis=1, keepdims=True), 0.0)
            acc0[at, :] = jnp.dot(
                p.astype(jnp.bfloat16), v_ref[...], preferred_element_type=jnp.float32
            )

    q1[...] = q0[...]
    l1[...] = l0[...]
    acc1[...] = acc0[...]

    for copy in copies:
        copy.wait()

    off = jnp.int32(0)
    base = 0
    for i in range(n_src):
        tall = talls[i]
        stage = stages[i]
        row = lax.broadcasted_iota(jnp.int32, (tall, HD), 0)
        lane = lanes(tall)
        alive = jnp.where((lane >= 1) & (lane <= 3), 1.0, 0.0).astype(jnp.float32)
        dead = jnp.where(lane == 0, DEAD, 0.0).astype(jnp.float32)

        def pack(j, off, base=base, tall=tall, stage=stage, row=row, alive=alive, dead=dead):
            count = count_ref[base + j]
            at = pl.ds(pl.multiple_of(off, 16), tall)
            kbuf[at, 0:HD] = stage[j, 0:tall, :]
            kbuf[at, HD : 2 * HD] = jnp.where(row < count, alive, dead).astype(jnp.bfloat16)
            vbuf[at, :] = stage[j, tall : 2 * tall, :]
            return off + ((count + 15) // 16) * 16

        off = lax.fori_loop(0, counts[i], pack, off)
        base += counts[i]
    at = pl.ds(pl.multiple_of(off, 16), WIDTH)
    kbuf[at, 0:HD] = jnp.zeros((WIDTH, HD), jnp.bfloat16)
    kbuf[at, HD : 2 * HD] = jnp.where(lanes(WIDTH) == 0, DEAD, 0.0).astype(jnp.bfloat16)
    vbuf[at, :] = jnp.zeros((WIDTH, HD), jnp.bfloat16)
    blocks = (off + WIDTH - 1) // WIDTH

    def block(i, track):
        at = pl.ds(pl.multiple_of(i * WIDTH, WIDTH), WIDTH)
        for t in range(TILES):
            rows = slice(t * TILE, (t + 1) * TILE)
            s = dot_t(q1[rows, :], kbuf[at, :])
            track = jnp.maximum(
                track, jnp.max(by_lanes(jnp.maximum, s).reshape(TILE // 8, 8, HD), axis=0)
            )
            p = jnp.exp2(s * SCALE)
            l1[rows, :] += by_lanes(jnp.add, p)
            acc1[rows, :] += jnp.dot(
                p.astype(jnp.bfloat16), vbuf[at, :], preferred_element_type=jnp.float32
            )
        return track

    track = lax.fori_loop(0, blocks, block, jnp.full((8, HD), DEAD, jnp.float32))

    @pl.when(jnp.max(track) > LIMIT)
    def _():
        for t in range(TILES):
            rows = slice(t * TILE, (t + 1) * TILE)

            def highest(i, top, rows=rows):
                at = pl.ds(pl.multiple_of(i * WIDTH, WIDTH), WIDTH)
                return jnp.maximum(top, by_lanes(jnp.maximum, dot_t(q0[rows, :], kbuf[at, :])))

            top = lax.fori_loop(0, blocks, highest, jnp.zeros((TILE, HD), jnp.float32))
            rise = jnp.max(top, axis=1, keepdims=True)
            columns = q0[rows, HD : 2 * HD].astype(jnp.float32)
            lane = lanes(TILE)
            m = -jnp.sum(
                jnp.where((lane >= 1) & (lane <= 3), columns, 0.0), axis=1, keepdims=True
            )
            factor = jnp.exp2(-rise * SCALE)
            q1[rows, HD : 2 * HD] = reference_columns(m + rise)
            l1[rows, :] = l0[rows, :] * factor
            acc1[rows, :] = acc0[rows, :] * factor
        lax.fori_loop(0, blocks, block, jnp.full((8, HD), DEAD, jnp.float32))

    if last:
        ok = lax.broadcasted_iota(jnp.int32, (CAP, HD), 0) < live
        for h in range(GROUP):
            at = slice(h * CAP, (h + 1) * CAP)
            total = jnp.sum(l1[at, :], axis=1, keepdims=True)
            result = jnp.where(ok, acc1[at, :] / total, 0.0)
            out_ref[:, h * HD : (h + 1) * HD] = result.astype(jnp.bfloat16)


def attention(first, last, count, live, sources, state, interpret=False):
    talls = [ROWS_B if s.shape[1] == TALL_B else ROWS_A for s in sources]
    counts = [s.shape[0] for s in sources]
    keys = sum(c * t for c, t in zip(counts, talls))
    vmem = pl.BlockSpec(memory_space=pltpu.VMEM)
    smem = pl.BlockSpec(memory_space=pltpu.SMEM)
    state_shapes = [
        ((ROWS, 2 * HD), jnp.bfloat16),
        ((ROWS, HD), jnp.float32),
        ((ROWS, HD), jnp.float32),
    ]
    scratch_state = [pltpu.VMEM(*s) for s in state_shapes]
    if last:
        out_shape = jax.ShapeDtypeStruct((CAP, GROUP * HD), jnp.bfloat16)
        out_specs = vmem
    else:
        out_shape = [jax.ShapeDtypeStruct(*s) for s in state_shapes]
        out_specs = [vmem] * 3
    scratch = (
        (scratch_state if last else [])
        + [
            pltpu.VMEM((keys + WIDTH, 2 * HD), jnp.bfloat16),
            pltpu.VMEM((keys + WIDTH, HD), jnp.bfloat16),
            pltpu.SemaphoreType.DMA((len(sources),)),
        ]
        + [pltpu.VMEM(s.shape, jnp.bfloat16) for s in sources]
        + (scratch_state if first else [])
    )

    def kernel(*refs):
        attention_kernel(first, last, talls, counts, *refs)

    return pl.pallas_call(
        kernel,
        out_shape=out_shape,
        in_specs=[smem, smem] + [pl.BlockSpec(memory_space=pl.ANY)] * len(sources) + [vmem] * 3,
        out_specs=out_specs,
        scratch_shapes=scratch,
        compiler_params=pltpu.CompilerParams(vmem_limit_bytes=VMEM_LIMIT),
        cost_estimate=pl.CostEstimate(
            flops=8 * ROWS * keys * HD, bytes_accessed=8 << 20, transcendentals=0
        ),
        interpret=interpret,
    )(count, live, *sources, *state)


def select_kernel(n_src, key_ref, value_ref, *refs):
    sources, (out_ref, pages, sems) = refs[:n_src], refs[n_src:]
    copies = []
    start = 0
    for i, source in enumerate(sources):
        count = source.shape[0]
        copies.append(
            pltpu.make_async_copy(source, pages.at[pl.ds(start, count)], sems.at[i])
        )
        start += count
    for copy in copies:
        copy.start()
    for copy in copies:
        copy.wait()

    def one(s, carry):
        place = key_ref[s]
        keep = jnp.where(place >= 0, 1.0, 0.0).astype(jnp.bfloat16)
        out_ref[s, :, 0:HD] = pages[jnp.maximum(place, 0)] * keep
        out_ref[s, :, HD : 2 * HD] = pages[jnp.maximum(value_ref[s], 0)] * keep
        return carry

    lax.fori_loop(0, 2 * N, one, 0, unroll=4)


def select_pages(key_place, value_place, sources, interpret=False):
    sources = [s.reshape(s.shape[0] * s.shape[1] // PAGE, PAGE, HD) for s in sources]
    total = sum(s.shape[0] for s in sources)
    smem = pl.BlockSpec(memory_space=pltpu.SMEM)

    def kernel(*refs):
        select_kernel(len(sources), *refs)

    return pl.pallas_call(
        kernel,
        out_shape=jax.ShapeDtypeStruct((2 * N, PAGE, 2 * HD), jnp.bfloat16),
        in_specs=[smem, smem] + [pl.BlockSpec(memory_space=pl.ANY)] * len(sources),
        out_specs=pl.BlockSpec(memory_space=pltpu.VMEM),
        scratch_shapes=[
            pltpu.VMEM((total, PAGE, HD), jnp.bfloat16),
            pltpu.SemaphoreType.DMA((len(sources),)),
        ],
        compiler_params=pltpu.CompilerParams(vmem_limit_bytes=VMEM_LIMIT),
        cost_estimate=pl.CostEstimate(flops=0, bytes_accessed=8 << 20, transcendentals=0),
        interpret=interpret,
    )(key_place, value_place, *sources)


def payloads(keys, values, page_owner):
    owner = page_owner[:, 0].astype(jnp.bfloat16)
    owner = jnp.broadcast_to(jnp.pad(owner, (0, HD - PAGES))[None, :], (PAD, HD))
    a = jnp.concatenate([keys[:ROWS_A], values[:ROWS_A], owner], axis=0)
    b = jnp.concatenate([keys[ROWS_A:], values[ROWS_A:]], axis=0)
    return a, b


def layout(me):
    mx, mz = me // NZ, me % NZ
    dx, dz = jnp.array(X_B, jnp.int32), jnp.array(Z_B, jnp.int32)
    piece_b = ((mx + dx + NX) % NX) * NZ + (mz + dz + NZ) % NZ
    dx = jnp.array(X_A * NZ, jnp.int32)
    piece_a = ((mx + dx + NX) % NX) * NZ + jnp.arange(N, dtype=jnp.int32) // NX
    return piece_a, piece_b


def pick(table, index):
    place = jnp.arange(N, dtype=jnp.int32)
    return jnp.sum(jnp.where(index[:, None] == place[None, :], table[None, :], 0), axis=1)


def inverse(index):
    place = jnp.arange(N, dtype=jnp.int32)
    return jnp.sum(jnp.where(index[None, :] == place[:, None], place[None, :], 0), axis=1)


def page_places(me, gathered, piece_a, piece_b, lengths):
    place = jnp.arange(N, dtype=jnp.int32)
    owners = gathered[:, 2 * ROWS_A, :PAGES]
    page = jnp.arange(PAGES, dtype=jnp.int32)[None, :]
    match = owners == me.astype(jnp.bfloat16)
    low = jnp.min(jnp.where(match, page, PAGES), axis=1)
    high = jnp.max(jnp.where(match, page, -1), axis=1)
    pages = jnp.stack([low, jnp.where(high > low, high, PAGES)], axis=1)
    hit = piece_a[None, :] == place[:, None]
    pages = jnp.sum(jnp.where(hit[:, :, None], pages[None, :, :], 0), axis=1)
    at_a = inverse(piece_a)[:, None] * (TALL_A // PAGE) + pages
    at_b = N * (TALL_A // PAGE) + inverse(piece_b)[:, None] * (TALL_B // PAGE) + pages - PAGES_A
    in_a = pages < PAGES_A
    key_place = jnp.where(in_a, at_a, at_b)
    value_place = key_place + jnp.where(in_a, PAGES_A, PAGES_B)
    finished = (pages < PAGES) & ((pages + 1) * PAGE <= lengths[:, None])
    key_place = jnp.where(finished, key_place, -1)
    value_place = jnp.where(finished, value_place, -1)
    return key_place.reshape(2 * N), value_place.reshape(2 * N)


def live_counts(me, lengths, piece_a, piece_b):
    count_a = jnp.where(piece_a < me, jnp.minimum(pick(lengths, piece_a), ROWS_A), 0)
    count_b = jnp.where(piece_b < me, jnp.maximum(pick(lengths, piece_b) - ROWS_A, 0), 0)
    return count_a, count_b


def body(queries, keys, values, lengths, page_owner):
    me = lax.axis_index("ctx")
    live = jnp.sum(jnp.where(jnp.arange(N, dtype=jnp.int32) == me, lengths, 0)).reshape(1)
    gathered, own, beside, across = exchange(*payloads(keys, values, page_owner))
    piece_a, piece_b = layout(me)
    count_a, count_b = live_counts(me, lengths, piece_a, piece_b)
    key_place, value_place = page_places(me, gathered, piece_a, piece_b, lengths)
    outgoing = select_pages(key_place, value_place, [gathered] + own + beside + across)
    decode_cache = lax.all_to_all(
        outgoing.reshape(2 * N, PAGE, 1, 2 * HD), "tp", split_axis=0, concat_axis=2, tiled=True
    )
    state = attention(True, False, count_b[:16], live, own, (queries, keys, values))
    state = attention(False, False, count_b[16:48], live, beside, state)
    attended = attention(
        False, True, jnp.concatenate([count_b[48:], count_a]), live, across + [gathered], state
    )
    return (attended, decode_cache.reshape((1,) + decode_cache.shape))


def solution(mesh):
    in_specs = (P("ctx", "tp"), P("ctx", "tp"), P("ctx", "tp"), P(), P("ctx", None))
    out_specs = (P("ctx", "tp"), P("ctx", "tp", None, None, None))
    return jax.shard_map(body, mesh=mesh, in_specs=in_specs, out_specs=out_specs, check_vma=False)
```

time: 479 us -> 200 us (0.42)
  the two profiles are of different devices: /device:TPU:502 before, /device:TPU:143 now
where the time goes in v2:
time: 200 us; the launch traced here: 199 us
  starting transfers between devices  80 us (40%)
  Pallas kernels  65.4 us (33%)
  waiting for transfers between devices  25.5 us (13%)
  between operations  14.6 us (7%)
  local copies, waits for them, and re-layouts  8.05 us (4%)
  other arithmetic  5.1 us (3%)
    ppermute x18, starting transfers between devices, shift(): return lax.ppermute(value, 'ctx', pairs)  63.4 us
    pallas_call x3, Pallas kernels, attention(): pl.pallas_call(kernel, out_shape=out_shape, in_specs=[smem, smem] + [pl.B...  60.2 us
    ppermute x18, waiting for transfers between devices, shift(): return lax.ppermute(value, 'ctx', pairs)  25.5 us
    all_to_all x1, starting transfers between devices, body(): lax.all_to_all(outgoing.reshape(2 * N, PAGE, 1, 2 * HD), 'tp', split_axis...  16.6 us
    pallas_call x1, Pallas kernels, select_pages(): pl.pallas_call(kernel, out_shape=jax.ShapeDtypeStruct((2 * N, PAGE, 2 * H...  5.19 us
  transfers between devices with their start and end apart: 20, of which 5 were waited for; matrix products, arithmetic and copies ran while one was open for 4% of the time, Pallas kernels for 30%

profile of v2, /device:TPU:143, one launch (start us, length us, event | category | flops | bytes accessed | tf_op | source)
XLA Modules:
  0.0 198.6 jit_solution(17603674141234631467)
XLA Ops:
  9.3 2.5 %collective-permute-start.15 = (bf16[144,128]{1,0:T(8,128)(2,1)S(1)}, bf16[144,128]{1,0:T(8,128)(2,1)S(1)}, u32[]{:S(2)}, u32[]{:S(2)}) collective-permute-start(bf16[144,128]{1,0:T(8,128)(2,1)S(1)} %get-tuple-element.25), channel_id=1, source_target_pairs={{0,384},{8,392},{16,400},{24,408},{32,416},{40,424},{48,432},{56,4... | collective-permute-start | bytes 110600 | tf_op jit(solution)/shard_map/ppermute | solution.py:46
  11.8 4.0 %collective-permute-start.14 = (bf16[144,128]{1,0:T(8,128)(2,1)S(1)}, bf16[144,128]{1,0:T(8,128)(2,1)S(1)}, u32[]{:S(2)}, u32[]{:S(2)}) collective-permute-start(bf16[144,128]{1,0:T(8,128)(2,1)S(1)} %get-tuple-element.25), channel_id=1, source_target_pairs={{0,128},{8,136},{16,144},{24,152},{32,160},{40,168},{48,176},{56,1... | collective-permute-start | bytes 110600 | tf_op jit(solution)/shard_map/ppermute | solution.py:46
  15.9 1.9 collective-permute-start.16
  17.8 4.3 %collective-permute-done.16 = bf16[144,128]{1,0:T(8,128)(2,1)S(1)} collective-permute-done((bf16[144,128]{1,0:T(8,128)(2,1)S(1)}, bf16[144,128]{1,0:T(8,128)(2,1)S(1)}, u32[]{:S(2)}, u32[]{:S(2)}) %collective-permute-start.16) | collective-permute-done | bytes 36896 | tf_op jit(solution)/shard_map/ppermute | solution.py:46
  22.8 0.8 slice.41
  23.6 0.8 slice.42
  24.3 8.8 %collective-permute-start.1 = (bf16[256,128]{1,0:T(8,128)(2,1)S(1)}, bf16[256,128]{1,0:T(8,128)(2,1)S(1)}, u32[]{:S(2)}, u32[]{:S(2)}) collective-permute-start(bf16[256,128]{1,0:T(8,128)(2,1)S(1)} %get-tuple-element.23), channel_id=1, source_target_pairs={{0,32},{8,40},{16,48},{24,56},{32,64},{40,72},{48,80},{56,88},{64,... | collective-permute-start | bytes 196616 | tf_op jit(solution)/shard_map/ppermute | solution.py:46
  33.2 1.9 collective-permute-start
  35.8 0.9 select_reduce_fusion.2
  36.7 7.3 %collective-permute-start.2 = (bf16[128,128]{1,0:T(8,128)(2,1)S(1)}, bf16[128,128]{1,0:T(8,128)(2,1)S(1)}, u32[]{:S(2)}, u32[]{:S(2)}) collective-permute-start(bf16[128,128]{1,0:T(8,128)(2,1)S(1)} %slice.52), channel_id=1, source_target_pairs={{0,32},{8,40},{16,48},{24,56},{32,64},{40,72},{48,80},{56,88},{64,... | collective-permute-start | bytes 98312 | tf_op jit(solution)/shard_map/ppermute | solution.py:46
  44.0 1.9 collective-permute-start.3
  46.5 6.3 %collective-permute-done.3 = bf16[128,128]{1,0:T(8,128)(2,1)S(1)} collective-permute-done((bf16[128,128]{1,0:T(8,128)(2,1)S(1)}, bf16[128,128]{1,0:T(8,128)(2,1)S(1)}, u32[]{:S(2)}, u32[]{:S(2)}) %collective-permute-start.3) | collective-permute-done | bytes 32800 | tf_op jit(solution)/shard_map/ppermute | solution.py:46
  52.9 1.9 collective-permute-start.7
  54.8 3.4 %collective-permute-start.6 = (bf16[4,256,128]{2,1,0:T(8,128)(2,1)S(1)}, bf16[4,256,128]{2,1,0:T(8,128)(2,1)S(1)}, u32[]{:S(2)}, u32[]{:S(2)}) collective-permute-start(bf16[4,256,128]{2,1,0:T(8,128)(2,1)S(1)} %pad_maximum_fusion.refs_2_), channel_id=1, source_target_pairs={{0,8},{8,16},{16,24},{24,32},{32,40},{40,48},{48,56},{56,64},{64,7... | collective-permute-start | bytes 786440 | tf_op jit(solution)/shard_map/ppermute | solution.py:46
  58.2 1.9 collective-permute-start.9
  60.2 4.3 %collective-permute-start.8 = (bf16[2,256,128]{2,1,0:T(8,128)(2,1)S(1)}, bf16[2,256,128]{2,1,0:T(8,128)(2,1)S(1)}, u32[]{:S(2)}, u32[]{:S(2)}) collective-permute-start(bf16[2,256,128]{2,1,0:T(8,128)(2,1)S(1)} %get-tuple-element.21), channel_id=1, source_target_pairs={{0,16},{8,24},{16,32},{24,40},{32,48},{40,56},{48,64},{56,72},{64,... | collective-permute-start | bytes 393224 | tf_op jit(solution)/shard_map/ppermute | solution.py:46
  64.8 7.0 %collective-permute-done.8 = bf16[2,256,128]{2,1,0:T(8,128)(2,1)S(1)} collective-permute-done((bf16[2,256,128]{2,1,0:T(8,128)(2,1)S(1)}, bf16[2,256,128]{2,1,0:T(8,128)(2,1)S(1)}, u32[]{:S(2)}, u32[]{:S(2)}) %collective-permute-start.8) | collective-permute-done | bytes 131104 | tf_op jit(solution)/shard_map/ppermute | solution.py:46
  71.9 1.9 collective-permute-start.12
  73.8 4.6 %collective-permute-start.10 = (bf16[12,256,128]{2,1,0:T(8,128)(2,1)S(1)}, bf16[12,256,128]{2,1,0:T(8,128)(2,1)S(1)}, u32[]{:S(2)}, u32[]{:S(2)}) collective-permute-start(bf16[12,256,128]{2,1,0:T(8,128)(2,1)S(1)} %constant_dynamic-update-slice_fusion.refs_3_), channel_id=1, source_target_pairs={{0,128},{8,136},{16,144},{24,152},{32,160},{40,168},{48,176},{56,1... | collective-permute-start | bytes 2359304 | tf_op jit(solution)/shard_map/ppermute | solution.py:46
  79.1 1.9 collective-permute-start.4
  82.2 3.4 %collective-permute-start.17 = (bf16[4,256,128]{2,1,0:T(8,128)(2,1)S(1)}, bf16[4,256,128]{2,1,0:T(8,128)(2,1)S(1)}, u32[]{:S(2)}, u32[]{:S(2)}) collective-permute-start(bf16[4,256,128]{2,1,0:T(8,128)(2,1)S(1)} %pad_maximum_fusion.refs_2_), channel_id=1, source_target_pairs={{0,384},{8,392},{16,400},{24,408},{32,416},{40,424},{48,432},{56,4... | collective-permute-start | bytes 786440 | tf_op jit(solution)/shard_map/ppermute | solution.py:46
  85.6 7.5 %collective-permute-done.4.refs_2_ = bf16[4,256,128]{2,1,0:T(8,128)(2,1)S(1)} collective-permute-done((bf16[4,256,128]{2,1,0:T(8,128)(2,1)S(1)}, bf16[4,256,128]{2,1,0:T(8,128)(2,1)S(1)}, u32[]{:S(2)}, u32[]{:S(2)}) %collective-permute-start.4) | collective-permute-done | bytes 262176 | tf_op jit(solution)/shard_map/ppermute | solution.py:46
  93.1 5.3 %collective-permute-start.5 = (bf16[4,256,128]{2,1,0:T(8,128)(2,1)S(1)}, bf16[4,256,128]{2,1,0:T(8,128)(2,1)}, u32[]{:S(2)}, u32[]{:S(2)}) collective-permute-start(bf16[4,256,128]{2,1,0:T(8,128)(2,1)S(1)} %collective-permute-done.4.refs_2_), channel_id=1, source_target_pairs={{0,128},{8,136},{16,144},{24,152},{32,160},{40,168},{48,176},{56,1... | collective-permute-start | bytes 786440 | tf_op jit(solution)/shard_map/ppermute | solution.py:46
  98.4 6.1 %shard_map.95 = (bf16[1536,256]{1,0:T(8,128)(2,1)}, f32[1536,128]{1,0:T(8,128)}, f32[1536,128]{1,0:T(8,128)}) custom-call(s32[16]{0:T(128)} %get-tuple-element.30.refs_0_, s32[1]{0:T(128)} %bitcast.refs_1_, bf16[4,256,128]{2,1,0:T(8,128)(2,1)} %copy-done.3, bf16[12,256,128]{2,1,0:T(8,128)(2,1)} %copy-done.2, bf16[192,1024]{1,0:T(8,128)(2,1)} %refs_4_.1, ...), custom_call_target="tpu_custom_call" | custom-call | flops 3221225472 | bytes 8388608 | tf_op jit(solution)/shard_map/pallas_call | solution.py:258
  104.6 1.9 collective-permute-start.13
  106.6 4.6 %collective-permute-start.11 = (bf16[4,256,128]{2,1,0:T(8,128)(2,1)S(1)}, bf16[4,256,128]{2,1,0:T(8,128)(2,1)S(1)}, u32[]{:S(2)}, u32[]{:S(2)}) collective-permute-start(bf16[4,256,128]{2,1,0:T(8,128)(2,1)S(1)} %slice.54), channel_id=1, source_target_pairs={{0,128},{8,136},{16,144},{24,152},{32,160},{40,168},{48,176},{56,1... | collective-permute-start | bytes 786440 | tf_op jit(solution)/shard_map/ppermute | solution.py:46
  111.9 13.3 %shard_map.96 = (bf16[1536,256]{1,0:T(8,128)(2,1)}, f32[1536,128]{1,0:T(8,128)}, f32[1536,128]{1,0:T(8,128)}) custom-call(s32[32]{0:T(128)} %slice.49.refs_0_, s32[1]{0:T(128)} %bitcast.refs_1_, bf16[4,256,128]{2,1,0:T(8,128)(2,1)} %copy-done.4, bf16[4,256,128]{2,1,0:T(8,128)(2,1)} %copy-done.5, bf16[12,256,128]{2,1,0:T(8,128)(2,1)} %copy-done.1, ...), custom_call_target="tpu_custom_call" | custom-call | flops 6442450944 | bytes 8388608 | tf_op jit(solution)/shard_map/pallas_call | solution.py:258
  125.3 0.9 slice.56
  128.5 5.2 %shard_map.98 = bf16[128,2,256]{2,1,0:T(2,128)(2,1)} custom-call(s32[128]{0:T(128)} %get-tuple-element.27.refs_0_, s32[128]{0:T(128)} %get-tuple-element.26.refs_1_, bf16[4608,2,128]{2,1,0:T(2,128)(2,1)} %bitcast.40, bf16[512,2,128]{2,1,0:T(2,128)(2,1)} %bitcast.44, bf16[1536,2,128]{2,1,0:T(2,128)(2,1)} %bitcast.43, bf16[512,2,128]{2,1,0:T(2,128)(2,1)} %bitcast.51, ...), custom_call_target="tpu_custom_call" | custom-call | bytes 8388608 | tf_op jit(solution)/shard_map/pallas_call | solution.py:305
  133.7 16.6 %all-to-all-start = ((bf16[128,2,1,256]{3,1,2,0:T(2,128)(2,1)}), bf16[128,2,1,256]{3,1,2,0:T(2,128)(2,1)S(1)}, u32[]{:S(2)}, u32[]{:S(2)}) async-start(bf16[128,2,1,256]{3,1,2,0:T(2,128)(2,1)} %bitcast.45), calls=%async_computation | async-start | bytes 262144 | tf_op jit(solution)/shard_map/all_to_all | solution.py:382
  150.3 40.7 %shard_map.97 = bf16[192,1024]{1,0:T(8,128)(2,1)} custom-call(s32[80]{0:T(128)} %pad_add_fusion.1.refs_0_, s32[1]{0:T(128)} %bitcast.refs_1_, bf16[4,256,128]{2,1,0:T(8,128)(2,1)} %collective-permute-done.5.refs_2_, bf16[4,256,128]{2,1,0:T(8,128)(2,1)} %copy-done.6, bf16[8,256,128]{2,1,0:T(8,128)(2,1)} %collective-permute-done.13.refs_4_, ...), custom_call_target="tpu_custom_call" | custom-call | flops 9663676416 | bytes 8388608 | tf_op jit(solution)/shard_map/pallas_call | solution.py:258
  191.1 0.7 copy.27
  (76 shorter events, 9.5 us)
Async XLA Ops:
  7.2 71.3 %copy-start.7 = (s32[64]{0:T(128)S(1)}, s32[64]{0:T(128)}, u32[]{:S(2)}) copy-start(s32[64]{0:T(128)} %param.11) | copy-start | bytes 772
  7.2 118.1 %all-gather.3.cloned.1.call-start = ((), (), s32[]{:S(2)}) async-start(), calls=%async_computation.1 | async-start | bytes 2506752 | tf_op jit(solution)/shard_map/all_gather | solution.py:50
  9.3 8.4 %collective-permute-start.15 = (bf16[144,128]{1,0:T(8,128)(2,1)S(1)}, bf16[144,128]{1,0:T(8,128)(2,1)S(1)}, u32[]{:S(2)}, u32[]{:S(2)}) collective-permute-start(bf16[144,128]{1,0:T(8,128)(2,1)S(1)} %get-tuple-element.25), channel_id=1, source_target_pairs={{0,384},{8,392},{16,400},{24,408},{32,416},{40,424},{48,432},{56,4... | collective-permute-start | bytes 110600 | tf_op jit(solution)/shard_map/ppermute | solution.py:46
  11.8 6.0 %collective-permute-start.14 = (bf16[144,128]{1,0:T(8,128)(2,1)S(1)}, bf16[144,128]{1,0:T(8,128)(2,1)S(1)}, u32[]{:S(2)}, u32[]{:S(2)}) collective-permute-start(bf16[144,128]{1,0:T(8,128)(2,1)S(1)} %get-tuple-element.25), channel_id=1, source_target_pairs={{0,128},{8,136},{16,144},{24,152},{32,160},{40,168},{48,176},{56,1... | collective-permute-start | bytes 110600 | tf_op jit(solution)/shard_map/ppermute | solution.py:46
  15.9 6.2 %collective-permute-start.16 = (bf16[144,128]{1,0:T(8,128)(2,1)S(1)}, bf16[144,128]{1,0:T(8,128)(2,1)S(1)}, u32[]{:S(2)}, u32[]{:S(2)}) collective-permute-start(bf16[144,128]{1,0:T(8,128)(2,1)S(1)} %get-tuple-element.25), channel_id=1, source_target_pairs={{0,256},{8,264},{16,272},{24,280},{32,288},{40,296},{48,304},{56,3... | collective-permute-start | bytes 110600 | tf_op jit(solution)/shard_map/ppermute | solution.py:46
  24.3 12.4 %collective-permute-start.1 = (bf16[256,128]{1,0:T(8,128)(2,1)S(1)}, bf16[256,128]{1,0:T(8,128)(2,1)S(1)}, u32[]{:S(2)}, u32[]{:S(2)}) collective-permute-start(bf16[256,128]{1,0:T(8,128)(2,1)S(1)} %get-tuple-element.23), channel_id=1, source_target_pairs={{0,32},{8,40},{16,48},{24,56},{32,64},{40,72},{48,80},{56,88},{64,... | collective-permute-start | bytes 196616 | tf_op jit(solution)/shard_map/ppermute | solution.py:46
  33.2 10.9 %collective-permute-start = (bf16[256,128]{1,0:T(8,128)(2,1)S(1)}, bf16[256,128]{1,0:T(8,128)(2,1)S(1)}, u32[]{:S(2)}, u32[]{:S(2)}) collective-permute-start(bf16[256,128]{1,0:T(8,128)(2,1)S(1)} %get-tuple-element.23), channel_id=1, source_target_pairs={{0,96},{8,104},{16,112},{24,120},{32,0},{40,8},{48,16},{56,24},{64... | collective-permute-start | bytes 196616 | tf_op jit(solution)/shard_map/ppermute | solution.py:46
  36.7 9.7 %collective-permute-start.2 = (bf16[128,128]{1,0:T(8,128)(2,1)S(1)}, bf16[128,128]{1,0:T(8,128)(2,1)S(1)}, u32[]{:S(2)}, u32[]{:S(2)}) collective-permute-start(bf16[128,128]{1,0:T(8,128)(2,1)S(1)} %slice.52), channel_id=1, source_target_pairs={{0,32},{8,40},{16,48},{24,56},{32,64},{40,72},{48,80},{56,88},{64,... | collective-permute-start | bytes 98312 | tf_op jit(solution)/shard_map/ppermute | solution.py:46
  44.0 8.8 %collective-permute-start.3 = (bf16[128,128]{1,0:T(8,128)(2,1)S(1)}, bf16[128,128]{1,0:T(8,128)(2,1)S(1)}, u32[]{:S(2)}, u32[]{:S(2)}) collective-permute-start(bf16[128,128]{1,0:T(8,128)(2,1)S(1)} %slice.53), channel_id=1, source_target_pairs={{0,96},{8,104},{16,112},{24,120},{32,0},{40,8},{48,16},{56,24},{64... | collective-permute-start | bytes 98312 | tf_op jit(solution)/shard_map/ppermute | solution.py:46
  52.9 45.5 %copy-start.3 = (bf16[4,256,128]{2,1,0:T(8,128)(2,1)}, bf16[4,256,128]{2,1,0:T(8,128)(2,1)S(1)}, u32[]{:S(2)}) copy-start(bf16[4,256,128]{2,1,0:T(8,128)(2,1)S(1)} %pad_maximum_fusion.refs_2_) | copy-start | bytes 786436
  52.9 11.9 %collective-permute-start.7 = (bf16[4,256,128]{2,1,0:T(8,128)(2,1)S(1)}, bf16[4,256,128]{2,1,0:T(8,128)(2,1)S(1)}, u32[]{:S(2)}, u32[]{:S(2)}) collective-permute-start(bf16[4,256,128]{2,1,0:T(8,128)(2,1)S(1)} %pad_maximum_fusion.refs_2_), channel_id=1, source_target_pairs={{0,120},{8,0},{16,8},{24,16},{32,24},{40,32},{48,40},{56,48},{64,5... | collective-permute-start | bytes 786440 | tf_op jit(solution)/shard_map/ppermute | solution.py:46
  54.8 9.9 %collective-permute-start.6 = (bf16[4,256,128]{2,1,0:T(8,128)(2,1)S(1)}, bf16[4,256,128]{2,1,0:T(8,128)(2,1)S(1)}, u32[]{:S(2)}, u32[]{:S(2)}) collective-permute-start(bf16[4,256,128]{2,1,0:T(8,128)(2,1)S(1)} %pad_maximum_fusion.refs_2_), channel_id=1, source_target_pairs={{0,8},{8,16},{16,24},{24,32},{32,40},{40,48},{48,56},{56,64},{64,7... | collective-permute-start | bytes 786440 | tf_op jit(solution)/shard_map/ppermute | solution.py:46
  58.2 13.6 %collective-permute-start.9 = (bf16[2,256,128]{2,1,0:T(8,128)(2,1)S(1)}, bf16[2,256,128]{2,1,0:T(8,128)(2,1)S(1)}, u32[]{:S(2)}, u32[]{:S(2)}) collective-permute-start(bf16[2,256,128]{2,1,0:T(8,128)(2,1)S(1)} %get-tuple-element.20), channel_id=1, source_target_pairs={{0,112},{8,120},{16,0},{24,8},{32,16},{40,24},{48,32},{56,40},{64,... | collective-permute-start | bytes 393224 | tf_op jit(solution)/shard_map/ppermute | solution.py:46
  60.2 11.7 %collective-permute-start.8 = (bf16[2,256,128]{2,1,0:T(8,128)(2,1)S(1)}, bf16[2,256,128]{2,1,0:T(8,128)(2,1)S(1)}, u32[]{:S(2)}, u32[]{:S(2)}) collective-permute-start(bf16[2,256,128]{2,1,0:T(8,128)(2,1)S(1)} %get-tuple-element.21), channel_id=1, source_target_pairs={{0,16},{8,24},{16,32},{24,40},{32,48},{40,56},{48,64},{56,72},{64,... | collective-permute-start | bytes 393224 | tf_op jit(solution)/shard_map/ppermute | solution.py:46
  71.9 26.5 %copy-start.2 = (bf16[12,256,128]{2,1,0:T(8,128)(2,1)}, bf16[12,256,128]{2,1,0:T(8,128)(2,1)S(1)}, u32[]{:S(2)}) copy-start(bf16[12,256,128]{2,1,0:T(8,128)(2,1)S(1)} %constant_dynamic-update-slice_fusion.refs_3_) | copy-start | bytes 2359300
  71.9 32.7 %collective-permute-start.12 = (bf16[12,256,128]{2,1,0:T(8,128)(2,1)S(1)}, bf16[12,256,128]{2,1,0:T(8,128)(2,1)S(1)}, u32[]{:S(2)}, u32[]{:S(2)}) collective-permute-start(bf16[12,256,128]{2,1,0:T(8,128)(2,1)S(1)} %constant_dynamic-update-slice_fusion.refs_3_), channel_id=1, source_target_pairs={{0,384},{8,392},{16,400},{24,408},{32,416},{40,424},{48,432},{56,4... | collective-permute-start | bytes 2359304 | tf_op jit(solution)/shard_map/ppermute | solution.py:46
  73.8 32.7 %collective-permute-start.10 = (bf16[12,256,128]{2,1,0:T(8,128)(2,1)S(1)}, bf16[12,256,128]{2,1,0:T(8,128)(2,1)S(1)}, u32[]{:S(2)}, u32[]{:S(2)}) collective-permute-start(bf16[12,256,128]{2,1,0:T(8,128)(2,1)S(1)} %constant_dynamic-update-slice_fusion.refs_3_), channel_id=1, source_target_pairs={{0,128},{8,136},{16,144},{24,152},{32,160},{40,168},{48,176},{56,1... | collective-permute-start | bytes 2359304 | tf_op jit(solution)/shard_map/ppermute | solution.py:46
  79.1 14.0 %collective-permute-start.4 = (bf16[4,256,128]{2,1,0:T(8,128)(2,1)S(1)}, bf16[4,256,128]{2,1,0:T(8,128)(2,1)S(1)}, u32[]{:S(2)}, u32[]{:S(2)}) collective-permute-start(bf16[4,256,128]{2,1,0:T(8,128)(2,1)S(1)} %pad_maximum_fusion.refs_2_), channel_id=1, source_target_pairs={{0,128},{8,136},{16,144},{24,152},{32,160},{40,168},{48,176},{56,1... | collective-permute-start | bytes 786440 | tf_op jit(solution)/shard_map/ppermute | solution.py:46
  82.2 29.0 %collective-permute-start.17 = (bf16[4,256,128]{2,1,0:T(8,128)(2,1)S(1)}, bf16[4,256,128]{2,1,0:T(8,128)(2,1)S(1)}, u32[]{:S(2)}, u32[]{:S(2)}) collective-permute-start(bf16[4,256,128]{2,1,0:T(8,128)(2,1)S(1)} %pad_maximum_fusion.refs_2_), channel_id=1, source_target_pairs={{0,384},{8,392},{16,400},{24,408},{32,416},{40,424},{48,432},{56,4... | collective-permute-start | bytes 786440 | tf_op jit(solution)/shard_map/ppermute | solution.py:46
  93.1 11.5 %copy-start.4 = (bf16[4,256,128]{2,1,0:T(8,128)(2,1)}, bf16[4,256,128]{2,1,0:T(8,128)(2,1)S(1)}, u32[]{:S(2)}) copy-start(bf16[4,256,128]{2,1,0:T(8,128)(2,1)S(1)} %collective-permute-done.4.refs_2_) | copy-start | bytes 786436
  93.1 34.7 %collective-permute-start.5 = (bf16[4,256,128]{2,1,0:T(8,128)(2,1)S(1)}, bf16[4,256,128]{2,1,0:T(8,128)(2,1)}, u32[]{:S(2)}, u32[]{:S(2)}) collective-permute-start(bf16[4,256,128]{2,1,0:T(8,128)(2,1)S(1)} %collective-permute-done.4.refs_2_), channel_id=1, source_target_pairs={{0,128},{8,136},{16,144},{24,152},{32,160},{40,168},{48,176},{56,1... | collective-permute-start | bytes 786440 | tf_op jit(solution)/shard_map/ppermute | solution.py:46
  104.6 6.6 %copy-start = (bf16[12,256,128]{2,1,0:T(8,128)(2,1)}, bf16[12,256,128]{2,1,0:T(8,128)(2,1)S(1)}, u32[]{:S(2)}) copy-start(bf16[12,256,128]{2,1,0:T(8,128)(2,1)S(1)} %collective-permute-done.12.refs_5_) | copy-start | bytes 2359300
  104.6 23.2 %collective-permute-start.13 = (bf16[8,256,128]{2,1,0:T(8,128)(2,1)S(1)}, bf16[8,256,128]{2,1,0:T(8,128)(2,1)}, u32[]{:S(2)}, u32[]{:S(2)}) collective-permute-start(bf16[8,256,128]{2,1,0:T(8,128)(2,1)S(1)} %slice.55), channel_id=1, source_target_pairs={{0,384},{8,392},{16,400},{24,408},{32,416},{40,424},{48,432},{56,4... | collective-permute-start | bytes 1572872 | tf_op jit(solution)/shard_map/ppermute | solution.py:46
  106.6 4.7 %copy-start.1 = (bf16[12,256,128]{2,1,0:T(8,128)(2,1)}, bf16[12,256,128]{2,1,0:T(8,128)(2,1)S(1)}, u32[]{:S(2)}) copy-start(bf16[12,256,128]{2,1,0:T(8,128)(2,1)S(1)} %collective-permute-done.10.refs_4_) | copy-start | bytes 2359300
  106.6 21.2 %collective-permute-start.11 = (bf16[4,256,128]{2,1,0:T(8,128)(2,1)S(1)}, bf16[4,256,128]{2,1,0:T(8,128)(2,1)S(1)}, u32[]{:S(2)}, u32[]{:S(2)}) collective-permute-start(bf16[4,256,128]{2,1,0:T(8,128)(2,1)S(1)} %slice.54), channel_id=1, source_target_pairs={{0,128},{8,136},{16,144},{24,152},{32,160},{40,168},{48,176},{56,1... | collective-permute-start | bytes 786440 | tf_op jit(solution)/shard_map/ppermute | solution.py:46
  111.2 0.7 copy-start.5
  127.8 0.7 copy-start.6
  133.7 57.3 %all-to-all-start = ((bf16[128,2,1,256]{3,1,2,0:T(2,128)(2,1)}), bf16[128,2,1,256]{3,1,2,0:T(2,128)(2,1)S(1)}, u32[]{:S(2)}, u32[]{:S(2)}) async-start(bf16[128,2,1,256]{3,1,2,0:T(2,128)(2,1)} %bitcast.45), calls=%async_computation | async-start | bytes 262144 | tf_op jit(solution)/shard_map/all_to_all | solution.py:382
Sparse Core Ops, SparseCore 0:
  22.9 73.1 all-gather.2

commit v3 on v2

--- a/solution.py
+++ b/solution.py
@@ -13,7 +13,7 @@
 NZ = 16
 N = NX * NZ
 CAP = 192
-ROWS_A = 64
+ROWS_A = 48
 ROWS_B = CAP - ROWS_A
 PAGES = CAP // PAGE
 PAGES_A = ROWS_A // PAGE
@@ -31,12 +31,13 @@
 LIMIT = 64.0 / SCALE
 VMEM_LIMIT = 56 * 1024 * 1024
 
+X_GROUPS = [[x * NZ + z for x in range(NX)] for z in range(NZ)]
 Z_GROUPS = [[x * NZ + z for z in range(NZ)] for x in range(NX)]
-Z_FIRST = [4, 0, -4, 8]
-Z_REST = [3, -1, -5, 7, 5, 1, -3, 9, -2, -6, 6, 2]
-X_A = [0, -1, 1, 2]
-X_B = [0] * 16 + [-1] * 4 + [1] * 4 + [-1] * 12 + [1] * 12 + [2] * 16
-Z_B = (Z_FIRST + Z_REST) + Z_FIRST * 2 + Z_REST * 2 + (Z_FIRST + Z_REST)
+STEP = 4
+STEP_GROUPS = [
+    [x * NZ + r + STEP * j for j in range(NZ // STEP)] for x in range(NX) for r in range(STEP)
+]
+RESIDUES = [0] * 4 + [-1] * 4 + [1] * 4 + [2] * 4
 
 
 def shift(value, dx, dz):
@@ -50,26 +51,29 @@
     return lax.all_gather(value, "ctx", axis=0, tiled=False, axis_index_groups=Z_GROUPS)
 
 
+def share(value, groups):
+    value = jnp.broadcast_to(value[None], (len(groups[0]),) + value.shape)
+    return lax.all_to_all(
+        value, "ctx", split_axis=0, concat_axis=0, tiled=True, axis_index_groups=groups
+    )
+
+
 def exchange(a, b):
-    left4, right4 = shift(b, 0, 4), shift(b, 0, -4)
-    near = [shift(a, dx, 0) for dx in (1, -1, 2)]
-    far4 = jnp.concatenate(
-        [shift(left4[:ROWS_B], 0, 4), shift(right4[ROWS_B:], 0, -4)], axis=0
-    )
-    first = jnp.stack([right4, b, left4, far4])
-    gathered = gather_z(jnp.stack([a] + near)).reshape(N, TALL_A, HD)
-    rest = jnp.concatenate(
-        [shift(first, 0, 1), shift(first, 0, -1), shift(first[1:3], 0, 2), shift(first[0:2], 0, -2)],
+    gathered = gather_z(share(a, X_GROUPS)).reshape(N, TALL_A, HD)
+    first = share(b, STEP_GROUPS)
+    own = jnp.concatenate(
+        [
+            first,
+            shift(first, 0, 1),
+            shift(first, 0, -1),
+            shift(first[:2], 0, 2),
+            shift(first[2:], 0, -2),
+        ],
         axis=0,
     )
-    first_left, first_right = shift(first, 1, 0), shift(first, -1, 0)
-    first_far = shift(first_left, 1, 0)
-    rest_left, rest_right = shift(rest, 1, 0), shift(rest, -1, 0)
-    far_left, far_right = shift(rest_left[:4], 1, 0), shift(rest_right[4:], -1, 0)
-    own = [first, rest]
-    beside = [first_left, first_right, rest_left, rest_right]
-    across = [first_far, far_left, far_right]
-    return gathered, own, beside, across
+    left, right = shift(own, 1, 0), shift(own, -1, 0)
+    far_left, far_right = shift(left[:8], 1, 0), shift(right[8:], -1, 0)
+    return gathered, [own], [left, right], [far_left, far_right]
 
 
 def lanes(rows):
@@ -269,8 +273,16 @@
     )(count, live, *sources, *state)
 
 
-def select_kernel(n_src, key_ref, value_ref, *refs):
-    sources, (out_ref, pages, sems) = refs[:n_src], refs[n_src:]
+def run_attention(
+    gathered, own, beside, across, count_a, count_b, live, arrays, interpret=False
+):
+    state = attention(True, False, count_b[:16], live, own, arrays, interpret)
+    count = jnp.concatenate([count_b[16:48], count_a])
+    state = attention(False, False, count, live, beside + [gathered], state, interpret)
+    return attention(False, True, count_b[48:], live, across, state, interpret)
+
+
+def fetch(sources, pages, sems):
     copies = []
     start = 0
     for i, source in enumerate(sources):
@@ -283,30 +295,58 @@
         copy.start()
     for copy in copies:
         copy.wait()
+    return start
+
+
+def select_kernel(n_src, key_ref, value_ref, *refs):
+    sources, (out_ref, pages, sems) = refs[:n_src], refs[n_src:]
+    total = fetch(sources, pages, sems)
 
     def one(s, carry):
         place = key_ref[s]
-        keep = jnp.where(place >= 0, 1.0, 0.0).astype(jnp.bfloat16)
-        out_ref[s, :, 0:HD] = pages[jnp.maximum(place, 0)] * keep
-        out_ref[s, :, HD : 2 * HD] = pages[jnp.maximum(value_ref[s], 0)] * keep
+        found = (place >= 0) & (place < total)
+        keep = jnp.where(found, 1.0, 0.0).astype(jnp.bfloat16)
+        key = jnp.where(found, place, 0)
+        value = jnp.where(found, value_ref[s], 0)
+        out_ref[s, :, 0:HD] = pages[key] * keep
+        out_ref[s, :, HD : 2 * HD] = pages[value] * keep
         return carry
 
     lax.fori_loop(0, 2 * N, one, 0, unroll=4)
 
 
-def select_pages(key_place, value_place, sources, interpret=False):
+def select_rest_kernel(n_src, base, key_ref, value_ref, piece_ref, old_ref, *refs):
+    sources, (out_ref, pages, sems) = refs[:n_src], refs[n_src:]
+    fetch(sources, pages, sems)
+    out_ref[...] = old_ref[...]
+
+    def one(j, carry):
+        for r in range(2):
+            s = piece_ref[j] * 2 + r
+            place = key_ref[s] - base
+
+            @pl.when(place >= 0)
+            def _():
+                out_ref[s, :, 0:HD] = pages[place]
+                out_ref[s, :, HD : 2 * HD] = pages[value_ref[s] - base]
+
+        return carry
+
+    lax.fori_loop(0, 16, one, 0)
+
+
+def select_call(kernel, scalars, arrays, sources, interpret):
     sources = [s.reshape(s.shape[0] * s.shape[1] // PAGE, PAGE, HD) for s in sources]
     total = sum(s.shape[0] for s in sources)
     smem = pl.BlockSpec(memory_space=pltpu.SMEM)
-
-    def kernel(*refs):
-        select_kernel(len(sources), *refs)
-
+    vmem = pl.BlockSpec(memory_space=pltpu.VMEM)
     return pl.pallas_call(
         kernel,
         out_shape=jax.ShapeDtypeStruct((2 * N, PAGE, 2 * HD), jnp.bfloat16),
-        in_specs=[smem, smem] + [pl.BlockSpec(memory_space=pl.ANY)] * len(sources),
-        out_specs=pl.BlockSpec(memory_space=pltpu.VMEM),
+        in_specs=[smem] * len(scalars)
+        + [vmem] * len(arrays)
+        + [pl.BlockSpec(memory_space=pl.ANY)] * len(sources),
+        out_specs=vmem,
         scratch_shapes=[
             pltpu.VMEM((total, PAGE, HD), jnp.bfloat16),
             pltpu.SemaphoreType.DMA((len(sources),)),
@@ -314,7 +354,22 @@
         compiler_params=pltpu.CompilerParams(vmem_limit_bytes=VMEM_LIMIT),
         cost_estimate=pl.CostEstimate(flops=0, bytes_accessed=8 << 20, transcendentals=0),
         interpret=interpret,
-    )(key_place, value_place, *sources)
+    )(*scalars, *arrays, *sources)
+
+
+def select_pages(key_place, value_place, near, far, piece_far, interpret=False):
+    base = sum(s.shape[0] * s.shape[1] // PAGE for s in near)
+
+    def kernel(*refs):
+        select_kernel(len(near), *refs)
+
+    def rest_kernel(*refs):
+        select_rest_kernel(len(far), base, *refs)
+
+    out = select_call(kernel, (key_place, value_place), (), near, interpret)
+    return select_call(
+        rest_kernel, (key_place, value_place, piece_far), (out,), far, interpret
+    )
 
 
 def payloads(keys, values, page_owner):
@@ -327,10 +382,11 @@
 
 def layout(me):
     mx, mz = me // NZ, me % NZ
-    dx, dz = jnp.array(X_B, jnp.int32), jnp.array(Z_B, jnp.int32)
-    piece_b = ((mx + dx + NX) % NX) * NZ + (mz + dz + NZ) % NZ
-    dx = jnp.array(X_A * NZ, jnp.int32)
-    piece_a = ((mx + dx + NX) % NX) * NZ + jnp.arange(N, dtype=jnp.int32) // NX
+    place = jnp.arange(N, dtype=jnp.int32)
+    dx = jnp.array([0] * 16 + [-1] * 16 + [1] * 16 + [2] * 16, jnp.int32)
+    residue = (mz + jnp.array(RESIDUES * NX, jnp.int32) + NZ) % STEP
+    piece_b = ((mx + dx + NX) % NX) * NZ + residue + STEP * (place % 4)
+    piece_a = (place % NX) * NZ + place // NX
     return piece_a, piece_b
 
 
@@ -378,14 +434,14 @@
     piece_a, piece_b = layout(me)
     count_a, count_b = live_counts(me, lengths, piece_a, piece_b)
     key_place, value_place = page_places(me, gathered, piece_a, piece_b, lengths)
-    outgoing = select_pages(key_place, value_place, [gathered] + own + beside + across)
+    outgoing = select_pages(
+        key_place, value_place, [gathered] + own + beside, across, piece_b[48:]
+    )
     decode_cache = lax.all_to_all(
         outgoing.reshape(2 * N, PAGE, 1, 2 * HD), "tp", split_axis=0, concat_axis=2, tiled=True
     )
-    state = attention(True, False, count_b[:16], live, own, (queries, keys, values))
-    state = attention(False, False, count_b[16:48], live, beside, state)
-    attended = attention(
-        False, True, jnp.concatenate([count_b[48:], count_a]), live, across + [gathered], state
+    attended = run_attention(
+        gathered, own, beside, across, count_a, count_b, live, (queries, keys, values)
     )
     return (attended, decode_cache.reshape((1,) + decode_cache.shape))
 

time: 200 us -> 202 us (1.010)
  the two profiles are of different devices: /device:TPU:143 before, /device:TPU:487 now
where the time goes in v3:
time: 202 us; the launch traced here: 201 us
  Pallas kernels  83.2 us (41%)
  starting transfers between devices  49.8 us (25%)
  waiting for transfers between devices  29.9 us (15%)
  between operations  14.4 us (7%)
  local copies, waits for them, and re-layouts  10 us (5%)
  blocking collectives  7.07 us (4%)
  other arithmetic  6.33 us (3%)
    pallas_call x3, Pallas kernels, attention(): pl.pallas_call(kernel, out_shape=out_shape, in_specs=[smem, smem] + [pl.B...  75 us
    ppermute x8, starting transfers between devices, shift(): return lax.ppermute(value, 'ctx', pairs)  31.9 us
    ppermute x8, waiting for transfers between devices, shift(): return lax.ppermute(value, 'ctx', pairs)  19.2 us
    all_to_all x1, waiting for transfers between devices, share(): lax.all_to_all(value, 'ctx', split_axis=0, concat_axis=0, tiled=True, axi...  10.6 us
    all_to_all x1, starting transfers between devices, share(): lax.all_to_all(value, 'ctx', split_axis=0, concat_axis=0, tiled=True, axi...  9.63 us
    all_to_all x1, starting transfers between devices, body(): lax.all_to_all(outgoing.reshape(2 * N, PAGE, 1, 2 * HD), 'tp', split_axis...  8.19 us
    pallas_call x2, Pallas kernels, select_call(): pl.pallas_call(kernel, out_shape=jax.ShapeDtypeStruct((2 * N, PAGE, 2 * H...  8.17 us
    all_to_all x1, blocking collectives, share(): lax.all_to_all(value, 'ctx', split_axis=0, concat_axis=0, tiled=True, axi...  7.07 us
  transfers between devices with their start and end apart: 11, of which 5 were waited for; matrix products, arithmetic and copies ran while one was open for 6% of the time, Pallas kernels for 40%

profile of v3, /device:TPU:487, one launch (start us, length us, event | category | flops | bytes accessed | tf_op | source)
XLA Modules:
  0.0 200.7 jit_solution(2790815719984404844)
XLA Ops:
  7.9 0.7 slice.47
  8.6 0.7 slice.48
  9.4 7.1 %all_to_all.25 = bf16[4,112,128]{2,1,0:T(8,128)(2,1)} all-to-all(bf16[4,112,128]{2,1,0:T(8,128)(2,1)S(1)} %broadcast_in_dim.124), channel_id=1, replica_groups={{0,128,256,384},{8,136,264,392},{16,144,272,400},{24,152,280,408},{32,1..., dimensions={0} | all-to-all | bytes 229376 | tf_op jit(solution)/shard_map/all_to_all | solution.py:56
  16.5 0.8 slice.40
  17.2 0.8 slice.41
  18.0 0.8 broadcast_in_dim.122
  18.8 9.6 %all-to-all-start = ((bf16[4,288,128]{2,1,0:T(8,128)(2,1)}), bf16[4,288,128]{2,1,0:T(8,128)(2,1)S(1)}, u32[]{:S(2)}, u32[]{:S(2)}) async-start(bf16[4,288,128]{2,1,0:T(8,128)(2,1)} %broadcast_in_dim.122), calls=%async_computation | async-start | bytes 589824 | tf_op jit(solution)/shard_map/all_to_all | solution.py:56
  30.8 10.6 %all-to-all-done = bf16[4,288,128]{2,1,0:T(8,128)(2,1)S(1)} async-done(((bf16[4,288,128]{2,1,0:T(8,128)(2,1)}), bf16[4,288,128]{2,1,0:T(8,128)(2,1)S(1)}, u32[]{:S(2)}, u32[]{:S(2)}) %all-to-all-start) | async-done | bytes 294944 | tf_op jit(solution)/shard_map/all_to_all | solution.py:56
  41.5 8.9 %collective-permute-start.1 = (bf16[4,288,128]{2,1,0:T(8,128)(2,1)S(1)}, bf16[4,288,128]{2,1,0:T(8,128)(2,1)S(1)}, u32[]{:S(2)}, u32[]{:S(2)}) collective-permute-start(bf16[4,288,128]{2,1,0:T(8,128)(2,1)S(1)} %all-to-all-done), channel_id=1, source_target_pairs={{0,120},{8,0},{16,8},{24,16},{32,24},{40,32},{48,40},{56,48},{64,5... | collective-permute-start | bytes 884744 | tf_op jit(solution)/shard_map/ppermute | solution.py:47
  50.4 1.9 collective-permute-start
  52.4 3.1 %collective-permute-start.3 = (bf16[2,288,128]{2,1,0:T(8,128)(2,1)S(1)}, bf16[2,288,128]{2,1,0:T(8,128)(2,1)S(1)}, u32[]{:S(2)}, u32[]{:S(2)}) collective-permute-start(bf16[2,288,128]{2,1,0:T(8,128)(2,1)S(1)} %get-tuple-element.20), channel_id=1, source_target_pairs={{0,112},{8,120},{16,0},{24,8},{32,16},{40,24},{48,32},{56,40},{64,... | collective-permute-start | bytes 442376 | tf_op jit(solution)/shard_map/ppermute | solution.py:47
  55.5 5.0 %collective-permute-start.2 = (bf16[2,288,128]{2,1,0:T(8,128)(2,1)S(1)}, bf16[2,288,128]{2,1,0:T(8,128)(2,1)S(1)}, u32[]{:S(2)}, u32[]{:S(2)}) collective-permute-start(bf16[2,288,128]{2,1,0:T(8,128)(2,1)S(1)} %get-tuple-element.21), channel_id=1, source_target_pairs={{0,16},{8,24},{16,32},{24,40},{32,48},{40,56},{48,64},{56,72},{64,... | collective-permute-start | bytes 442376 | tf_op jit(solution)/shard_map/ppermute | solution.py:47
  60.5 1.3 collective-permute-done
  61.9 8.4 %collective-permute-done.2 = bf16[2,288,128]{2,1,0:T(8,128)(2,1)S(1)} collective-permute-done((bf16[2,288,128]{2,1,0:T(8,128)(2,1)S(1)}, bf16[2,288,128]{2,1,0:T(8,128)(2,1)S(1)}, u32[]{:S(2)}, u32[]{:S(2)}) %collective-permute-start.2) | collective-permute-done | bytes 147488 | tf_op jit(solution)/shard_map/ppermute | solution.py:47
  70.4 3.3 %collective-permute-start.6 = (bf16[16,288,128]{2,1,0:T(8,128)(2,1)S(1)}, bf16[16,288,128]{2,1,0:T(8,128)(2,1)S(1)}, u32[]{:S(2)}, u32[]{:S(2)}) collective-permute-start(bf16[16,288,128]{2,1,0:T(8,128)(2,1)S(1)} %constant_dynamic-update-slice_fusion.refs_2_), channel_id=1, source_target_pairs={{0,384},{8,392},{16,400},{24,408},{32,416},{40,424},{48,432},{56,4... | collective-permute-start | bytes 3538952 | tf_op jit(solution)/shard_map/ppermute | solution.py:47
  73.7 3.1 %collective-permute-start.4 = (bf16[16,288,128]{2,1,0:T(8,128)(2,1)S(1)}, bf16[16,288,128]{2,1,0:T(8,128)(2,1)S(1)}, u32[]{:S(2)}, u32[]{:S(2)}) collective-permute-start(bf16[16,288,128]{2,1,0:T(8,128)(2,1)S(1)} %constant_dynamic-update-slice_fusion.refs_2_), channel_id=1, source_target_pairs={{0,128},{8,136},{16,144},{24,152},{32,160},{40,168},{48,176},{56,1... | collective-permute-start | bytes 3538952 | tf_op jit(solution)/shard_map/ppermute | solution.py:47
  78.1 0.7 fusion.4
  78.8 1.2 broadcast_multiply_fusion
  80.6 8.6 %shard_map.86 = (bf16[1536,256]{1,0:T(8,128)(2,1)}, f32[1536,128]{1,0:T(8,128)}, f32[1536,128]{1,0:T(8,128)}) custom-call(s32[16]{0:T(128)} %get-tuple-element.26.refs_0_, s32[1]{0:T(128)} %bitcast.refs_1_, bf16[16,288,128]{2,1,0:T(8,128)(2,1)} %copy-done.2, bf16[192,1024]{1,0:T(8,128)(2,1)} %refs_3_.1, bf16[192,128]{1,0:T(8,128)(2,1)} %refs_4_.1, ...), custom_call_target="tpu_custom_call" | custom-call | flops 3623878656 | bytes 8388608 | tf_op jit(solution)/shard_map/pallas_call | solution.py:262
  89.2 7.3 %collective-permute-done.6.refs_3_ = bf16[16,288,128]{2,1,0:T(8,128)(2,1)S(1)} collective-permute-done((bf16[16,288,128]{2,1,0:T(8,128)(2,1)S(1)}, bf16[16,288,128]{2,1,0:T(8,128)(2,1)S(1)}, u32[]{:S(2)}, u32[]{:S(2)}) %collective-permute-start.6) | collective-permute-done | bytes 1179680 | tf_op jit(solution)/shard_map/ppermute | solution.py:47
  96.5 1.0 slice.55
  97.5 3.8 %collective-permute-start.7 = (bf16[8,288,128]{2,1,0:T(8,128)(2,1)}, bf16[8,288,128]{2,1,0:T(8,128)(2,1)}, u32[]{:S(2)}, u32[]{:S(2)}) collective-permute-start(bf16[8,288,128]{2,1,0:T(8,128)(2,1)} %slice.55), channel_id=1, source_target_pairs={{0,384},{8,392},{16,400},{24,408},{32,416},{40,424},{48,432},{56,4... | collective-permute-start | bytes 1769480 | tf_op jit(solution)/shard_map/ppermute | solution.py:47
  101.4 2.6 %collective-permute-start.5 = (bf16[8,288,128]{2,1,0:T(8,128)(2,1)S(1)}, bf16[8,288,128]{2,1,0:T(8,128)(2,1)S(1)}, u32[]{:S(2)}, u32[]{:S(2)}) collective-permute-start(bf16[8,288,128]{2,1,0:T(8,128)(2,1)S(1)} %slice.54), channel_id=1, source_target_pairs={{0,128},{8,136},{16,144},{24,152},{32,160},{40,168},{48,176},{56,1... | collective-permute-start | bytes 1769480 | tf_op jit(solution)/shard_map/ppermute | solution.py:47
  104.1 0.9 slice.56
  107.2 4.8 %shard_map.89.refs_3_ = bf16[128,2,256]{2,1,0:T(2,128)(2,1)} custom-call(s32[128]{0:T(128)} %get-tuple-element.23.refs_0_, s32[128]{0:T(128)} %get-tuple-element.22.refs_1_, bf16[3584,2,128]{2,1,0:T(2,128)(2,1)} %bitcast.27, bf16[2304,2,128]{2,1,0:T(2,128)(2,1)} %bitcast.28, bf16[2304,2,128]{2,1,0:T(2,128)(2,1)} %bitcast.26, bf16[2304,2,128]{2,1,0:T(2,128)(2,1)} %bitcast.25), custom_call_target="tpu_custom_call" | custom-call | bytes 8388608 | tf_op jit(solution)/shard_map/pallas_call | solution.py:343
  112.1 2.2 %collective-permute-done.5.refs_2_ = bf16[8,288,128]{2,1,0:T(8,128)(2,1)S(1)} collective-permute-done((bf16[8,288,128]{2,1,0:T(8,128)(2,1)S(1)}, bf16[8,288,128]{2,1,0:T(8,128)(2,1)S(1)}, u32[]{:S(2)}, u32[]{:S(2)}) %collective-permute-start.5) | collective-permute-done | bytes 589856 | tf_op jit(solution)/shard_map/ppermute | solution.py:47
  114.3 0.8 copy-done.3
  115.1 3.3 %shard_map.90 = bf16[128,2,256]{2,1,0:T(2,128)(2,1)} custom-call(s32[128]{0:T(128)} %get-tuple-element.23.refs_0_, s32[128]{0:T(128)} %get-tuple-element.22.refs_1_, s32[16]{0:T(128)} %slice.51.refs_2_, bf16[128,2,256]{2,1,0:T(2,128)(2,1)} %shard_map.89.refs_3_, bf16[1152,2,128]{2,1,0:T(2,128)(2,1)} %bitcast.29, bf16[1152,2,128]{2,1,0:T(2,128)(2,1)} %bitcast.10.refs_5_), custom_call_target="tpu_custom_call" | custom-call | bytes 8388608 | tf_op jit(solution)/shard_map/pallas_call | solution.py:343
  118.5 8.2 %all-to-all-start.2 = ((bf16[128,2,1,256]{3,1,2,0:T(2,128)(2,1)}), bf16[128,2,1,256]{3,1,2,0:T(2,128)(2,1)S(1)}, u32[]{:S(2)}, u32[]{:S(2)}) async-start(bf16[128,2,1,256]{3,1,2,0:T(2,128)(2,1)} %bitcast.30), calls=%async_computation.2 | async-start | bytes 262144 | tf_op jit(solution)/shard_map/all_to_all | solution.py:440
  126.6 56.3 %shard_map.87 = (bf16[1536,256]{1,0:T(8,128)(2,1)}, f32[1536,128]{1,0:T(8,128)}, f32[1536,128]{1,0:T(8,128)}) custom-call(s32[96]{0:T(128)} %pad_add_fusion.1.refs_0_, s32[1]{0:T(128)} %bitcast.refs_1_, bf16[16,288,128]{2,1,0:T(8,128)(2,1)} %copy-done.1, bf16[16,288,128]{2,1,0:T(8,128)(2,1)} %copy-done, ...), custom_call_target="tpu_custom_call" | custom-call | flops 12079595520 | bytes 8388608 | tf_op jit(solution)/shard_map/pallas_call | solution.py:262
  183.0 10.1 %shard_map.88 = bf16[192,1024]{1,0:T(8,128)(2,1)} custom-call(s32[16]{0:T(128)} %get-tuple-element.27.refs_0_, s32[1]{0:T(128)} %bitcast.refs_1_, bf16[8,288,128]{2,1,0:T(8,128)(2,1)} %copy-done.3, bf16[8,288,128]{2,1,0:T(8,128)(2,1)} %collective-permute-done.7.refs_3_, bf16[1536,256]{1,0:T(8,128)(2,1)} %get-tuple-element.11.refs_4_, ...), custom_call_target="tpu_custom_call" | custom-call | flops 3623878656 | bytes 8388608 | tf_op jit(solution)/shard_map/pallas_call | solution.py:262
  193.1 0.7 copy.26
  (63 shorter events, 7.4 us)
Async XLA Ops:
  7.2 21.2 %copy-start.6 = (s32[64]{0:T(128)S(1)}, s32[64]{0:T(128)}, u32[]{:S(2)}) copy-start(s32[64]{0:T(128)} %constant.120.clone) | copy-start | bytes 772
  7.2 21.2 %copy-start.7 = (s32[64]{0:T(128)S(1)}, s32[64]{0:T(128)}, u32[]{:S(2)}) copy-start(s32[64]{0:T(128)} %constant.119.clone) | copy-start | bytes 772
  7.2 21.2 %copy-start.4 = (s32[64]{0:T(128)S(1)}, s32[64]{0:T(128)}, u32[]{:S(2)}) copy-start(s32[64]{0:T(128)} %param.10) | copy-start | bytes 772
  7.2 96.9 %all-gather.3.cloned.1.call-start = ((), (), s32[]{:S(2)}) async-start(), calls=%async_computation.3 | async-start | bytes 1949696 | tf_op jit(solution)/shard_map/all_gather | solution.py:51
  18.8 22.7 %all-to-all-start = ((bf16[4,288,128]{2,1,0:T(8,128)(2,1)}), bf16[4,288,128]{2,1,0:T(8,128)(2,1)S(1)}, u32[]{:S(2)}, u32[]{:S(2)}) async-start(bf16[4,288,128]{2,1,0:T(8,128)(2,1)} %broadcast_in_dim.122), calls=%async_computation | async-start | bytes 589824 | tf_op jit(solution)/shard_map/all_to_all | solution.py:56
  41.5 20.4 %collective-permute-start.1 = (bf16[4,288,128]{2,1,0:T(8,128)(2,1)S(1)}, bf16[4,288,128]{2,1,0:T(8,128)(2,1)S(1)}, u32[]{:S(2)}, u32[]{:S(2)}) collective-permute-start(bf16[4,288,128]{2,1,0:T(8,128)(2,1)S(1)} %all-to-all-done), channel_id=1, source_target_pairs={{0,120},{8,0},{16,8},{24,16},{32,24},{40,32},{48,40},{56,48},{64,5... | collective-permute-start | bytes 884744 | tf_op jit(solution)/shard_map/ppermute | solution.py:47
  50.4 11.4 %collective-permute-start = (bf16[4,288,128]{2,1,0:T(8,128)(2,1)S(1)}, bf16[4,288,128]{2,1,0:T(8,128)(2,1)S(1)}, u32[]{:S(2)}, u32[]{:S(2)}) collective-permute-start(bf16[4,288,128]{2,1,0:T(8,128)(2,1)S(1)} %all-to-all-done), channel_id=1, source_target_pairs={{0,8},{8,16},{16,24},{24,32},{32,40},{40,48},{48,56},{56,64},{64,7... | collective-permute-start | bytes 884744 | tf_op jit(solution)/shard_map/ppermute | solution.py:47
  52.4 18.0 %collective-permute-start.3 = (bf16[2,288,128]{2,1,0:T(8,128)(2,1)S(1)}, bf16[2,288,128]{2,1,0:T(8,128)(2,1)S(1)}, u32[]{:S(2)}, u32[]{:S(2)}) collective-permute-start(bf16[2,288,128]{2,1,0:T(8,128)(2,1)S(1)} %get-tuple-element.20), channel_id=1, source_target_pairs={{0,112},{8,120},{16,0},{24,8},{32,16},{40,24},{48,32},{56,40},{64,... | collective-permute-start | bytes 442376 | tf_op jit(solution)/shard_map/ppermute | solution.py:47
  55.5 21.4 %copy-start.8 = (s32[32]{0:T(128)S(1)}, s32[32]{0:T(128)}, u32[]{:S(2)}) copy-start(s32[32]{0:T(128)} %slice.46) | copy-start | bytes 388
  55.5 21.4 %copy-start.9 = (s32[64]{0:T(128)S(1)}, s32[64]{0:T(128)}, u32[]{:S(2)}) copy-start(s32[64]{0:T(128)} %compare_select_fusion.5) | copy-start | bytes 772
  55.5 14.8 %collective-permute-start.2 = (bf16[2,288,128]{2,1,0:T(8,128)(2,1)S(1)}, bf16[2,288,128]{2,1,0:T(8,128)(2,1)S(1)}, u32[]{:S(2)}, u32[]{:S(2)}) collective-permute-start(bf16[2,288,128]{2,1,0:T(8,128)(2,1)S(1)} %get-tuple-element.21), channel_id=1, source_target_pairs={{0,16},{8,24},{16,32},{24,40},{32,48},{40,56},{48,64},{56,72},{64,... | collective-permute-start | bytes 442376 | tf_op jit(solution)/shard_map/ppermute | solution.py:47
  70.4 10.2 %copy-start.2 = (bf16[16,288,128]{2,1,0:T(8,128)(2,1)}, bf16[16,288,128]{2,1,0:T(8,128)(2,1)S(1)}, u32[]{:S(2)}) copy-start(bf16[16,288,128]{2,1,0:T(8,128)(2,1)S(1)} %constant_dynamic-update-slice_fusion.refs_2_) | copy-start | bytes 3538948
  70.4 26.1 %collective-permute-start.6 = (bf16[16,288,128]{2,1,0:T(8,128)(2,1)S(1)}, bf16[16,288,128]{2,1,0:T(8,128)(2,1)S(1)}, u32[]{:S(2)}, u32[]{:S(2)}) collective-permute-start(bf16[16,288,128]{2,1,0:T(8,128)(2,1)S(1)} %constant_dynamic-update-slice_fusion.refs_2_), channel_id=1, source_target_pairs={{0,384},{8,392},{16,400},{24,408},{32,416},{40,424},{48,432},{56,4... | collective-permute-start | bytes 3538952 | tf_op jit(solution)/shard_map/ppermute | solution.py:47
  73.7 27.6 %collective-permute-start.4 = (bf16[16,288,128]{2,1,0:T(8,128)(2,1)S(1)}, bf16[16,288,128]{2,1,0:T(8,128)(2,1)S(1)}, u32[]{:S(2)}, u32[]{:S(2)}) collective-permute-start(bf16[16,288,128]{2,1,0:T(8,128)(2,1)S(1)} %constant_dynamic-update-slice_fusion.refs_2_), channel_id=1, source_target_pairs={{0,128},{8,136},{16,144},{24,152},{32,160},{40,168},{48,176},{56,1... | collective-permute-start | bytes 3538952 | tf_op jit(solution)/shard_map/ppermute | solution.py:47
  89.2 16.4 %copy-start.5 = (s32[64]{0:T(128)S(1)}, s32[64]{0:T(128)}, u32[]{:S(2)}) copy-start(s32[64]{0:T(128)} %get-tuple-element.29) | copy-start | bytes 772
  96.5 4.9 %copy-start = (bf16[16,288,128]{2,1,0:T(8,128)(2,1)}, bf16[16,288,128]{2,1,0:T(8,128)(2,1)S(1)}, u32[]{:S(2)}) copy-start(bf16[16,288,128]{2,1,0:T(8,128)(2,1)S(1)} %collective-permute-done.6.refs_3_) | copy-start | bytes 3538948
  97.5 14.6 %collective-permute-start.7 = (bf16[8,288,128]{2,1,0:T(8,128)(2,1)}, bf16[8,288,128]{2,1,0:T(8,128)(2,1)}, u32[]{:S(2)}, u32[]{:S(2)}) collective-permute-start(bf16[8,288,128]{2,1,0:T(8,128)(2,1)} %slice.55), channel_id=1, source_target_pairs={{0,384},{8,392},{16,400},{24,408},{32,416},{40,424},{48,432},{56,4... | collective-permute-start | bytes 1769480 | tf_op jit(solution)/shard_map/ppermute | solution.py:47
  101.3 5.9 %copy-start.1 = (bf16[16,288,128]{2,1,0:T(8,128)(2,1)}, bf16[16,288,128]{2,1,0:T(8,128)(2,1)S(1)}, u32[]{:S(2)}) copy-start(bf16[16,288,128]{2,1,0:T(8,128)(2,1)S(1)} %collective-permute-done.4.refs_2_) | copy-start | bytes 3538948
  101.4 12.9 %collective-permute-start.5 = (bf16[8,288,128]{2,1,0:T(8,128)(2,1)S(1)}, bf16[8,288,128]{2,1,0:T(8,128)(2,1)S(1)}, u32[]{:S(2)}, u32[]{:S(2)}) collective-permute-start(bf16[8,288,128]{2,1,0:T(8,128)(2,1)S(1)} %slice.54), channel_id=1, source_target_pairs={{0,128},{8,136},{16,144},{24,152},{32,160},{40,168},{48,176},{56,1... | collective-permute-start | bytes 1769480 | tf_op jit(solution)/shard_map/ppermute | solution.py:47
  114.3 0.8 copy-start.3
  118.5 74.6 %all-to-all-start.2 = ((bf16[128,2,1,256]{3,1,2,0:T(2,128)(2,1)}), bf16[128,2,1,256]{3,1,2,0:T(2,128)(2,1)S(1)}, u32[]{:S(2)}, u32[]{:S(2)}) async-start(bf16[128,2,1,256]{3,1,2,0:T(2,128)(2,1)} %bitcast.30), calls=%async_computation.2 | async-start | bytes 262144 | tf_op jit(solution)/shard_map/all_to_all | solution.py:440
Sparse Core Ops, SparseCore 0:
  16.6 71.6 all-gather.2

commit v4 on v3

--- a/solution.py
+++ b/solution.py
@@ -13,7 +13,7 @@
 NZ = 16
 N = NX * NZ
 CAP = 192
-ROWS_A = 48
+ROWS_A = 64
 ROWS_B = CAP - ROWS_A
 PAGES = CAP // PAGE
 PAGES_A = ROWS_A // PAGE
@@ -31,13 +31,11 @@
 LIMIT = 64.0 / SCALE
 VMEM_LIMIT = 56 * 1024 * 1024
 
-X_GROUPS = [[x * NZ + z for x in range(NX)] for z in range(NZ)]
+X_ORDER = [0, -1, 1, 2]
+Z_ORDER = [4, 0, -4, 8]
 Z_GROUPS = [[x * NZ + z for z in range(NZ)] for x in range(NX)]
 STEP = 4
-STEP_GROUPS = [
-    [x * NZ + r + STEP * j for j in range(NZ // STEP)] for x in range(NX) for r in range(STEP)
-]
-RESIDUES = [0] * 4 + [-1] * 4 + [1] * 4 + [2] * 4
+Z_ALL = [d + s for d in (0, -1, 1) for s in Z_ORDER] + [-2, -6, 6, 2]
 
 
 def shift(value, dx, dz):
@@ -51,23 +49,19 @@
     return lax.all_gather(value, "ctx", axis=0, tiled=False, axis_index_groups=Z_GROUPS)
 
 
-def share(value, groups):
-    value = jnp.broadcast_to(value[None], (len(groups[0]),) + value.shape)
-    return lax.all_to_all(
-        value, "ctx", split_axis=0, concat_axis=0, tiled=True, axis_index_groups=groups
-    )
-
-
 def exchange(a, b):
-    gathered = gather_z(share(a, X_GROUPS)).reshape(N, TALL_A, HD)
-    first = share(b, STEP_GROUPS)
+    near = [shift(a, dx, 0) for dx in (1, -1, 2)]
+    left, right = shift(b, 0, 4), shift(b, 0, -4)
+    gathered = gather_z(jnp.stack([a] + near)).reshape(N, TALL_A, HD)
+    far = jnp.concatenate([shift(left[:ROWS_B], 0, 4), shift(right[ROWS_B:], 0, -4)], axis=0)
+    first = jnp.stack([right, b, left, far])
     own = jnp.concatenate(
         [
             first,
             shift(first, 0, 1),
             shift(first, 0, -1),
-            shift(first[:2], 0, 2),
-            shift(first[2:], 0, -2),
+            shift(first[1:3], 0, 2),
+            shift(first[:2], 0, -2),
         ],
         axis=0,
     )
@@ -273,12 +267,13 @@
     )(count, live, *sources, *state)
 
 
-def run_attention(
-    gathered, own, beside, across, count_a, count_b, live, arrays, interpret=False
-):
+def early_attention(gathered, own, beside, count_a, count_b, live, arrays, interpret=False):
     state = attention(True, False, count_b[:16], live, own, arrays, interpret)
-    count = jnp.concatenate([count_b[16:48], count_a])
-    state = attention(False, False, count, live, beside + [gathered], state, interpret)
+    state = attention(False, False, count_b[16:48], live, beside, state, interpret)
+    return attention(False, False, count_a, live, [gathered], state, interpret)
+
+
+def late_attention(across, count_b, live, state, interpret=False):
     return attention(False, True, count_b[48:], live, across, state, interpret)
 
 
@@ -315,78 +310,95 @@
     lax.fori_loop(0, 2 * N, one, 0, unroll=4)
 
 
-def select_rest_kernel(n_src, base, key_ref, value_ref, piece_ref, old_ref, *refs):
+def select_rest_kernel(n_src, base, key_ref, value_ref, old_ref, after_ref, *refs):
     sources, (out_ref, pages, sems) = refs[:n_src], refs[n_src:]
     fetch(sources, pages, sems)
     out_ref[...] = old_ref[...]
 
-    def one(j, carry):
-        for r in range(2):
-            s = piece_ref[j] * 2 + r
-            place = key_ref[s] - base
-
-            @pl.when(place >= 0)
-            def _():
-                out_ref[s, :, 0:HD] = pages[place]
-                out_ref[s, :, HD : 2 * HD] = pages[value_ref[s] - base]
+    def one(s, carry):
+        place = key_ref[s] - base
+
+        @pl.when(place >= 0)
+        def _():
+            out_ref[s, :, 0:HD] = pages[place]
+            out_ref[s, :, HD : 2 * HD] = pages[value_ref[s] - base]
 
         return carry
 
-    lax.fori_loop(0, 16, one, 0)
+    lax.fori_loop(0, 2 * N, one, 0, unroll=2)
 
 
 def select_call(kernel, scalars, arrays, sources, interpret):
-    sources = [s.reshape(s.shape[0] * s.shape[1] // PAGE, PAGE, HD) for s in sources]
     total = sum(s.shape[0] for s in sources)
     smem = pl.BlockSpec(memory_space=pltpu.SMEM)
     vmem = pl.BlockSpec(memory_space=pltpu.VMEM)
+    anywhere = pl.BlockSpec(memory_space=pl.ANY)
     return pl.pallas_call(
         kernel,
         out_shape=jax.ShapeDtypeStruct((2 * N, PAGE, 2 * HD), jnp.bfloat16),
         in_specs=[smem] * len(scalars)
-        + [vmem] * len(arrays)
-        + [pl.BlockSpec(memory_space=pl.ANY)] * len(sources),
+        + [vmem, anywhere][: len(arrays)]
+        + [anywhere] * len(sources),
         out_specs=vmem,
         scratch_shapes=[
             pltpu.VMEM((total, PAGE, HD), jnp.bfloat16),
             pltpu.SemaphoreType.DMA((len(sources),)),
         ],
         compiler_params=pltpu.CompilerParams(vmem_limit_bytes=VMEM_LIMIT),
-        cost_estimate=pl.CostEstimate(flops=0, bytes_accessed=8 << 20, transcendentals=0),
+        cost_estimate=pl.CostEstimate(flops=0, bytes_accessed=4 << 20, transcendentals=0),
         interpret=interpret,
     )(*scalars, *arrays, *sources)
 
 
-def select_pages(key_place, value_place, near, far, piece_far, interpret=False):
-    base = sum(s.shape[0] * s.shape[1] // PAGE for s in near)
+def as_pages(sources):
+    return [s.reshape(s.shape[0] * s.shape[1] // PAGE, PAGE, HD) for s in sources]
+
+
+def select_pages(places, near, rest, after, interpret=False):
+    near, rest = as_pages(near), as_pages(rest)
+    base = sum(s.shape[0] for s in near)
 
     def kernel(*refs):
         select_kernel(len(near), *refs)
 
     def rest_kernel(*refs):
-        select_rest_kernel(len(far), base, *refs)
-
-    out = select_call(kernel, (key_place, value_place), (), near, interpret)
-    return select_call(
-        rest_kernel, (key_place, value_place, piece_far), (out,), far, interpret
-    )
-
-
-def payloads(keys, values, page_owner):
-    owner = page_owner[:, 0].astype(jnp.bfloat16)
-    owner = jnp.broadcast_to(jnp.pad(owner, (0, HD - PAGES))[None, :], (PAD, HD))
-    a = jnp.concatenate([keys[:ROWS_A], values[:ROWS_A], owner], axis=0)
-    b = jnp.concatenate([keys[ROWS_A:], values[ROWS_A:]], axis=0)
-    return a, b
+        select_rest_kernel(len(rest), base, *refs)
+
+    out = select_call(kernel, places, (), near, interpret)
+    return select_call(rest_kernel, places, (out, after), rest, interpret)
+
+
+def payload_kernel(k_ref, v_ref, owner_ref, a_ref, b_ref):
+    a_ref[0:ROWS_A, :] = k_ref[0:ROWS_A, :]
+    a_ref[ROWS_A : 2 * ROWS_A, :] = v_ref[0:ROWS_A, :]
+    a_ref[2 * ROWS_A :, :] = jnp.zeros((PAD, HD), jnp.bfloat16)
+    owner = jnp.broadcast_to(owner_ref[...].astype(jnp.float32), (PAD, PAGES))
+    a_ref[2 * ROWS_A :, 0:PAGES] = owner.astype(jnp.bfloat16)
+    b_ref[0:ROWS_B, :] = k_ref[ROWS_A:, :]
+    b_ref[ROWS_B:, :] = v_ref[ROWS_A:, :]
+
+
+def payloads(keys, values, page_owner, interpret=False):
+    vmem = pl.BlockSpec(memory_space=pltpu.VMEM)
+    return pl.pallas_call(
+        payload_kernel,
+        out_shape=[
+            jax.ShapeDtypeStruct((TALL_A, HD), jnp.bfloat16),
+            jax.ShapeDtypeStruct((TALL_B, HD), jnp.bfloat16),
+        ],
+        in_specs=[vmem] * 3,
+        out_specs=[vmem] * 2,
+        interpret=interpret,
+    )(keys, values, page_owner.reshape(1, PAGES))
 
 
 def layout(me):
     mx, mz = me // NZ, me % NZ
-    place = jnp.arange(N, dtype=jnp.int32)
     dx = jnp.array([0] * 16 + [-1] * 16 + [1] * 16 + [2] * 16, jnp.int32)
-    residue = (mz + jnp.array(RESIDUES * NX, jnp.int32) + NZ) % STEP
-    piece_b = ((mx + dx + NX) % NX) * NZ + residue + STEP * (place % 4)
-    piece_a = (place % NX) * NZ + place // NX
+    dz = jnp.array(Z_ALL * NX, jnp.int32)
+    piece_b = ((mx + dx + NX) % NX) * NZ + (mz + dz + NZ) % NZ
+    dx = jnp.array(X_ORDER * NZ, jnp.int32)
+    piece_a = ((mx + dx + NX) % NX) * NZ + jnp.arange(N, dtype=jnp.int32) // NX
     return piece_a, piece_b
 
 
@@ -410,8 +422,8 @@
     pages = jnp.stack([low, jnp.where(high > low, high, PAGES)], axis=1)
     hit = piece_a[None, :] == place[:, None]
     pages = jnp.sum(jnp.where(hit[:, :, None], pages[None, :, :], 0), axis=1)
-    at_a = inverse(piece_a)[:, None] * (TALL_A // PAGE) + pages
-    at_b = N * (TALL_A // PAGE) + inverse(piece_b)[:, None] * (TALL_B // PAGE) + pages - PAGES_A
+    at_a = N * (TALL_B // PAGE) + inverse(piece_a)[:, None] * (TALL_A // PAGE) + pages
+    at_b = inverse(piece_b)[:, None] * (TALL_B // PAGE) + pages - PAGES_A
     in_a = pages < PAGES_A
     key_place = jnp.where(in_a, at_a, at_b)
     value_place = key_place + jnp.where(in_a, PAGES_A, PAGES_B)
@@ -434,15 +446,16 @@
     piece_a, piece_b = layout(me)
     count_a, count_b = live_counts(me, lengths, piece_a, piece_b)
     key_place, value_place = page_places(me, gathered, piece_a, piece_b, lengths)
+    state = early_attention(
+        gathered, own, beside, count_a, count_b, live, (queries, keys, values)
+    )
     outgoing = select_pages(
-        key_place, value_place, [gathered] + own + beside, across, piece_b[48:]
+        (key_place, value_place), own + beside, across + [gathered], state[1]
     )
     decode_cache = lax.all_to_all(
         outgoing.reshape(2 * N, PAGE, 1, 2 * HD), "tp", split_axis=0, concat_axis=2, tiled=True
     )
-    attended = run_attention(
-        gathered, own, beside, across, count_a, count_b, live, (queries, keys, values)
-    )
+    attended = late_attention(across, count_b, live, state)
     return (attended, decode_cache.reshape((1,) + decode_cache.shape))
 
 

time: 202 us -> 184 us (0.911)
  the two profiles are of different devices: /device:TPU:487 before, /device:TPU:367 now
where the time goes in v4:
time: 184 us; the launch traced here: 183 us
  Pallas kernels  73 us (40%)
  starting transfers between devices  58.8 us (32%)
  waiting for transfers between devices  23.7 us (13%)
  between operations  14.5 us (8%)
  other arithmetic  7.45 us (4%)
  local copies, waits for them, and re-layouts  5.48 us (3%)
    pallas_call x4, Pallas kernels, attention(): pl.pallas_call(kernel, out_shape=out_shape, in_specs=[smem, smem] + [pl.B...  62.2 us
    ppermute x15, starting transfers between devices, shift(): return lax.ppermute(value, 'ctx', pairs)  51.2 us
    ppermute x15, waiting for transfers between devices, shift(): return lax.ppermute(value, 'ctx', pairs)  23.7 us
    pallas_call x2, Pallas kernels, select_call(): pl.pallas_call(kernel, out_shape=jax.ShapeDtypeStruct((2 * N, PAGE, 2 * H...  9.28 us
    all_to_all x1, starting transfers between devices, body(): lax.all_to_all(outgoing.reshape(2 * N, PAGE, 1, 2 * HD), 'tp', split_axis...  7.62 us
  transfers between devices with their start and end apart: 17, of which 4 were waited for; matrix products, arithmetic and copies ran while one was open for 5% of the time, Pallas kernels for 36%

profile of v4, /device:TPU:367, one launch (start us, length us, event | category | flops | bytes accessed | tf_op | source)
XLA Modules:
  0.0 183.0 jit_solution(11372220397150117054)
XLA Ops:
  7.2 1.5 shard_map.95
  8.7 2.1 %collective-permute-start.12 = (bf16[144,128]{1,0:T(8,128)(2,1)}, bf16[144,128]{1,0:T(8,128)(2,1)S(1)}, u32[]{:S(2)}, u32[]{:S(2)}) collective-permute-start(bf16[144,128]{1,0:T(8,128)(2,1)} %get-tuple-element.14), channel_id=1, source_target_pairs={{0,128},{8,136},{16,144},{24,152},{32,160},{40,168},{48,176},{56,1... | collective-permute-start | bytes 110600 | tf_op jit(solution)/shard_map/ppermute | solution.py:45
  10.8 3.2 %collective-permute-start.13 = (bf16[144,128]{1,0:T(8,128)(2,1)}, bf16[144,128]{1,0:T(8,128)(2,1)S(1)}, u32[]{:S(2)}, u32[]{:S(2)}) collective-permute-start(bf16[144,128]{1,0:T(8,128)(2,1)} %get-tuple-element.14), channel_id=1, source_target_pairs={{0,384},{8,392},{16,400},{24,408},{32,416},{40,424},{48,432},{56,4... | collective-permute-start | bytes 110600 | tf_op jit(solution)/shard_map/ppermute | solution.py:45
  14.0 3.0 %collective-permute-start.14 = (bf16[144,128]{1,0:T(8,128)(2,1)}, bf16[144,128]{1,0:T(8,128)(2,1)S(1)}, u32[]{:S(2)}, u32[]{:S(2)}) collective-permute-start(bf16[144,128]{1,0:T(8,128)(2,1)} %get-tuple-element.14), channel_id=1, source_target_pairs={{0,256},{8,264},{16,272},{24,280},{32,288},{40,296},{48,304},{56,3... | collective-permute-start | bytes 110600 | tf_op jit(solution)/shard_map/ppermute | solution.py:45
  17.1 3.4 %collective-permute-done.14 = bf16[144,128]{1,0:T(8,128)(2,1)S(1)} collective-permute-done((bf16[144,128]{1,0:T(8,128)(2,1)}, bf16[144,128]{1,0:T(8,128)(2,1)S(1)}, u32[]{:S(2)}, u32[]{:S(2)}) %collective-permute-start.14) | collective-permute-done | bytes 36896 | tf_op jit(solution)/shard_map/ppermute | solution.py:45
  20.4 1.4 pad_maximum_fusion.1
  21.9 4.0 %collective-permute-start.1 = (bf16[256,128]{1,0:T(8,128)(2,1)}, bf16[256,128]{1,0:T(8,128)(2,1)S(1)}, u32[]{:S(2)}, u32[]{:S(2)}) collective-permute-start(bf16[256,128]{1,0:T(8,128)(2,1)} %get-tuple-element.13), channel_id=1, source_target_pairs={{0,32},{8,40},{16,48},{24,56},{32,64},{40,72},{48,80},{56,88},{64,... | collective-permute-start | bytes 196616 | tf_op jit(solution)/shard_map/ppermute | solution.py:45
  25.9 5.2 %collective-permute-start = (bf16[256,128]{1,0:T(8,128)(2,1)}, bf16[256,128]{1,0:T(8,128)(2,1)S(1)}, u32[]{:S(2)}, u32[]{:S(2)}) collective-permute-start(bf16[256,128]{1,0:T(8,128)(2,1)} %get-tuple-element.13), channel_id=1, source_target_pairs={{0,96},{8,104},{16,112},{24,120},{32,0},{40,8},{48,16},{56,24},{64... | collective-permute-start | bytes 196616 | tf_op jit(solution)/shard_map/ppermute | solution.py:45
  32.5 0.9 select_reduce_fusion.2
  34.6 4.0 %collective-permute-start.2 = (bf16[128,128]{1,0:T(8,128)(2,1)S(1)}, bf16[128,128]{1,0:T(8,128)(2,1)S(1)}, u32[]{:S(2)}, u32[]{:S(2)}) collective-permute-start(bf16[128,128]{1,0:T(8,128)(2,1)S(1)} %slice.36), channel_id=1, source_target_pairs={{0,32},{8,40},{16,48},{24,56},{32,64},{40,72},{48,80},{56,88},{64,... | collective-permute-start | bytes 98312 | tf_op jit(solution)/shard_map/ppermute | solution.py:45
  38.6 5.2 %collective-permute-start.3 = (bf16[128,128]{1,0:T(8,128)(2,1)S(1)}, bf16[128,128]{1,0:T(8,128)(2,1)S(1)}, u32[]{:S(2)}, u32[]{:S(2)}) collective-permute-start(bf16[128,128]{1,0:T(8,128)(2,1)S(1)} %slice.37), channel_id=1, source_target_pairs={{0,96},{8,104},{16,112},{24,120},{32,0},{40,8},{48,16},{56,24},{64... | collective-permute-start | bytes 98312 | tf_op jit(solution)/shard_map/ppermute | solution.py:45
  44.7 0.9 pad_maximum_fusion.3
  45.6 3.1 %collective-permute-start.6 = (bf16[2,256,128]{2,1,0:T(8,128)(2,1)S(1)}, bf16[2,256,128]{2,1,0:T(8,128)(2,1)S(1)}, u32[]{:S(2)}, u32[]{:S(2)}) collective-permute-start(bf16[2,256,128]{2,1,0:T(8,128)(2,1)S(1)} %get-tuple-element.31), channel_id=1, source_target_pairs={{0,16},{8,24},{16,32},{24,40},{32,48},{40,56},{48,64},{56,72},{64,... | collective-permute-start | bytes 393224 | tf_op jit(solution)/shard_map/ppermute | solution.py:45
  48.7 3.1 %collective-permute-start.7 = (bf16[2,256,128]{2,1,0:T(8,128)(2,1)S(1)}, bf16[2,256,128]{2,1,0:T(8,128)(2,1)S(1)}, u32[]{:S(2)}, u32[]{:S(2)}) collective-permute-start(bf16[2,256,128]{2,1,0:T(8,128)(2,1)S(1)} %get-tuple-element.30), channel_id=1, source_target_pairs={{0,112},{8,120},{16,0},{24,8},{32,16},{40,24},{48,32},{56,40},{64,... | collective-permute-start | bytes 393224 | tf_op jit(solution)/shard_map/ppermute | solution.py:45
  51.8 0.9 pad_maximum_fusion
  52.7 3.9 %collective-permute-start.4 = (bf16[4,256,128]{2,1,0:T(8,128)(2,1)S(1)}, bf16[4,256,128]{2,1,0:T(8,128)(2,1)S(1)}, u32[]{:S(2)}, u32[]{:S(2)}) collective-permute-start(bf16[4,256,128]{2,1,0:T(8,128)(2,1)S(1)} %pad_maximum_fusion), channel_id=1, source_target_pairs={{0,8},{8,16},{16,24},{24,32},{32,40},{40,48},{48,56},{56,64},{64,7... | collective-permute-start | bytes 786440 | tf_op jit(solution)/shard_map/ppermute | solution.py:45
  56.6 1.9 %collective-permute-start.5 = (bf16[4,256,128]{2,1,0:T(8,128)(2,1)S(1)}, bf16[4,256,128]{2,1,0:T(8,128)(2,1)S(1)}, u32[]{:S(2)}, u32[]{:S(2)}) collective-permute-start(bf16[4,256,128]{2,1,0:T(8,128)(2,1)S(1)} %pad_maximum_fusion), channel_id=1, source_target_pairs={{0,120},{8,0},{16,8},{24,16},{32,24},{40,32},{48,40},{56,48},{64,5... | collective-permute-start | bytes 786440 | tf_op jit(solution)/shard_map/ppermute | solution.py:45
  58.6 9.6 %collective-permute-done.4 = bf16[4,256,128]{2,1,0:T(8,128)(2,1)S(1)} collective-permute-done((bf16[4,256,128]{2,1,0:T(8,128)(2,1)S(1)}, bf16[4,256,128]{2,1,0:T(8,128)(2,1)S(1)}, u32[]{:S(2)}, u32[]{:S(2)}) %collective-permute-start.4) | collective-permute-done | bytes 262176 | tf_op jit(solution)/shard_map/ppermute | solution.py:45
  68.2 3.1 %collective-permute-done.5 = bf16[4,256,128]{2,1,0:T(8,128)(2,1)S(1)} collective-permute-done((bf16[4,256,128]{2,1,0:T(8,128)(2,1)S(1)}, bf16[4,256,128]{2,1,0:T(8,128)(2,1)S(1)}, u32[]{:S(2)}, u32[]{:S(2)}) %collective-permute-start.5) | collective-permute-done | bytes 262176 | tf_op jit(solution)/shard_map/ppermute | solution.py:45
  71.4 3.6 %collective-permute-start.8 = (bf16[16,256,128]{2,1,0:T(8,128)(2,1)S(1)}, bf16[16,256,128]{2,1,0:T(8,128)(2,1)S(1)}, u32[]{:S(2)}, u32[]{:S(2)}) collective-permute-start(bf16[16,256,128]{2,1,0:T(8,128)(2,1)S(1)} %constant_dynamic-update-slice_fusion.refs_2_), channel_id=1, source_target_pairs={{0,128},{8,136},{16,144},{24,152},{32,160},{40,168},{48,176},{56,1... | collective-permute-start | bytes 3145736 | tf_op jit(solution)/shard_map/ppermute | solution.py:45
  75.1 1.9 %collective-permute-start.10 = (bf16[16,256,128]{2,1,0:T(8,128)(2,1)S(1)}, bf16[16,256,128]{2,1,0:T(8,128)(2,1)S(1)}, u32[]{:S(2)}, u32[]{:S(2)}) collective-permute-start(bf16[16,256,128]{2,1,0:T(8,128)(2,1)S(1)} %constant_dynamic-update-slice_fusion.refs_2_), channel_id=1, source_target_pairs={{0,384},{8,392},{16,400},{24,408},{32,416},{40,424},{48,432},{56,4... | collective-permute-start | bytes 3145736 | tf_op jit(solution)/shard_map/ppermute | solution.py:45
  78.2 8.6 %shard_map.96 = (bf16[1536,256]{1,0:T(8,128)(2,1)}, f32[1536,128]{1,0:T(8,128)}, f32[1536,128]{1,0:T(8,128)}) custom-call(s32[16]{0:T(128)} %get-tuple-element.36.refs_0_, s32[1]{0:T(128)} %bitcast.refs_1_, bf16[16,256,128]{2,1,0:T(8,128)(2,1)} %copy-done.2, bf16[192,1024]{1,0:T(8,128)(2,1)} %refs_3_.1, bf16[192,128]{1,0:T(8,128)(2,1)} %refs_4_.1, ...), custom_call_target="tpu_custom_call" | custom-call | flops 3221225472 | bytes 8388608 | tf_op jit(solution)/shard_map/pallas_call | solution.py:256
  86.8 7.5 %collective-permute-done.8.refs_2_ = bf16[16,256,128]{2,1,0:T(8,128)(2,1)S(1)} collective-permute-done((bf16[16,256,128]{2,1,0:T(8,128)(2,1)S(1)}, bf16[16,256,128]{2,1,0:T(8,128)(2,1)S(1)}, u32[]{:S(2)}, u32[]{:S(2)}) %collective-permute-start.8) | collective-permute-done | bytes 1048608 | tf_op jit(solution)/shard_map/ppermute | solution.py:45
  94.4 5.1 %collective-permute-start.9 = (bf16[8,256,128]{2,1,0:T(8,128)(2,1)S(1)}, bf16[8,256,128]{2,1,0:T(8,128)(2,1)}, u32[]{:S(2)}, u32[]{:S(2)}) collective-permute-start(bf16[8,256,128]{2,1,0:T(8,128)(2,1)S(1)} %slice.38), channel_id=1, source_target_pairs={{0,128},{8,136},{16,144},{24,152},{32,160},{40,168},{48,176},{56,1... | collective-permute-start | bytes 1572872 | tf_op jit(solution)/shard_map/ppermute | solution.py:45
  99.5 1.9 %collective-permute-start.11 = (bf16[8,256,128]{2,1,0:T(8,128)(2,1)S(1)}, bf16[8,256,128]{2,1,0:T(8,128)(2,1)S(1)}, u32[]{:S(2)}, u32[]{:S(2)}) collective-permute-start(bf16[8,256,128]{2,1,0:T(8,128)(2,1)S(1)} %slice.39), channel_id=1, source_target_pairs={{0,384},{8,392},{16,400},{24,408},{32,416},{40,424},{48,432},{56,4... | collective-permute-start | bytes 1572872 | tf_op jit(solution)/shard_map/ppermute | solution.py:45
  101.4 28.8 %shard_map.97 = (bf16[1536,256]{1,0:T(8,128)(2,1)}, f32[1536,128]{1,0:T(8,128)}, f32[1536,128]{1,0:T(8,128)}) custom-call(s32[32]{0:T(128)} %slice.33.refs_0_, s32[1]{0:T(128)} %bitcast.refs_1_, bf16[16,256,128]{2,1,0:T(8,128)(2,1)} %copy-done, bf16[16,256,128]{2,1,0:T(8,128)(2,1)} %copy-done.1, bf16[1536,256]{1,0:T(8,128)(2,1)} %get-tuple-element.15.refs_4_, ...), custom_call_target="tpu_custom_call" | custom-call | flops 6442450944 | bytes 8388608 | tf_op jit(solution)/shard_map/pallas_call | solution.py:256
  130.3 0.9 slice.40
  132.7 4.1 %shard_map.100.refs_2_ = bf16[128,2,256]{2,1,0:T(2,128)(2,1)} custom-call(s32[128]{0:T(128)} %get-tuple-element.33.refs_0_, s32[128]{0:T(128)} %get-tuple-element.32.refs_1_, bf16[2048,2,128]{2,1,0:T(2,128)(2,1)} %bitcast.41, bf16[2048,2,128]{2,1,0:T(2,128)(2,1)} %bitcast.39, bf16[2048,2,128]{2,1,0:T(2,128)(2,1)} %bitcast.40), custom_call_target="tpu_custom_call" | custom-call | bytes 4194304 | tf_op jit(solution)/shard_map/pallas_call | solution.py:336
  136.9 16.3 %shard_map.98 = (bf16[1536,256]{1,0:T(8,128)(2,1)}, f32[1536,128]{1,0:T(8,128)}, f32[1536,128]{1,0:T(8,128)}) custom-call(s32[64]{0:T(128)} %compare_select_fusion.7.refs_0_, s32[1]{0:T(128)} %bitcast.refs_1_, bf16[64,144,128]{2,1,0:T(8,128)(2,1)} %all-gather.3.cloned.1.call-done.refs_2_, bf16[1536,256]{1,0:T(8,128)(2,1)} %get-tuple-element.18.refs_3_, ...), custom_call_target="tpu_custom_call" | custom-call | flops 6442450944 | bytes 8388608 | tf_op jit(solution)/shard_map/pallas_call | solution.py:256
  154.0 5.1 %shard_map.101 = bf16[128,2,256]{2,1,0:T(2,128)(2,1)} custom-call(s32[128]{0:T(128)} %get-tuple-element.33.refs_0_, s32[128]{0:T(128)} %get-tuple-element.32.refs_1_, bf16[128,2,256]{2,1,0:T(2,128)(2,1)} %shard_map.100.refs_2_, f32[1536,128]{1,0:T(8,128)} %get-tuple-element.22.refs_5_.refs_3_, bf16[1024,2,128]{2,1,0:T(2,128)(2,1)} %bitcast.16.refs_4_, ...), custom_call_target="tpu_custom_call" | custom-call | bytes 4194304 | tf_op jit(solution)/shard_map/pallas_call | solution.py:336
  159.2 7.6 %all-to-all-start = ((bf16[128,2,1,256]{3,1,2,0:T(2,128)(2,1)}), bf16[128,2,1,256]{3,1,2,0:T(2,128)(2,1)S(1)}, u32[]{:S(2)}, u32[]{:S(2)}) async-start(bf16[128,2,1,256]{3,1,2,0:T(2,128)(2,1)} %bitcast.49), calls=%async_computation | async-start | bytes 262144 | tf_op jit(solution)/shard_map/all_to_all | solution.py:455
  166.8 8.6 %shard_map.99 = bf16[192,1024]{1,0:T(8,128)(2,1)} custom-call(s32[16]{0:T(128)} %get-tuple-element.37.refs_0_, s32[1]{0:T(128)} %bitcast.refs_1_, bf16[8,256,128]{2,1,0:T(8,128)(2,1)} %collective-permute-done.9.refs_2_, bf16[8,256,128]{2,1,0:T(8,128)(2,1)} %copy-done.3, bf16[1536,256]{1,0:T(8,128)(2,1)} %get-tuple-element.21.refs_4_, ...), custom_call_target="tpu_custom_call" | custom-call | flops 3221225472 | bytes 8388608 | tf_op jit(solution)/shard_map/pallas_call | solution.py:256
  (63 shorter events, 8.0 us)
Async XLA Ops:
  7.2 70.5 %copy-start.5 = (s32[64]{0:T(128)S(1)}, s32[64]{0:T(128)}, u32[]{:S(2)}) copy-start(s32[64]{0:T(128)} %constant.106.clone) | copy-start | bytes 772
  7.2 69.8 %copy-start.4 = (s32[64]{0:T(128)S(1)}, s32[64]{0:T(128)}, u32[]{:S(2)}) copy-start(s32[64]{0:T(128)} %param.11) | copy-start | bytes 772
  7.2 123.1 %all-gather.3.cloned.1.call-start = ((), (), s32[]{:S(2)}) async-start(), calls=%async_computation.1 | async-start | bytes 2506752 | tf_op jit(solution)/shard_map/all_gather | solution.py:49
  8.7 8.3 %collective-permute-start.12 = (bf16[144,128]{1,0:T(8,128)(2,1)}, bf16[144,128]{1,0:T(8,128)(2,1)S(1)}, u32[]{:S(2)}, u32[]{:S(2)}) collective-permute-start(bf16[144,128]{1,0:T(8,128)(2,1)} %get-tuple-element.14), channel_id=1, source_target_pairs={{0,128},{8,136},{16,144},{24,152},{32,160},{40,168},{48,176},{56,1... | collective-permute-start | bytes 110600 | tf_op jit(solution)/shard_map/ppermute | solution.py:45
  10.8 6.2 %collective-permute-start.13 = (bf16[144,128]{1,0:T(8,128)(2,1)}, bf16[144,128]{1,0:T(8,128)(2,1)S(1)}, u32[]{:S(2)}, u32[]{:S(2)}) collective-permute-start(bf16[144,128]{1,0:T(8,128)(2,1)} %get-tuple-element.14), channel_id=1, source_target_pairs={{0,384},{8,392},{16,400},{24,408},{32,416},{40,424},{48,432},{56,4... | collective-permute-start | bytes 110600 | tf_op jit(solution)/shard_map/ppermute | solution.py:45
  14.0 6.4 %collective-permute-start.14 = (bf16[144,128]{1,0:T(8,128)(2,1)}, bf16[144,128]{1,0:T(8,128)(2,1)S(1)}, u32[]{:S(2)}, u32[]{:S(2)}) collective-permute-start(bf16[144,128]{1,0:T(8,128)(2,1)} %get-tuple-element.14), channel_id=1, source_target_pairs={{0,256},{8,264},{16,272},{24,280},{32,288},{40,296},{48,304},{56,3... | collective-permute-start | bytes 110600 | tf_op jit(solution)/shard_map/ppermute | solution.py:45
  21.9 12.7 %collective-permute-start.1 = (bf16[256,128]{1,0:T(8,128)(2,1)}, bf16[256,128]{1,0:T(8,128)(2,1)S(1)}, u32[]{:S(2)}, u32[]{:S(2)}) collective-permute-start(bf16[256,128]{1,0:T(8,128)(2,1)} %get-tuple-element.13), channel_id=1, source_target_pairs={{0,32},{8,40},{16,48},{24,56},{32,64},{40,72},{48,80},{56,88},{64,... | collective-permute-start | bytes 196616 | tf_op jit(solution)/shard_map/ppermute | solution.py:45
  25.9 12.7 %collective-permute-start = (bf16[256,128]{1,0:T(8,128)(2,1)}, bf16[256,128]{1,0:T(8,128)(2,1)S(1)}, u32[]{:S(2)}, u32[]{:S(2)}) collective-permute-start(bf16[256,128]{1,0:T(8,128)(2,1)} %get-tuple-element.13), channel_id=1, source_target_pairs={{0,96},{8,104},{16,112},{24,120},{32,0},{40,8},{48,16},{56,24},{64... | collective-permute-start | bytes 196616 | tf_op jit(solution)/shard_map/ppermute | solution.py:45
  34.6 17.2 %collective-permute-start.2 = (bf16[128,128]{1,0:T(8,128)(2,1)S(1)}, bf16[128,128]{1,0:T(8,128)(2,1)S(1)}, u32[]{:S(2)}, u32[]{:S(2)}) collective-permute-start(bf16[128,128]{1,0:T(8,128)(2,1)S(1)} %slice.36), channel_id=1, source_target_pairs={{0,32},{8,40},{16,48},{24,56},{32,64},{40,72},{48,80},{56,88},{64,... | collective-permute-start | bytes 98312 | tf_op jit(solution)/shard_map/ppermute | solution.py:45
  38.6 13.2 %collective-permute-start.3 = (bf16[128,128]{1,0:T(8,128)(2,1)S(1)}, bf16[128,128]{1,0:T(8,128)(2,1)S(1)}, u32[]{:S(2)}, u32[]{:S(2)}) collective-permute-start(bf16[128,128]{1,0:T(8,128)(2,1)S(1)} %slice.37), channel_id=1, source_target_pairs={{0,96},{8,104},{16,112},{24,120},{32,0},{40,8},{48,16},{56,24},{64... | collective-permute-start | bytes 98312 | tf_op jit(solution)/shard_map/ppermute | solution.py:45
  45.6 25.8 %collective-permute-start.6 = (bf16[2,256,128]{2,1,0:T(8,128)(2,1)S(1)}, bf16[2,256,128]{2,1,0:T(8,128)(2,1)S(1)}, u32[]{:S(2)}, u32[]{:S(2)}) collective-permute-start(bf16[2,256,128]{2,1,0:T(8,128)(2,1)S(1)} %get-tuple-element.31), channel_id=1, source_target_pairs={{0,16},{8,24},{16,32},{24,40},{32,48},{40,56},{48,64},{56,72},{64,... | collective-permute-start | bytes 393224 | tf_op jit(solution)/shard_map/ppermute | solution.py:45
  48.7 22.7 %collective-permute-start.7 = (bf16[2,256,128]{2,1,0:T(8,128)(2,1)S(1)}, bf16[2,256,128]{2,1,0:T(8,128)(2,1)S(1)}, u32[]{:S(2)}, u32[]{:S(2)}) collective-permute-start(bf16[2,256,128]{2,1,0:T(8,128)(2,1)S(1)} %get-tuple-element.30), channel_id=1, source_target_pairs={{0,112},{8,120},{16,0},{24,8},{32,16},{40,24},{48,32},{56,40},{64,... | collective-permute-start | bytes 393224 | tf_op jit(solution)/shard_map/ppermute | solution.py:45
  52.7 15.5 %collective-permute-start.4 = (bf16[4,256,128]{2,1,0:T(8,128)(2,1)S(1)}, bf16[4,256,128]{2,1,0:T(8,128)(2,1)S(1)}, u32[]{:S(2)}, u32[]{:S(2)}) collective-permute-start(bf16[4,256,128]{2,1,0:T(8,128)(2,1)S(1)} %pad_maximum_fusion), channel_id=1, source_target_pairs={{0,8},{8,16},{16,24},{24,32},{32,40},{40,48},{48,56},{56,64},{64,7... | collective-permute-start | bytes 786440 | tf_op jit(solution)/shard_map/ppermute | solution.py:45
  56.6 14.7 %collective-permute-start.5 = (bf16[4,256,128]{2,1,0:T(8,128)(2,1)S(1)}, bf16[4,256,128]{2,1,0:T(8,128)(2,1)S(1)}, u32[]{:S(2)}, u32[]{:S(2)}) collective-permute-start(bf16[4,256,128]{2,1,0:T(8,128)(2,1)S(1)} %pad_maximum_fusion), channel_id=1, source_target_pairs={{0,120},{8,0},{16,8},{24,16},{32,24},{40,32},{48,40},{56,48},{64,5... | collective-permute-start | bytes 786440 | tf_op jit(solution)/shard_map/ppermute | solution.py:45
  71.4 6.7 %copy-start.2 = (bf16[16,256,128]{2,1,0:T(8,128)(2,1)}, bf16[16,256,128]{2,1,0:T(8,128)(2,1)S(1)}, u32[]{:S(2)}) copy-start(bf16[16,256,128]{2,1,0:T(8,128)(2,1)S(1)} %constant_dynamic-update-slice_fusion.refs_2_) | copy-start | bytes 3145732
  71.4 22.9 %collective-permute-start.8 = (bf16[16,256,128]{2,1,0:T(8,128)(2,1)S(1)}, bf16[16,256,128]{2,1,0:T(8,128)(2,1)S(1)}, u32[]{:S(2)}, u32[]{:S(2)}) collective-permute-start(bf16[16,256,128]{2,1,0:T(8,128)(2,1)S(1)} %constant_dynamic-update-slice_fusion.refs_2_), channel_id=1, source_target_pairs={{0,128},{8,136},{16,144},{24,152},{32,160},{40,168},{48,176},{56,1... | collective-permute-start | bytes 3145736 | tf_op jit(solution)/shard_map/ppermute | solution.py:45
  75.1 24.3 %collective-permute-start.10 = (bf16[16,256,128]{2,1,0:T(8,128)(2,1)S(1)}, bf16[16,256,128]{2,1,0:T(8,128)(2,1)S(1)}, u32[]{:S(2)}, u32[]{:S(2)}) collective-permute-start(bf16[16,256,128]{2,1,0:T(8,128)(2,1)S(1)} %constant_dynamic-update-slice_fusion.refs_2_), channel_id=1, source_target_pairs={{0,384},{8,392},{16,400},{24,408},{32,416},{40,424},{48,432},{56,4... | collective-permute-start | bytes 3145736 | tf_op jit(solution)/shard_map/ppermute | solution.py:45
  94.3 7.1 %copy-start = (bf16[16,256,128]{2,1,0:T(8,128)(2,1)}, bf16[16,256,128]{2,1,0:T(8,128)(2,1)S(1)}, u32[]{:S(2)}) copy-start(bf16[16,256,128]{2,1,0:T(8,128)(2,1)S(1)} %collective-permute-done.8.refs_2_) | copy-start | bytes 3145732
  94.4 58.9 %collective-permute-start.9 = (bf16[8,256,128]{2,1,0:T(8,128)(2,1)S(1)}, bf16[8,256,128]{2,1,0:T(8,128)(2,1)}, u32[]{:S(2)}, u32[]{:S(2)}) collective-permute-start(bf16[8,256,128]{2,1,0:T(8,128)(2,1)S(1)} %slice.38), channel_id=1, source_target_pairs={{0,128},{8,136},{16,144},{24,152},{32,160},{40,168},{48,176},{56,1... | collective-permute-start | bytes 1572872 | tf_op jit(solution)/shard_map/ppermute | solution.py:45
  99.4 2.0 %copy-start.1 = (bf16[16,256,128]{2,1,0:T(8,128)(2,1)}, bf16[16,256,128]{2,1,0:T(8,128)(2,1)S(1)}, u32[]{:S(2)}) copy-start(bf16[16,256,128]{2,1,0:T(8,128)(2,1)S(1)} %collective-permute-done.10.refs_3_) | copy-start | bytes 3145732
  99.5 53.7 %collective-permute-start.11 = (bf16[8,256,128]{2,1,0:T(8,128)(2,1)S(1)}, bf16[8,256,128]{2,1,0:T(8,128)(2,1)S(1)}, u32[]{:S(2)}, u32[]{:S(2)}) collective-permute-start(bf16[8,256,128]{2,1,0:T(8,128)(2,1)S(1)} %slice.39), channel_id=1, source_target_pairs={{0,384},{8,392},{16,400},{24,408},{32,416},{40,424},{48,432},{56,4... | collective-permute-start | bytes 1572872 | tf_op jit(solution)/shard_map/ppermute | solution.py:45
  153.2 0.8 copy-start.3
  159.2 16.2 %all-to-all-start = ((bf16[128,2,1,256]{3,1,2,0:T(2,128)(2,1)}), bf16[128,2,1,256]{3,1,2,0:T(2,128)(2,1)S(1)}, u32[]{:S(2)}, u32[]{:S(2)}) async-start(bf16[128,2,1,256]{3,1,2,0:T(2,128)(2,1)} %bitcast.49), calls=%async_computation | async-start | bytes 262144 | tf_op jit(solution)/shard_map/all_to_all | solution.py:455
Sparse Core Ops, SparseCore 0:
  22.0 69.8 all-gather.2

commit v5 on v4

--- a/solution.py
+++ b/solution.py
@@ -13,7 +13,7 @@
 NZ = 16
 N = NX * NZ
 CAP = 192
-ROWS_A = 64
+ROWS_A = 96
 ROWS_B = CAP - ROWS_A
 PAGES = CAP // PAGE
 PAGES_A = ROWS_A // PAGE
@@ -23,7 +23,7 @@
 TALL_B = 2 * ROWS_B
 GROUP = 8
 ROWS = GROUP * CAP
-TILES = 4
+TILES = 2
 TILE = ROWS // TILES
 WIDTH = 512
 DEAD = -1e30
@@ -267,17 +267,18 @@
     )(count, live, *sources, *state)
 
 
-def early_attention(gathered, own, beside, count_a, count_b, live, arrays, interpret=False):
+def early_attention(own, beside, count_b, live, arrays, interpret=False):
     state = attention(True, False, count_b[:16], live, own, arrays, interpret)
-    state = attention(False, False, count_b[16:48], live, beside, state, interpret)
-    return attention(False, False, count_a, live, [gathered], state, interpret)
-
-
-def late_attention(across, count_b, live, state, interpret=False):
-    return attention(False, True, count_b[48:], live, across, state, interpret)
-
-
-def fetch(sources, pages, sems):
+    return attention(False, False, count_b[16:48], live, beside, state, interpret)
+
+
+def late_attention(gathered, across, count_a, count_b, live, state, interpret=False):
+    count = jnp.concatenate([count_b[48:], count_a])
+    return attention(False, True, count, live, across + [gathered], state, interpret)
+
+
+def select_kernel(n_src, key_ref, value_ref, after_ref, *refs):
+    sources, (out_ref, pages, sems) = refs[:n_src], refs[n_src:]
     copies = []
     start = 0
     for i, source in enumerate(sources):
@@ -290,82 +291,39 @@
         copy.start()
     for copy in copies:
         copy.wait()
-    return start
-
-
-def select_kernel(n_src, key_ref, value_ref, *refs):
-    sources, (out_ref, pages, sems) = refs[:n_src], refs[n_src:]
-    total = fetch(sources, pages, sems)
 
     def one(s, carry):
         place = key_ref[s]
-        found = (place >= 0) & (place < total)
-        keep = jnp.where(found, 1.0, 0.0).astype(jnp.bfloat16)
-        key = jnp.where(found, place, 0)
-        value = jnp.where(found, value_ref[s], 0)
-        out_ref[s, :, 0:HD] = pages[key] * keep
-        out_ref[s, :, HD : 2 * HD] = pages[value] * keep
+        keep = jnp.where(place >= 0, 1.0, 0.0).astype(jnp.bfloat16)
+        out_ref[s, :, 0:HD] = pages[jnp.maximum(place, 0)] * keep
+        out_ref[s, :, HD : 2 * HD] = pages[jnp.maximum(value_ref[s], 0)] * keep
         return carry
 
     lax.fori_loop(0, 2 * N, one, 0, unroll=4)
 
 
-def select_rest_kernel(n_src, base, key_ref, value_ref, old_ref, after_ref, *refs):
-    sources, (out_ref, pages, sems) = refs[:n_src], refs[n_src:]
-    fetch(sources, pages, sems)
-    out_ref[...] = old_ref[...]
-
-    def one(s, carry):
-        place = key_ref[s] - base
-
-        @pl.when(place >= 0)
-        def _():
-            out_ref[s, :, 0:HD] = pages[place]
-            out_ref[s, :, HD : 2 * HD] = pages[value_ref[s] - base]
-
-        return carry
-
-    lax.fori_loop(0, 2 * N, one, 0, unroll=2)
-
-
-def select_call(kernel, scalars, arrays, sources, interpret):
+def select_pages(places, sources, after, interpret=False):
+    sources = [s.reshape(s.shape[0] * s.shape[1] // PAGE, PAGE, HD) for s in sources]
     total = sum(s.shape[0] for s in sources)
     smem = pl.BlockSpec(memory_space=pltpu.SMEM)
-    vmem = pl.BlockSpec(memory_space=pltpu.VMEM)
     anywhere = pl.BlockSpec(memory_space=pl.ANY)
+
+    def kernel(*refs):
+        select_kernel(len(sources), *refs)
+
     return pl.pallas_call(
         kernel,
         out_shape=jax.ShapeDtypeStruct((2 * N, PAGE, 2 * HD), jnp.bfloat16),
-        in_specs=[smem] * len(scalars)
-        + [vmem, anywhere][: len(arrays)]
-        + [anywhere] * len(sources),
-        out_specs=vmem,
+        in_specs=[smem] * 2 + [anywhere] * (1 + len(sources)),
+        out_specs=pl.BlockSpec(memory_space=pltpu.VMEM),
         scratch_shapes=[
             pltpu.VMEM((total, PAGE, HD), jnp.bfloat16),
             pltpu.SemaphoreType.DMA((len(sources),)),
         ],
         compiler_params=pltpu.CompilerParams(vmem_limit_bytes=VMEM_LIMIT),
-        cost_estimate=pl.CostEstimate(flops=0, bytes_accessed=4 << 20, transcendentals=0),
+        cost_estimate=pl.CostEstimate(flops=0, bytes_accessed=8 << 20, transcendentals=0),
         interpret=interpret,
-    )(*scalars, *arrays, *sources)
-
-
-def as_pages(sources):
-    return [s.reshape(s.shape[0] * s.shape[1] // PAGE, PAGE, HD) for s in sources]
-
-
-def select_pages(places, near, rest, after, interpret=False):
-    near, rest = as_pages(near), as_pages(rest)
-    base = sum(s.shape[0] for s in near)
-
-    def kernel(*refs):
-        select_kernel(len(near), *refs)
-
-    def rest_kernel(*refs):
-        select_rest_kernel(len(rest), base, *refs)
-
-    out = select_call(kernel, places, (), near, interpret)
-    return select_call(rest_kernel, places, (out, after), rest, interpret)
+    )(*places, after, *sources)
 
 
 def payload_kernel(k_ref, v_ref, owner_ref, a_ref, b_ref):
@@ -446,16 +404,14 @@
     piece_a, piece_b = layout(me)
     count_a, count_b = live_counts(me, lengths, piece_a, piece_b)
     key_place, value_place = page_places(me, gathered, piece_a, piece_b, lengths)
-    state = early_attention(
-        gathered, own, beside, count_a, count_b, live, (queries, keys, values)
-    )
+    state = early_attention(own, beside, count_b, live, (queries, keys, values))
     outgoing = select_pages(
-        (key_place, value_place), own + beside, across + [gathered], state[1]
+        (key_place, value_place), own + beside + across + [gathered], state[1]
     )
     decode_cache = lax.all_to_all(
         outgoing.reshape(2 * N, PAGE, 1, 2 * HD), "tp", split_axis=0, concat_axis=2, tiled=True
     )
-    attended = late_attention(across, count_b, live, state)
+    attended = late_attention(gathered, across, count_a, count_b, live, state)
     return (attended, decode_cache.reshape((1,) + decode_cache.shape))
 
 

time: 184 us -> 177 us (0.962)
  the two profiles are of different devices: /device:TPU:367 before, /device:TPU:39 now
where the time goes in v5:
time: 177 us; the launch traced here: 175 us
  starting transfers between devices  67.3 us (38%)
  Pallas kernels  62.5 us (35%)
  waiting for transfers between devices  18.4 us (10%)
  between operations  14.5 us (8%)
  other arithmetic  7.59 us (4%)
  local copies, waits for them, and re-layouts  5.17 us (3%)
    ppermute x15, starting transfers between devices, shift(): return lax.ppermute(value, 'ctx', pairs)  57.2 us
    pallas_call x3, Pallas kernels, attention(): pl.pallas_call(kernel, out_shape=out_shape, in_specs=[smem, smem] + [pl.B...  55.8 us
    ppermute x15, waiting for transfers between devices, shift(): return lax.ppermute(value, 'ctx', pairs)  18.4 us
    all_to_all x1, starting transfers between devices, body(): lax.all_to_all(outgoing.reshape(2 * N, PAGE, 1, 2 * HD), 'tp', split_axis...  10 us
    pallas_call x1, Pallas kernels, select_pages(): pl.pallas_call(kernel, out_shape=jax.ShapeDtypeStruct((2 * N, PAGE, 2 * H...  5.25 us
  transfers between devices with their start and end apart: 17, of which 5 were waited for; matrix products, arithmetic and copies ran while one was open for 5% of the time, Pallas kernels for 32%

profile of v5, /device:TPU:39, one launch (start us, length us, event | category | flops | bytes accessed | tf_op | source)
XLA Modules:
  0.0 175.5 jit_solution(4409687124799913412)
XLA Ops:
  7.2 1.5 shard_map.95
  8.7 2.1 %collective-permute-start.12 = (bf16[208,128]{1,0:T(8,128)(2,1)}, bf16[208,128]{1,0:T(8,128)(2,1)S(1)}, u32[]{:S(2)}, u32[]{:S(2)}) collective-permute-start(bf16[208,128]{1,0:T(8,128)(2,1)} %get-tuple-element.11), channel_id=1, source_target_pairs={{0,128},{8,136},{16,144},{24,152},{32,160},{40,168},{48,176},{56,1... | collective-permute-start | bytes 159752 | tf_op jit(solution)/shard_map/ppermute | solution.py:45
  10.8 3.2 %collective-permute-start.13 = (bf16[208,128]{1,0:T(8,128)(2,1)}, bf16[208,128]{1,0:T(8,128)(2,1)S(1)}, u32[]{:S(2)}, u32[]{:S(2)}) collective-permute-start(bf16[208,128]{1,0:T(8,128)(2,1)} %get-tuple-element.11), channel_id=1, source_target_pairs={{0,384},{8,392},{16,400},{24,408},{32,416},{40,424},{48,432},{56,4... | collective-permute-start | bytes 159752 | tf_op jit(solution)/shard_map/ppermute | solution.py:45
  14.0 3.0 %collective-permute-start.14 = (bf16[208,128]{1,0:T(8,128)(2,1)}, bf16[208,128]{1,0:T(8,128)(2,1)S(1)}, u32[]{:S(2)}, u32[]{:S(2)}) collective-permute-start(bf16[208,128]{1,0:T(8,128)(2,1)} %get-tuple-element.11), channel_id=1, source_target_pairs={{0,256},{8,264},{16,272},{24,280},{32,288},{40,296},{48,304},{56,3... | collective-permute-start | bytes 159752 | tf_op jit(solution)/shard_map/ppermute | solution.py:45
  17.1 3.5 %collective-permute-done.14 = bf16[208,128]{1,0:T(8,128)(2,1)S(1)} collective-permute-done((bf16[208,128]{1,0:T(8,128)(2,1)}, bf16[208,128]{1,0:T(8,128)(2,1)S(1)}, u32[]{:S(2)}, u32[]{:S(2)}) %collective-permute-start.14) | collective-permute-done | bytes 53280 | tf_op jit(solution)/shard_map/ppermute | solution.py:45
  20.6 1.5 pad_maximum_fusion
  22.1 8.8 %collective-permute-start.1 = (bf16[192,128]{1,0:T(8,128)(2,1)}, bf16[192,128]{1,0:T(8,128)(2,1)S(1)}, u32[]{:S(2)}, u32[]{:S(2)}) collective-permute-start(bf16[192,128]{1,0:T(8,128)(2,1)} %get-tuple-element.10), channel_id=1, source_target_pairs={{0,32},{8,40},{16,48},{24,56},{32,64},{40,72},{48,80},{56,88},{64,... | collective-permute-start | bytes 147464 | tf_op jit(solution)/shard_map/ppermute | solution.py:45
  30.9 4.7 %collective-permute-start = (bf16[192,128]{1,0:T(8,128)(2,1)}, bf16[192,128]{1,0:T(8,128)(2,1)S(1)}, u32[]{:S(2)}, u32[]{:S(2)}) collective-permute-start(bf16[192,128]{1,0:T(8,128)(2,1)} %get-tuple-element.10), channel_id=1, source_target_pairs={{0,96},{8,104},{16,112},{24,120},{32,0},{40,8},{48,16},{56,24},{64... | collective-permute-start | bytes 147464 | tf_op jit(solution)/shard_map/ppermute | solution.py:45
  36.3 0.9 select_reduce_fusion.2
  37.8 1.3 fusion.4
  39.6 5.2 %collective-permute-start.2 = (bf16[96,128]{1,0:T(8,128)(2,1)S(1)}, bf16[96,128]{1,0:T(8,128)(2,1)S(1)}, u32[]{:S(2)}, u32[]{:S(2)}) collective-permute-start(bf16[96,128]{1,0:T(8,128)(2,1)S(1)} %slice.36), channel_id=1, source_target_pairs={{0,32},{8,40},{16,48},{24,56},{32,64},{40,72},{48,80},{56,88},{64,... | collective-permute-start | bytes 73736 | tf_op jit(solution)/shard_map/ppermute | solution.py:45
  44.8 4.0 %collective-permute-start.3 = (bf16[96,128]{1,0:T(8,128)(2,1)S(1)}, bf16[96,128]{1,0:T(8,128)(2,1)S(1)}, u32[]{:S(2)}, u32[]{:S(2)}) collective-permute-start(bf16[96,128]{1,0:T(8,128)(2,1)S(1)} %slice.37), channel_id=1, source_target_pairs={{0,96},{8,104},{16,112},{24,120},{32,0},{40,8},{48,16},{56,24},{64... | collective-permute-start | bytes 73736 | tf_op jit(solution)/shard_map/ppermute | solution.py:45
  48.8 0.8 constant_dynamic-update-slice_fusion.6
  49.6 0.9 pad_maximum_fusion.3
  50.5 3.1 %collective-permute-start.6 = (bf16[2,192,128]{2,1,0:T(8,128)(2,1)S(1)}, bf16[2,192,128]{2,1,0:T(8,128)(2,1)S(1)}, u32[]{:S(2)}, u32[]{:S(2)}) collective-permute-start(bf16[2,192,128]{2,1,0:T(8,128)(2,1)S(1)} %get-tuple-element.25), channel_id=1, source_target_pairs={{0,16},{8,24},{16,32},{24,40},{32,48},{40,56},{48,64},{56,72},{64,... | collective-permute-start | bytes 294920 | tf_op jit(solution)/shard_map/ppermute | solution.py:45
  53.6 5.2 %collective-permute-start.7 = (bf16[2,192,128]{2,1,0:T(8,128)(2,1)S(1)}, bf16[2,192,128]{2,1,0:T(8,128)(2,1)S(1)}, u32[]{:S(2)}, u32[]{:S(2)}) collective-permute-start(bf16[2,192,128]{2,1,0:T(8,128)(2,1)S(1)} %get-tuple-element.24), channel_id=1, source_target_pairs={{0,112},{8,120},{16,0},{24,8},{32,16},{40,24},{48,32},{56,40},{64,... | collective-permute-start | bytes 294920 | tf_op jit(solution)/shard_map/ppermute | solution.py:45
  58.9 0.8 pad_maximum_fusion.1
  59.7 1.9 %collective-permute-start.4 = (bf16[4,192,128]{2,1,0:T(8,128)(2,1)S(1)}, bf16[4,192,128]{2,1,0:T(8,128)(2,1)S(1)}, u32[]{:S(2)}, u32[]{:S(2)}) collective-permute-start(bf16[4,192,128]{2,1,0:T(8,128)(2,1)S(1)} %pad_maximum_fusion.1), channel_id=1, source_target_pairs={{0,8},{8,16},{16,24},{24,32},{32,40},{40,48},{48,56},{56,64},{64,7... | collective-permute-start | bytes 589832 | tf_op jit(solution)/shard_map/ppermute | solution.py:45
  61.7 3.4 %collective-permute-start.5 = (bf16[4,192,128]{2,1,0:T(8,128)(2,1)S(1)}, bf16[4,192,128]{2,1,0:T(8,128)(2,1)S(1)}, u32[]{:S(2)}, u32[]{:S(2)}) collective-permute-start(bf16[4,192,128]{2,1,0:T(8,128)(2,1)S(1)} %pad_maximum_fusion.1), channel_id=1, source_target_pairs={{0,120},{8,0},{16,8},{24,16},{32,24},{40,32},{48,40},{56,48},{64,5... | collective-permute-start | bytes 589832 | tf_op jit(solution)/shard_map/ppermute | solution.py:45
  65.0 5.0 %collective-permute-done.4 = bf16[4,192,128]{2,1,0:T(8,128)(2,1)S(1)} collective-permute-done((bf16[4,192,128]{2,1,0:T(8,128)(2,1)S(1)}, bf16[4,192,128]{2,1,0:T(8,128)(2,1)S(1)}, u32[]{:S(2)}, u32[]{:S(2)}) %collective-permute-start.4) | collective-permute-done | bytes 196640 | tf_op jit(solution)/shard_map/ppermute | solution.py:45
  70.0 2.3 %collective-permute-done.5 = bf16[4,192,128]{2,1,0:T(8,128)(2,1)S(1)} collective-permute-done((bf16[4,192,128]{2,1,0:T(8,128)(2,1)S(1)}, bf16[4,192,128]{2,1,0:T(8,128)(2,1)S(1)}, u32[]{:S(2)}, u32[]{:S(2)}) %collective-permute-start.5) | collective-permute-done | bytes 196640 | tf_op jit(solution)/shard_map/ppermute | solution.py:45
  72.4 3.0 %collective-permute-start.10 = (bf16[16,192,128]{2,1,0:T(8,128)(2,1)S(1)}, bf16[16,192,128]{2,1,0:T(8,128)(2,1)S(1)}, u32[]{:S(2)}, u32[]{:S(2)}) collective-permute-start(bf16[16,192,128]{2,1,0:T(8,128)(2,1)S(1)} %constant_dynamic-update-slice_fusion.refs_2_), channel_id=1, source_target_pairs={{0,384},{8,392},{16,400},{24,408},{32,416},{40,424},{48,432},{56,4... | collective-permute-start | bytes 2359304 | tf_op jit(solution)/shard_map/ppermute | solution.py:45
  75.5 3.4 %collective-permute-start.8 = (bf16[16,192,128]{2,1,0:T(8,128)(2,1)S(1)}, bf16[16,192,128]{2,1,0:T(8,128)(2,1)S(1)}, u32[]{:S(2)}, u32[]{:S(2)}) collective-permute-start(bf16[16,192,128]{2,1,0:T(8,128)(2,1)S(1)} %constant_dynamic-update-slice_fusion.refs_2_), channel_id=1, source_target_pairs={{0,128},{8,136},{16,144},{24,152},{32,160},{40,168},{48,176},{56,1... | collective-permute-start | bytes 2359304 | tf_op jit(solution)/shard_map/ppermute | solution.py:45
  79.6 5.9 %shard_map.96 = (bf16[1536,256]{1,0:T(8,128)(2,1)}, f32[1536,128]{1,0:T(8,128)}, f32[1536,128]{1,0:T(8,128)}) custom-call(s32[16]{0:T(128)} %get-tuple-element.28.refs_0_, s32[1]{0:T(128)} %bitcast.refs_1_, bf16[16,192,128]{2,1,0:T(8,128)(2,1)} %copy-done.2, bf16[192,1024]{1,0:T(8,128)(2,1)} %refs_3_.1, bf16[192,128]{1,0:T(8,128)(2,1)} %refs_4_.1, ...), custom_call_target="tpu_custom_call" | custom-call | flops 2415919104 | bytes 8388608 | tf_op jit(solution)/shard_map/pallas_call | solution.py:256
  85.4 7.6 %collective-permute-done.8.refs_2_ = bf16[16,192,128]{2,1,0:T(8,128)(2,1)S(1)} collective-permute-done((bf16[16,192,128]{2,1,0:T(8,128)(2,1)S(1)}, bf16[16,192,128]{2,1,0:T(8,128)(2,1)S(1)}, u32[]{:S(2)}, u32[]{:S(2)}) %collective-permute-start.8) | collective-permute-done | bytes 786464 | tf_op jit(solution)/shard_map/ppermute | solution.py:45
  93.1 4.3 %collective-permute-start.9 = (bf16[8,192,128]{2,1,0:T(8,128)(2,1)S(1)}, bf16[8,192,128]{2,1,0:T(8,128)(2,1)S(1)}, u32[]{:S(2)}, u32[]{:S(2)}) collective-permute-start(bf16[8,192,128]{2,1,0:T(8,128)(2,1)S(1)} %slice.38), channel_id=1, source_target_pairs={{0,128},{8,136},{16,144},{24,152},{32,160},{40,168},{48,176},{56,1... | collective-permute-start | bytes 1179656 | tf_op jit(solution)/shard_map/ppermute | solution.py:45
  97.4 1.9 %collective-permute-start.11 = (bf16[8,192,128]{2,1,0:T(8,128)(2,1)S(1)}, bf16[8,192,128]{2,1,0:T(8,128)(2,1)S(1)}, u32[]{:S(2)}, u32[]{:S(2)}) collective-permute-start(bf16[8,192,128]{2,1,0:T(8,128)(2,1)S(1)} %slice.39), channel_id=1, source_target_pairs={{0,384},{8,392},{16,400},{24,408},{32,416},{40,424},{48,432},{56,4... | collective-permute-start | bytes 1179656 | tf_op jit(solution)/shard_map/ppermute | solution.py:45
  99.4 9.8 %shard_map.97 = (bf16[1536,256]{1,0:T(8,128)(2,1)}, f32[1536,128]{1,0:T(8,128)}, f32[1536,128]{1,0:T(8,128)}) custom-call(s32[32]{0:T(128)} %slice.33.refs_0_, s32[1]{0:T(128)} %bitcast.refs_1_, bf16[16,192,128]{2,1,0:T(8,128)(2,1)} %copy-done.1, bf16[16,192,128]{2,1,0:T(8,128)(2,1)} %copy-done, bf16[1536,256]{1,0:T(8,128)(2,1)} %get-tuple-element.12.refs_4_, ...), custom_call_target="tpu_custom_call" | custom-call | flops 4831838208 | bytes 8388608 | tf_op jit(solution)/shard_map/pallas_call | solution.py:256
  109.2 0.9 slice.40
  112.5 5.2 %shard_map.99 = bf16[128,2,256]{2,1,0:T(2,128)(2,1)} custom-call(s32[128]{0:T(128)} %get-tuple-element.27.refs_0_, s32[128]{0:T(128)} %get-tuple-element.26.refs_1_, f32[1536,128]{1,0:T(8,128)} %get-tuple-element.16.refs_6_.refs_2_, bf16[1536,2,128]{2,1,0:T(2,128)(2,1)} %bitcast.41, bf16[1536,2,128]{2,1,0:T(2,128)(2,1)} %bitcast.40, ...), custom_call_target="tpu_custom_call" | custom-call | bytes 8388608 | tf_op jit(solution)/shard_map/pallas_call | solution.py:314
  117.8 10.0 %all-to-all-start = ((bf16[128,2,1,256]{3,1,2,0:T(2,128)(2,1)}), bf16[128,2,1,256]{3,1,2,0:T(2,128)(2,1)S(1)}, u32[]{:S(2)}, u32[]{:S(2)}) async-start(bf16[128,2,1,256]{3,1,2,0:T(2,128)(2,1)} %bitcast.46), calls=%async_computation | async-start | bytes 262144 | tf_op jit(solution)/shard_map/all_to_all | solution.py:411
  127.8 40.1 %shard_map.98 = bf16[192,1024]{1,0:T(8,128)(2,1)} custom-call(s32[80]{0:T(128)} %pad_add_fusion.1.refs_0_, s32[1]{0:T(128)} %bitcast.refs_1_, bf16[8,192,128]{2,1,0:T(8,128)(2,1)} %copy-done.3, bf16[8,192,128]{2,1,0:T(8,128)(2,1)} %copy-done.4, bf16[64,208,128]{2,1,0:T(8,128)(2,1)} %all-gather.3.cloned.1.call-done.refs_4_, ...), custom_call_target="tpu_custom_call" | custom-call | flops 12079595520 | bytes 8388608 | tf_op jit(solution)/shard_map/pallas_call | solution.py:256
  (60 shorter events, 5.8 us)
Async XLA Ops:
  7.2 102.1 %all-gather.3.cloned.1.call-start = ((), (), s32[]{:S(2)}) async-start(), calls=%async_computation.1 | async-start | bytes 3620864 | tf_op jit(solution)/shard_map/all_gather | solution.py:49
  8.7 8.3 %collective-permute-start.12 = (bf16[208,128]{1,0:T(8,128)(2,1)}, bf16[208,128]{1,0:T(8,128)(2,1)S(1)}, u32[]{:S(2)}, u32[]{:S(2)}) collective-permute-start(bf16[208,128]{1,0:T(8,128)(2,1)} %get-tuple-element.11), channel_id=1, source_target_pairs={{0,128},{8,136},{16,144},{24,152},{32,160},{40,168},{48,176},{56,1... | collective-permute-start | bytes 159752 | tf_op jit(solution)/shard_map/ppermute | solution.py:45
  10.8 6.3 %collective-permute-start.13 = (bf16[208,128]{1,0:T(8,128)(2,1)}, bf16[208,128]{1,0:T(8,128)(2,1)S(1)}, u32[]{:S(2)}, u32[]{:S(2)}) collective-permute-start(bf16[208,128]{1,0:T(8,128)(2,1)} %get-tuple-element.11), channel_id=1, source_target_pairs={{0,384},{8,392},{16,400},{24,408},{32,416},{40,424},{48,432},{56,4... | collective-permute-start | bytes 159752 | tf_op jit(solution)/shard_map/ppermute | solution.py:45
  14.0 6.6 %collective-permute-start.14 = (bf16[208,128]{1,0:T(8,128)(2,1)}, bf16[208,128]{1,0:T(8,128)(2,1)S(1)}, u32[]{:S(2)}, u32[]{:S(2)}) collective-permute-start(bf16[208,128]{1,0:T(8,128)(2,1)} %get-tuple-element.11), channel_id=1, source_target_pairs={{0,256},{8,264},{16,272},{24,280},{32,288},{40,296},{48,304},{56,3... | collective-permute-start | bytes 159752 | tf_op jit(solution)/shard_map/ppermute | solution.py:45
  22.1 17.5 %collective-permute-start.1 = (bf16[192,128]{1,0:T(8,128)(2,1)}, bf16[192,128]{1,0:T(8,128)(2,1)S(1)}, u32[]{:S(2)}, u32[]{:S(2)}) collective-permute-start(bf16[192,128]{1,0:T(8,128)(2,1)} %get-tuple-element.10), channel_id=1, source_target_pairs={{0,32},{8,40},{16,48},{24,56},{32,64},{40,72},{48,80},{56,88},{64,... | collective-permute-start | bytes 147464 | tf_op jit(solution)/shard_map/ppermute | solution.py:45
  30.9 13.8 %collective-permute-start = (bf16[192,128]{1,0:T(8,128)(2,1)}, bf16[192,128]{1,0:T(8,128)(2,1)S(1)}, u32[]{:S(2)}, u32[]{:S(2)}) collective-permute-start(bf16[192,128]{1,0:T(8,128)(2,1)} %get-tuple-element.10), channel_id=1, source_target_pairs={{0,96},{8,104},{16,112},{24,120},{32,0},{40,8},{48,16},{56,24},{64... | collective-permute-start | bytes 147464 | tf_op jit(solution)/shard_map/ppermute | solution.py:45
  39.6 19.3 %collective-permute-start.2 = (bf16[96,128]{1,0:T(8,128)(2,1)S(1)}, bf16[96,128]{1,0:T(8,128)(2,1)S(1)}, u32[]{:S(2)}, u32[]{:S(2)}) collective-permute-start(bf16[96,128]{1,0:T(8,128)(2,1)S(1)} %slice.36), channel_id=1, source_target_pairs={{0,32},{8,40},{16,48},{24,56},{32,64},{40,72},{48,80},{56,88},{64,... | collective-permute-start | bytes 73736 | tf_op jit(solution)/shard_map/ppermute | solution.py:45
  44.8 14.1 %collective-permute-start.3 = (bf16[96,128]{1,0:T(8,128)(2,1)S(1)}, bf16[96,128]{1,0:T(8,128)(2,1)S(1)}, u32[]{:S(2)}, u32[]{:S(2)}) collective-permute-start(bf16[96,128]{1,0:T(8,128)(2,1)S(1)} %slice.37), channel_id=1, source_target_pairs={{0,96},{8,104},{16,112},{24,120},{32,0},{40,8},{48,16},{56,24},{64... | collective-permute-start | bytes 73736 | tf_op jit(solution)/shard_map/ppermute | solution.py:45
  50.5 21.8 %collective-permute-start.6 = (bf16[2,192,128]{2,1,0:T(8,128)(2,1)S(1)}, bf16[2,192,128]{2,1,0:T(8,128)(2,1)S(1)}, u32[]{:S(2)}, u32[]{:S(2)}) collective-permute-start(bf16[2,192,128]{2,1,0:T(8,128)(2,1)S(1)} %get-tuple-element.25), channel_id=1, source_target_pairs={{0,16},{8,24},{16,32},{24,40},{32,48},{40,56},{48,64},{56,72},{64,... | collective-permute-start | bytes 294920 | tf_op jit(solution)/shard_map/ppermute | solution.py:45
  53.6 18.7 %collective-permute-start.7 = (bf16[2,192,128]{2,1,0:T(8,128)(2,1)S(1)}, bf16[2,192,128]{2,1,0:T(8,128)(2,1)S(1)}, u32[]{:S(2)}, u32[]{:S(2)}) collective-permute-start(bf16[2,192,128]{2,1,0:T(8,128)(2,1)S(1)} %get-tuple-element.24), channel_id=1, source_target_pairs={{0,112},{8,120},{16,0},{24,8},{32,16},{40,24},{48,32},{56,40},{64,... | collective-permute-start | bytes 294920 | tf_op jit(solution)/shard_map/ppermute | solution.py:45
  59.7 10.3 %collective-permute-start.4 = (bf16[4,192,128]{2,1,0:T(8,128)(2,1)S(1)}, bf16[4,192,128]{2,1,0:T(8,128)(2,1)S(1)}, u32[]{:S(2)}, u32[]{:S(2)}) collective-permute-start(bf16[4,192,128]{2,1,0:T(8,128)(2,1)S(1)} %pad_maximum_fusion.1), channel_id=1, source_target_pairs={{0,8},{8,16},{16,24},{24,32},{32,40},{40,48},{48,56},{56,64},{64,7... | collective-permute-start | bytes 589832 | tf_op jit(solution)/shard_map/ppermute | solution.py:45
  61.7 10.7 %collective-permute-start.5 = (bf16[4,192,128]{2,1,0:T(8,128)(2,1)S(1)}, bf16[4,192,128]{2,1,0:T(8,128)(2,1)S(1)}, u32[]{:S(2)}, u32[]{:S(2)}) collective-permute-start(bf16[4,192,128]{2,1,0:T(8,128)(2,1)S(1)} %pad_maximum_fusion.1), channel_id=1, source_target_pairs={{0,120},{8,0},{16,8},{24,16},{32,24},{40,32},{48,40},{56,48},{64,5... | collective-permute-start | bytes 589832 | tf_op jit(solution)/shard_map/ppermute | solution.py:45
  72.4 7.2 %copy-start.2 = (bf16[16,192,128]{2,1,0:T(8,128)(2,1)}, bf16[16,192,128]{2,1,0:T(8,128)(2,1)S(1)}, u32[]{:S(2)}) copy-start(bf16[16,192,128]{2,1,0:T(8,128)(2,1)S(1)} %constant_dynamic-update-slice_fusion.refs_2_) | copy-start | bytes 2359300
  72.4 24.9 %collective-permute-start.10 = (bf16[16,192,128]{2,1,0:T(8,128)(2,1)S(1)}, bf16[16,192,128]{2,1,0:T(8,128)(2,1)S(1)}, u32[]{:S(2)}, u32[]{:S(2)}) collective-permute-start(bf16[16,192,128]{2,1,0:T(8,128)(2,1)S(1)} %constant_dynamic-update-slice_fusion.refs_2_), channel_id=1, source_target_pairs={{0,384},{8,392},{16,400},{24,408},{32,416},{40,424},{48,432},{56,4... | collective-permute-start | bytes 2359304 | tf_op jit(solution)/shard_map/ppermute | solution.py:45
  75.5 17.6 %collective-permute-start.8 = (bf16[16,192,128]{2,1,0:T(8,128)(2,1)S(1)}, bf16[16,192,128]{2,1,0:T(8,128)(2,1)S(1)}, u32[]{:S(2)}, u32[]{:S(2)}) collective-permute-start(bf16[16,192,128]{2,1,0:T(8,128)(2,1)S(1)} %constant_dynamic-update-slice_fusion.refs_2_), channel_id=1, source_target_pairs={{0,128},{8,136},{16,144},{24,152},{32,160},{40,168},{48,176},{56,1... | collective-permute-start | bytes 2359304 | tf_op jit(solution)/shard_map/ppermute | solution.py:45
  93.0 6.3 %copy-start.1 = (bf16[16,192,128]{2,1,0:T(8,128)(2,1)}, bf16[16,192,128]{2,1,0:T(8,128)(2,1)S(1)}, u32[]{:S(2)}) copy-start(bf16[16,192,128]{2,1,0:T(8,128)(2,1)S(1)} %collective-permute-done.8.refs_2_) | copy-start | bytes 2359300
  93.1 18.5 %collective-permute-start.9 = (bf16[8,192,128]{2,1,0:T(8,128)(2,1)S(1)}, bf16[8,192,128]{2,1,0:T(8,128)(2,1)S(1)}, u32[]{:S(2)}, u32[]{:S(2)}) collective-permute-start(bf16[8,192,128]{2,1,0:T(8,128)(2,1)S(1)} %slice.38), channel_id=1, source_target_pairs={{0,128},{8,136},{16,144},{24,152},{32,160},{40,168},{48,176},{56,1... | collective-permute-start | bytes 1179656 | tf_op jit(solution)/shard_map/ppermute | solution.py:45
  97.4 2.0 %copy-start = (bf16[16,192,128]{2,1,0:T(8,128)(2,1)}, bf16[16,192,128]{2,1,0:T(8,128)(2,1)S(1)}, u32[]{:S(2)}) copy-start(bf16[16,192,128]{2,1,0:T(8,128)(2,1)S(1)} %collective-permute-done.10.refs_3_) | copy-start | bytes 2359300
  97.4 14.2 %collective-permute-start.11 = (bf16[8,192,128]{2,1,0:T(8,128)(2,1)S(1)}, bf16[8,192,128]{2,1,0:T(8,128)(2,1)S(1)}, u32[]{:S(2)}, u32[]{:S(2)}) collective-permute-start(bf16[8,192,128]{2,1,0:T(8,128)(2,1)S(1)} %slice.39), channel_id=1, source_target_pairs={{0,384},{8,392},{16,400},{24,408},{32,416},{40,424},{48,432},{56,4... | collective-permute-start | bytes 1179656 | tf_op jit(solution)/shard_map/ppermute | solution.py:45
  99.4 11.3 %copy-start.5 = (s32[64]{0:T(128)S(1)}, s32[64]{0:T(128)}, u32[]{:S(2)}) copy-start(s32[64]{0:T(128)} %param.11) | copy-start | bytes 772
  111.6 0.8 copy-start.3
  111.6 0.9 copy-start.4
  117.8 50.1 %all-to-all-start = ((bf16[128,2,1,256]{3,1,2,0:T(2,128)(2,1)}), bf16[128,2,1,256]{3,1,2,0:T(2,128)(2,1)S(1)}, u32[]{:S(2)}, u32[]{:S(2)}) async-start(bf16[128,2,1,256]{3,1,2,0:T(2,128)(2,1)} %bitcast.46), calls=%async_computation | async-start | bytes 262144 | tf_op jit(solution)/shard_map/all_to_all | solution.py:411
Sparse Core Ops, SparseCore 0:
  22.2 79.6 all-gather.2

commit v6 on v5

--- a/solution.py
+++ b/solution.py
@@ -28,7 +28,7 @@
 WIDTH = 512
 DEAD = -1e30
 SCALE = math.log2(math.e) / math.sqrt(HD)
-LIMIT = 64.0 / SCALE
+LIMIT = 2.0**64
 VMEM_LIMIT = 56 * 1024 * 1024
 
 X_ORDER = [0, -1, 1, 2]
@@ -108,13 +108,13 @@
     if first:
         (q_ref, k_ref, v_ref), refs = refs[:3], refs[3:]
     else:
-        (q0, l0, acc0), refs = refs[:3], refs[3:]
+        (q0, acc0), refs = refs[:2], refs[2:]
     if last:
         out_ref, refs = refs[0], refs[1:]
-    q1, l1, acc1, kbuf, vbuf, sems = refs[:6]
-    stages, refs = refs[6 : 6 + n_src], refs[6 + n_src :]
+    q1, acc1, kbuf, vbuf, sems = refs[:5]
+    stages, refs = refs[5 : 5 + n_src], refs[5 + n_src :]
     if first:
-        q0, l0, acc0 = refs
+        q0, acc0 = refs
     live = live_ref[0]
 
     copies = [
@@ -135,14 +135,29 @@
             p = jnp.exp2((s - top) * SCALE)
             q0[at, 0:HD] = q
             q0[at, HD : 2 * HD] = reference_columns(top)
-            l0[at, :] = jnp.where(lanes(CAP) == 0, jnp.sum(p, axis=1, keepdims=True), 0.0)
-            acc0[at, :] = jnp.dot(
+            acc0[at, 0:HD] = jnp.dot(
                 p.astype(jnp.bfloat16), v_ref[...], preferred_element_type=jnp.float32
             )
+            acc0[at, HD : 2 * HD] = jnp.where(
+                lanes(CAP) == 0, jnp.sum(p, axis=1, keepdims=True), 0.0
+            )
 
     q1[...] = q0[...]
-    l1[...] = l0[...]
     acc1[...] = acc0[...]
+
+    height = kbuf.shape[0]
+    lane = lanes(16)
+    alive = jnp.where((lane >= 1) & (lane <= 3), 1.0, 0.0).astype(jnp.float32)
+    dead = jnp.where(lane == 0, DEAD, 0.0).astype(jnp.float32)
+    step = lax.broadcasted_iota(jnp.int32, (16, HD), 0)
+    fill = lanes(WIDTH)
+    fill_alive = jnp.where((fill >= 1) & (fill <= 3), 1.0, 0.0).astype(jnp.bfloat16)
+    fill_dead = jnp.where(fill == 0, DEAD, 0.0).astype(jnp.bfloat16)
+    fill_ones = jnp.where(fill == 0, 1.0, 0.0).astype(jnp.bfloat16)
+    for i in range(height // WIDTH):
+        at = slice(i * WIDTH, (i + 1) * WIDTH)
+        kbuf[at, HD : 2 * HD] = fill_alive
+        vbuf[at, HD : 2 * HD] = fill_ones
 
     for copy in copies:
         copy.wait()
@@ -150,47 +165,45 @@
     off = jnp.int32(0)
     base = 0
     for i in range(n_src):
-        tall = talls[i]
-        stage = stages[i]
-        row = lax.broadcasted_iota(jnp.int32, (tall, HD), 0)
-        lane = lanes(tall)
-        alive = jnp.where((lane >= 1) & (lane <= 3), 1.0, 0.0).astype(jnp.float32)
-        dead = jnp.where(lane == 0, DEAD, 0.0).astype(jnp.float32)
-
-        def pack(j, off, base=base, tall=tall, stage=stage, row=row, alive=alive, dead=dead):
+
+        def pack(j, off, base=base, tall=talls[i], stage=stages[i]):
             count = count_ref[base + j]
             at = pl.ds(pl.multiple_of(off, 16), tall)
             kbuf[at, 0:HD] = stage[j, 0:tall, :]
-            kbuf[at, HD : 2 * HD] = jnp.where(row < count, alive, dead).astype(jnp.bfloat16)
-            vbuf[at, :] = stage[j, tall : 2 * tall, :]
+            vbuf[at, 0:HD] = stage[j, tall : 2 * tall, :]
+            whole = (count // 16) * 16
+            part = count - whole
+
+            @pl.when(part > 0)
+            def _():
+                edge = pl.ds(pl.multiple_of(off + whole, 16), 16)
+                kbuf[edge, HD : 2 * HD] = jnp.where(step < part, alive, dead).astype(jnp.bfloat16)
+
             return off + ((count + 15) // 16) * 16
 
         off = lax.fori_loop(0, counts[i], pack, off)
         base += counts[i]
     at = pl.ds(pl.multiple_of(off, 16), WIDTH)
     kbuf[at, 0:HD] = jnp.zeros((WIDTH, HD), jnp.bfloat16)
-    kbuf[at, HD : 2 * HD] = jnp.where(lanes(WIDTH) == 0, DEAD, 0.0).astype(jnp.bfloat16)
-    vbuf[at, :] = jnp.zeros((WIDTH, HD), jnp.bfloat16)
+    kbuf[at, HD : 2 * HD] = fill_dead
+    vbuf[at, 0:HD] = jnp.zeros((WIDTH, HD), jnp.bfloat16)
     blocks = (off + WIDTH - 1) // WIDTH
 
     def block(i, track):
         at = pl.ds(pl.multiple_of(i * WIDTH, WIDTH), WIDTH)
         for t in range(TILES):
             rows = slice(t * TILE, (t + 1) * TILE)
-            s = dot_t(q1[rows, :], kbuf[at, :])
+            p = jnp.exp2(dot_t(q1[rows, :], kbuf[at, :]) * SCALE).astype(jnp.bfloat16)
             track = jnp.maximum(
-                track, jnp.max(by_lanes(jnp.maximum, s).reshape(TILE // 8, 8, HD), axis=0)
+                track, jnp.max(by_lanes(jnp.maximum, p).reshape(TILE // 16, 16, HD), axis=0)
             )
-            p = jnp.exp2(s * SCALE)
-            l1[rows, :] += by_lanes(jnp.add, p)
-            acc1[rows, :] += jnp.dot(
-                p.astype(jnp.bfloat16), vbuf[at, :], preferred_element_type=jnp.float32
-            )
+            acc1[rows, :] += jnp.dot(p, vbuf[at, :], preferred_element_type=jnp.float32)
         return track
 
-    track = lax.fori_loop(0, blocks, block, jnp.full((8, HD), DEAD, jnp.float32))
-
-    @pl.when(jnp.max(track) > LIMIT)
+    none = jnp.zeros((16, HD), jnp.bfloat16)
+    track = lax.fori_loop(0, blocks, block, none)
+
+    @pl.when(jnp.max(track.astype(jnp.float32)) > LIMIT)
     def _():
         for t in range(TILES):
             rows = slice(t * TILE, (t + 1) * TILE)
@@ -206,18 +219,16 @@
             m = -jnp.sum(
                 jnp.where((lane >= 1) & (lane <= 3), columns, 0.0), axis=1, keepdims=True
             )
-            factor = jnp.exp2(-rise * SCALE)
             q1[rows, HD : 2 * HD] = reference_columns(m + rise)
-            l1[rows, :] = l0[rows, :] * factor
-            acc1[rows, :] = acc0[rows, :] * factor
-        lax.fori_loop(0, blocks, block, jnp.full((8, HD), DEAD, jnp.float32))
+            acc1[rows, :] = acc0[rows, :] * jnp.exp2(-rise * SCALE)
+        lax.fori_loop(0, blocks, block, none)
 
     if last:
         ok = lax.broadcasted_iota(jnp.int32, (CAP, HD), 0) < live
         for h in range(GROUP):
             at = slice(h * CAP, (h + 1) * CAP)
-            total = jnp.sum(l1[at, :], axis=1, keepdims=True)
-            result = jnp.where(ok, acc1[at, :] / total, 0.0)
+            total = jnp.sum(acc1[at, HD : 2 * HD], axis=1, keepdims=True)
+            result = jnp.where(ok, acc1[at, 0:HD] / total, 0.0)
             out_ref[:, h * HD : (h + 1) * HD] = result.astype(jnp.bfloat16)
 
 
@@ -225,12 +236,12 @@
     talls = [ROWS_B if s.shape[1] == TALL_B else ROWS_A for s in sources]
     counts = [s.shape[0] for s in sources]
     keys = sum(c * t for c, t in zip(counts, talls))
+    height = (keys // WIDTH + 2) * WIDTH
     vmem = pl.BlockSpec(memory_space=pltpu.VMEM)
     smem = pl.BlockSpec(memory_space=pltpu.SMEM)
     state_shapes = [
         ((ROWS, 2 * HD), jnp.bfloat16),
-        ((ROWS, HD), jnp.float32),
-        ((ROWS, HD), jnp.float32),
+        ((ROWS, 2 * HD), jnp.float32),
     ]
     scratch_state = [pltpu.VMEM(*s) for s in state_shapes]
     if last:
@@ -238,12 +249,12 @@
         out_specs = vmem
     else:
         out_shape = [jax.ShapeDtypeStruct(*s) for s in state_shapes]
-        out_specs = [vmem] * 3
+        out_specs = [vmem] * 2
     scratch = (
         (scratch_state if last else [])
         + [
-            pltpu.VMEM((keys + WIDTH, 2 * HD), jnp.bfloat16),
-            pltpu.VMEM((keys + WIDTH, HD), jnp.bfloat16),
+            pltpu.VMEM((height, 2 * HD), jnp.bfloat16),
+            pltpu.VMEM((height, 2 * HD), jnp.bfloat16),
             pltpu.SemaphoreType.DMA((len(sources),)),
         ]
         + [pltpu.VMEM(s.shape, jnp.bfloat16) for s in sources]
@@ -256,7 +267,8 @@
     return pl.pallas_call(
         kernel,
         out_shape=out_shape,
-        in_specs=[smem, smem] + [pl.BlockSpec(memory_space=pl.ANY)] * len(sources) + [vmem] * 3,
+        in_specs=[smem, smem] + [pl.BlockSpec(memory_space=pl.ANY)] * len(sources)
+        + [vmem] * len(state),
         out_specs=out_specs,
         scratch_shapes=scratch,
         compiler_params=pltpu.CompilerParams(vmem_limit_bytes=VMEM_LIMIT),
@@ -402,6 +414,7 @@
     live = jnp.sum(jnp.where(jnp.arange(N, dtype=jnp.int32) == me, lengths, 0)).reshape(1)
     gathered, own, beside, across = exchange(*payloads(keys, values, page_owner))
     piece_a, piece_b = layout(me)
+    own, lengths = lax.optimization_barrier((own, lengths))
     count_a, count_b = live_counts(me, lengths, piece_a, piece_b)
     key_place, value_place = page_places(me, gathered, piece_a, piece_b, lengths)
     state = early_attention(own, beside, count_b, live, (queries, keys, values))

time: 177 us -> 190 us (1.073)
  the two profiles are of different devices: /device:TPU:39 before, /device:TPU:471 now
where the time goes in v6:
time: 190 us; the launch traced here: 189 us
  Pallas kernels  74.8 us (39%)
  starting transfers between devices  73 us (38%)
  waiting for transfers between devices  14.8 us (8%)
  between operations  14.5 us (8%)
  other arithmetic  6.89 us (4%)
  local copies, waits for them, and re-layouts  5.19 us (3%)
    pallas_call x3, Pallas kernels, attention(): pl.pallas_call(kernel, out_shape=out_shape, in_specs=[smem, smem] + [pl.B...  68 us
    ppermute x15, starting transfers between devices, shift(): return lax.ppermute(value, 'ctx', pairs)  52.4 us
    all_to_all x1, starting transfers between devices, body(): lax.all_to_all(outgoing.reshape(2 * N, PAGE, 1, 2 * HD), 'tp', split_axis...  20.6 us
    ppermute x15, waiting for transfers between devices, shift(): return lax.ppermute(value, 'ctx', pairs)  14.7 us
    pallas_call x1, Pallas kernels, select_pages(): pl.pallas_call(kernel, out_shape=jax.ShapeDtypeStruct((2 * N, PAGE, 2 * H...  5.25 us
  transfers between devices with their start and end apart: 17, of which 5 were waited for; matrix products, arithmetic and copies ran while one was open for 5% of the time, Pallas kernels for 36%

profile of v6, /device:TPU:471, one launch (start us, length us, event | category | flops | bytes accessed | tf_op | source)
XLA Modules:
  0.0 189.1 jit_solution(6546153304484443655)
XLA Ops:
  7.2 1.5 shard_map.95
  8.7 2.1 %collective-permute-start.12 = (bf16[208,128]{1,0:T(8,128)(2,1)}, bf16[208,128]{1,0:T(8,128)(2,1)S(1)}, u32[]{:S(2)}, u32[]{:S(2)}) collective-permute-start(bf16[208,128]{1,0:T(8,128)(2,1)} %get-tuple-element.12), channel_id=1, source_target_pairs={{0,128},{8,136},{16,144},{24,152},{32,160},{40,168},{48,176},{56,1... | collective-permute-start | bytes 159752 | tf_op jit(solution)/shard_map/ppermute | solution.py:45
  10.8 3.2 %collective-permute-start.13 = (bf16[208,128]{1,0:T(8,128)(2,1)}, bf16[208,128]{1,0:T(8,128)(2,1)S(1)}, u32[]{:S(2)}, u32[]{:S(2)}) collective-permute-start(bf16[208,128]{1,0:T(8,128)(2,1)} %get-tuple-element.12), channel_id=1, source_target_pairs={{0,384},{8,392},{16,400},{24,408},{32,416},{40,424},{48,432},{56,4... | collective-permute-start | bytes 159752 | tf_op jit(solution)/shard_map/ppermute | solution.py:45
  14.0 3.0 %collective-permute-start.14 = (bf16[208,128]{1,0:T(8,128)(2,1)}, bf16[208,128]{1,0:T(8,128)(2,1)S(1)}, u32[]{:S(2)}, u32[]{:S(2)}) collective-permute-start(bf16[208,128]{1,0:T(8,128)(2,1)} %get-tuple-element.12), channel_id=1, source_target_pairs={{0,256},{8,264},{16,272},{24,280},{32,288},{40,296},{48,304},{56,3... | collective-permute-start | bytes 159752 | tf_op jit(solution)/shard_map/ppermute | solution.py:45
  17.1 3.5 %collective-permute-done.14 = bf16[208,128]{1,0:T(8,128)(2,1)S(1)} collective-permute-done((bf16[208,128]{1,0:T(8,128)(2,1)}, bf16[208,128]{1,0:T(8,128)(2,1)S(1)}, u32[]{:S(2)}, u32[]{:S(2)}) %collective-permute-start.14) | collective-permute-done | bytes 53280 | tf_op jit(solution)/shard_map/ppermute | solution.py:45
  20.6 1.5 pad_maximum_fusion
  22.1 1.9 %collective-permute-start.1 = (bf16[192,128]{1,0:T(8,128)(2,1)}, bf16[192,128]{1,0:T(8,128)(2,1)S(1)}, u32[]{:S(2)}, u32[]{:S(2)}) collective-permute-start(bf16[192,128]{1,0:T(8,128)(2,1)} %get-tuple-element.10), channel_id=1, source_target_pairs={{0,32},{8,40},{16,48},{24,56},{32,64},{40,72},{48,80},{56,88},{64,... | collective-permute-start | bytes 147464 | tf_op jit(solution)/shard_map/ppermute | solution.py:45
  24.1 7.3 %collective-permute-start = (bf16[192,128]{1,0:T(8,128)(2,1)}, bf16[192,128]{1,0:T(8,128)(2,1)S(1)}, u32[]{:S(2)}, u32[]{:S(2)}) collective-permute-start(bf16[192,128]{1,0:T(8,128)(2,1)} %get-tuple-element.10), channel_id=1, source_target_pairs={{0,96},{8,104},{16,112},{24,120},{32,0},{40,8},{48,16},{56,24},{64... | collective-permute-start | bytes 147464 | tf_op jit(solution)/shard_map/ppermute | solution.py:45
  32.8 1.9 %collective-permute-start.2 = (bf16[96,128]{1,0:T(8,128)(2,1)S(1)}, bf16[96,128]{1,0:T(8,128)(2,1)S(1)}, u32[]{:S(2)}, u32[]{:S(2)}) collective-permute-start(bf16[96,128]{1,0:T(8,128)(2,1)S(1)} %slice.36), channel_id=1, source_target_pairs={{0,32},{8,40},{16,48},{24,56},{32,64},{40,72},{48,80},{56,88},{64,... | collective-permute-start | bytes 73736 | tf_op jit(solution)/shard_map/ppermute | solution.py:45
  34.7 7.3 %collective-permute-start.3 = (bf16[96,128]{1,0:T(8,128)(2,1)S(1)}, bf16[96,128]{1,0:T(8,128)(2,1)S(1)}, u32[]{:S(2)}, u32[]{:S(2)}) collective-permute-start(bf16[96,128]{1,0:T(8,128)(2,1)S(1)} %slice.37), channel_id=1, source_target_pairs={{0,96},{8,104},{16,112},{24,120},{32,0},{40,8},{48,16},{56,24},{64... | collective-permute-start | bytes 73736 | tf_op jit(solution)/shard_map/ppermute | solution.py:45
  42.0 0.8 constant_dynamic-update-slice_fusion.6
  42.8 0.9 pad_maximum_fusion.3
  43.7 1.9 %collective-permute-start.6 = (bf16[2,192,128]{2,1,0:T(8,128)(2,1)S(1)}, bf16[2,192,128]{2,1,0:T(8,128)(2,1)S(1)}, u32[]{:S(2)}, u32[]{:S(2)}) collective-permute-start(bf16[2,192,128]{2,1,0:T(8,128)(2,1)S(1)} %get-tuple-element.25), channel_id=1, source_target_pairs={{0,16},{8,24},{16,32},{24,40},{32,48},{40,56},{48,64},{56,72},{64,... | collective-permute-start | bytes 294920 | tf_op jit(solution)/shard_map/ppermute | solution.py:45
  45.6 4.3 %collective-permute-start.7 = (bf16[2,192,128]{2,1,0:T(8,128)(2,1)S(1)}, bf16[2,192,128]{2,1,0:T(8,128)(2,1)S(1)}, u32[]{:S(2)}, u32[]{:S(2)}) collective-permute-start(bf16[2,192,128]{2,1,0:T(8,128)(2,1)S(1)} %get-tuple-element.24), channel_id=1, source_target_pairs={{0,112},{8,120},{16,0},{24,8},{32,16},{40,24},{48,32},{56,40},{64,... | collective-permute-start | bytes 294920 | tf_op jit(solution)/shard_map/ppermute | solution.py:45
  49.9 0.8 pad_maximum_fusion.1
  50.8 2.6 %collective-permute-start.4 = (bf16[4,192,128]{2,1,0:T(8,128)(2,1)S(1)}, bf16[4,192,128]{2,1,0:T(8,128)(2,1)S(1)}, u32[]{:S(2)}, u32[]{:S(2)}) collective-permute-start(bf16[4,192,128]{2,1,0:T(8,128)(2,1)S(1)} %pad_maximum_fusion.1), channel_id=1, source_target_pairs={{0,8},{8,16},{16,24},{24,32},{32,40},{40,48},{48,56},{56,64},{64,7... | collective-permute-start | bytes 589832 | tf_op jit(solution)/shard_map/ppermute | solution.py:45
  53.4 3.1 %collective-permute-start.5 = (bf16[4,192,128]{2,1,0:T(8,128)(2,1)S(1)}, bf16[4,192,128]{2,1,0:T(8,128)(2,1)S(1)}, u32[]{:S(2)}, u32[]{:S(2)}) collective-permute-start(bf16[4,192,128]{2,1,0:T(8,128)(2,1)S(1)} %pad_maximum_fusion.1), channel_id=1, source_target_pairs={{0,120},{8,0},{16,8},{24,16},{32,24},{40,32},{48,40},{56,48},{64,5... | collective-permute-start | bytes 589832 | tf_op jit(solution)/shard_map/ppermute | solution.py:45
  56.6 6.3 %collective-permute-done.4 = bf16[4,192,128]{2,1,0:T(8,128)(2,1)S(1)} collective-permute-done((bf16[4,192,128]{2,1,0:T(8,128)(2,1)S(1)}, bf16[4,192,128]{2,1,0:T(8,128)(2,1)S(1)}, u32[]{:S(2)}, u32[]{:S(2)}) %collective-permute-start.4) | collective-permute-done | bytes 196640 | tf_op jit(solution)/shard_map/ppermute | solution.py:45
  62.9 2.4 %collective-permute-done.5 = bf16[4,192,128]{2,1,0:T(8,128)(2,1)S(1)} collective-permute-done((bf16[4,192,128]{2,1,0:T(8,128)(2,1)S(1)}, bf16[4,192,128]{2,1,0:T(8,128)(2,1)S(1)}, u32[]{:S(2)}, u32[]{:S(2)}) %collective-permute-start.5) | collective-permute-done | bytes 196640 | tf_op jit(solution)/shard_map/ppermute | solution.py:45
  65.4 1.9 %collective-permute-start.10 = (bf16[16,192,128]{2,1,0:T(8,128)(2,1)S(1)}, bf16[16,192,128]{2,1,0:T(8,128)(2,1)S(1)}, u32[]{:S(2)}, u32[]{:S(2)}) collective-permute-start(bf16[16,192,128]{2,1,0:T(8,128)(2,1)S(1)} %constant_dynamic-update-slice_fusion.refs_2_), channel_id=1, source_target_pairs={{0,384},{8,392},{16,400},{24,408},{32,416},{40,424},{48,432},{56,4... | collective-permute-start | bytes 2359304 | tf_op jit(solution)/shard_map/ppermute | solution.py:45
  67.3 4.6 %collective-permute-start.8 = (bf16[16,192,128]{2,1,0:T(8,128)(2,1)S(1)}, bf16[16,192,128]{2,1,0:T(8,128)(2,1)S(1)}, u32[]{:S(2)}, u32[]{:S(2)}) collective-permute-start(bf16[16,192,128]{2,1,0:T(8,128)(2,1)S(1)} %constant_dynamic-update-slice_fusion.refs_2_), channel_id=1, source_target_pairs={{0,128},{8,136},{16,144},{24,152},{32,160},{40,168},{48,176},{56,1... | collective-permute-start | bytes 2359304 | tf_op jit(solution)/shard_map/ppermute | solution.py:45
  74.5 7.4 %shard_map.96 = (bf16[1536,256]{1,0:T(8,128)(2,1)}, f32[1536,256]{1,0:T(8,128)}) custom-call(s32[16]{0:T(128)} %get-tuple-element.28.refs_0_, s32[1]{0:T(128)} %bitcast.5.refs_1_, bf16[16,192,128]{2,1,0:T(8,128)(2,1)} %copy-done.2, bf16[192,1024]{1,0:T(8,128)(2,1)} %refs_3_.1, bf16[192,128]{1,0:T(8,128)(2,1)} %refs_4_.1, bf16[192,128]{1,0:T(8,128)(2,1)} %refs_5_.1), custom_call_target="tpu_custom_call" | custom-call | flops 2415919104 | bytes 8388608 | tf_op jit(solution)/shard_map/pallas_call | solution.py:267
  81.9 2.5 %collective-permute-done.8.refs_2_ = bf16[16,192,128]{2,1,0:T(8,128)(2,1)S(1)} collective-permute-done((bf16[16,192,128]{2,1,0:T(8,128)(2,1)S(1)}, bf16[16,192,128]{2,1,0:T(8,128)(2,1)S(1)}, u32[]{:S(2)}, u32[]{:S(2)}) %collective-permute-start.8) | collective-permute-done | bytes 786464 | tf_op jit(solution)/shard_map/ppermute | solution.py:45
  84.5 5.3 %collective-permute-start.9 = (bf16[8,192,128]{2,1,0:T(8,128)(2,1)S(1)}, bf16[8,192,128]{2,1,0:T(8,128)(2,1)S(1)}, u32[]{:S(2)}, u32[]{:S(2)}) collective-permute-start(bf16[8,192,128]{2,1,0:T(8,128)(2,1)S(1)} %slice.38), channel_id=1, source_target_pairs={{0,128},{8,136},{16,144},{24,152},{32,160},{40,168},{48,176},{56,1... | collective-permute-start | bytes 1179656 | tf_op jit(solution)/shard_map/ppermute | solution.py:45
  89.9 1.9 %collective-permute-start.11 = (bf16[8,192,128]{2,1,0:T(8,128)(2,1)S(1)}, bf16[8,192,128]{2,1,0:T(8,128)(2,1)S(1)}, u32[]{:S(2)}, u32[]{:S(2)}) collective-permute-start(bf16[8,192,128]{2,1,0:T(8,128)(2,1)S(1)} %slice.39), channel_id=1, source_target_pairs={{0,384},{8,392},{16,400},{24,408},{32,416},{40,424},{48,432},{56,4... | collective-permute-start | bytes 1179656 | tf_op jit(solution)/shard_map/ppermute | solution.py:45
  91.8 11.7 %shard_map.97 = (bf16[1536,256]{1,0:T(8,128)(2,1)}, f32[1536,256]{1,0:T(8,128)}) custom-call(s32[32]{0:T(128)} %slice.33.refs_0_, s32[1]{0:T(128)} %bitcast.5.refs_1_, bf16[16,192,128]{2,1,0:T(8,128)(2,1)} %copy-done.1, bf16[16,192,128]{2,1,0:T(8,128)(2,1)} %copy-done, bf16[1536,256]{1,0:T(8,128)(2,1)} %get-tuple-element.14.refs_4_, ...), custom_call_target="tpu_custom_call" | custom-call | flops 4831838208 | bytes 8388608 | tf_op jit(solution)/shard_map/pallas_call | solution.py:267
  103.5 0.9 slice.40
  105.8 0.7 copy-done.3
  106.7 5.2 %shard_map.99 = bf16[128,2,256]{2,1,0:T(2,128)(2,1)} custom-call(s32[128]{0:T(128)} %get-tuple-element.27.refs_0_, s32[128]{0:T(128)} %get-tuple-element.26.refs_1_, f32[1536,256]{1,0:T(8,128)} %get-tuple-element.17.refs_6_.refs_2_, bf16[1536,2,128]{2,1,0:T(2,128)(2,1)} %bitcast.41, bf16[1536,2,128]{2,1,0:T(2,128)(2,1)} %bitcast.40, ...), custom_call_target="tpu_custom_call" | custom-call | bytes 8388608 | tf_op jit(solution)/shard_map/pallas_call | solution.py:326
  112.0 20.6 %all-to-all-start = ((bf16[128,2,1,256]{3,1,2,0:T(2,128)(2,1)}), bf16[128,2,1,256]{3,1,2,0:T(2,128)(2,1)S(1)}, u32[]{:S(2)}, u32[]{:S(2)}) async-start(bf16[128,2,1,256]{3,1,2,0:T(2,128)(2,1)} %bitcast.46), calls=%async_computation | async-start | bytes 262144 | tf_op jit(solution)/shard_map/all_to_all | solution.py:424
  132.6 48.9 %shard_map.98 = bf16[192,1024]{1,0:T(8,128)(2,1)} custom-call(s32[80]{0:T(128)} %pad_add_fusion.1.refs_0_, s32[1]{0:T(128)} %bitcast.5.refs_1_, bf16[8,192,128]{2,1,0:T(8,128)(2,1)} %copy-done.3, bf16[8,192,128]{2,1,0:T(8,128)(2,1)} %copy-done.4, bf16[64,208,128]{2,1,0:T(8,128)(2,1)} %all-gather.3.cloned.1.call-done.refs_4_, ...), custom_call_target="tpu_custom_call" | custom-call | flops 12079595520 | bytes 8388608 | tf_op jit(solution)/shard_map/pallas_call | solution.py:267
  181.5 0.7 copy.26
  (61 shorter events, 5.8 us)
Async XLA Ops:
  7.2 96.4 %all-gather.3.cloned.1.call-start = ((), (), s32[]{:S(2)}) async-start(), calls=%async_computation.1 | async-start | bytes 3620864 | tf_op jit(solution)/shard_map/all_gather | solution.py:49
  8.7 8.3 %collective-permute-start.12 = (bf16[208,128]{1,0:T(8,128)(2,1)}, bf16[208,128]{1,0:T(8,128)(2,1)S(1)}, u32[]{:S(2)}, u32[]{:S(2)}) collective-permute-start(bf16[208,128]{1,0:T(8,128)(2,1)} %get-tuple-element.12), channel_id=1, source_target_pairs={{0,128},{8,136},{16,144},{24,152},{32,160},{40,168},{48,176},{56,1... | collective-permute-start | bytes 159752 | tf_op jit(solution)/shard_map/ppermute | solution.py:45
  10.8 6.3 %collective-permute-start.13 = (bf16[208,128]{1,0:T(8,128)(2,1)}, bf16[208,128]{1,0:T(8,128)(2,1)S(1)}, u32[]{:S(2)}, u32[]{:S(2)}) collective-permute-start(bf16[208,128]{1,0:T(8,128)(2,1)} %get-tuple-element.12), channel_id=1, source_target_pairs={{0,384},{8,392},{16,400},{24,408},{32,416},{40,424},{48,432},{56,4... | collective-permute-start | bytes 159752 | tf_op jit(solution)/shard_map/ppermute | solution.py:45
  14.0 6.6 %collective-permute-start.14 = (bf16[208,128]{1,0:T(8,128)(2,1)}, bf16[208,128]{1,0:T(8,128)(2,1)S(1)}, u32[]{:S(2)}, u32[]{:S(2)}) collective-permute-start(bf16[208,128]{1,0:T(8,128)(2,1)} %get-tuple-element.12), channel_id=1, source_target_pairs={{0,256},{8,264},{16,272},{24,280},{32,288},{40,296},{48,304},{56,3... | collective-permute-start | bytes 159752 | tf_op jit(solution)/shard_map/ppermute | solution.py:45
  20.6 51.3 %copy-start.5 = (s32[64]{0:T(128)S(1)}, s32[64]{0:T(128)}, u32[]{:S(2)}) copy-start(s32[64]{0:T(128)} %param.11) | copy-start | bytes 772
  20.6 52.2 %copy-start.6 = (s32[64]{0:T(128)S(1)}, s32[64]{0:T(128)}, u32[]{:S(2)}) copy-start(s32[64]{0:T(128)} %constant.103.clone) | copy-start | bytes 772
  22.1 10.6 %collective-permute-start.1 = (bf16[192,128]{1,0:T(8,128)(2,1)}, bf16[192,128]{1,0:T(8,128)(2,1)S(1)}, u32[]{:S(2)}, u32[]{:S(2)}) collective-permute-start(bf16[192,128]{1,0:T(8,128)(2,1)} %get-tuple-element.10), channel_id=1, source_target_pairs={{0,32},{8,40},{16,48},{24,56},{32,64},{40,72},{48,80},{56,88},{64,... | collective-permute-start | bytes 147464 | tf_op jit(solution)/shard_map/ppermute | solution.py:45
  24.1 10.6 %collective-permute-start = (bf16[192,128]{1,0:T(8,128)(2,1)}, bf16[192,128]{1,0:T(8,128)(2,1)S(1)}, u32[]{:S(2)}, u32[]{:S(2)}) collective-permute-start(bf16[192,128]{1,0:T(8,128)(2,1)} %get-tuple-element.10), channel_id=1, source_target_pairs={{0,96},{8,104},{16,112},{24,120},{32,0},{40,8},{48,16},{56,24},{64... | collective-permute-start | bytes 147464 | tf_op jit(solution)/shard_map/ppermute | solution.py:45
  32.8 17.1 %collective-permute-start.2 = (bf16[96,128]{1,0:T(8,128)(2,1)S(1)}, bf16[96,128]{1,0:T(8,128)(2,1)S(1)}, u32[]{:S(2)}, u32[]{:S(2)}) collective-permute-start(bf16[96,128]{1,0:T(8,128)(2,1)S(1)} %slice.36), channel_id=1, source_target_pairs={{0,32},{8,40},{16,48},{24,56},{32,64},{40,72},{48,80},{56,88},{64,... | collective-permute-start | bytes 73736 | tf_op jit(solution)/shard_map/ppermute | solution.py:45
  34.7 15.2 %collective-permute-start.3 = (bf16[96,128]{1,0:T(8,128)(2,1)S(1)}, bf16[96,128]{1,0:T(8,128)(2,1)S(1)}, u32[]{:S(2)}, u32[]{:S(2)}) collective-permute-start(bf16[96,128]{1,0:T(8,128)(2,1)S(1)} %slice.37), channel_id=1, source_target_pairs={{0,96},{8,104},{16,112},{24,120},{32,0},{40,8},{48,16},{56,24},{64... | collective-permute-start | bytes 73736 | tf_op jit(solution)/shard_map/ppermute | solution.py:45
  43.7 21.6 %collective-permute-start.6 = (bf16[2,192,128]{2,1,0:T(8,128)(2,1)S(1)}, bf16[2,192,128]{2,1,0:T(8,128)(2,1)S(1)}, u32[]{:S(2)}, u32[]{:S(2)}) collective-permute-start(bf16[2,192,128]{2,1,0:T(8,128)(2,1)S(1)} %get-tuple-element.25), channel_id=1, source_target_pairs={{0,16},{8,24},{16,32},{24,40},{32,48},{40,56},{48,64},{56,72},{64,... | collective-permute-start | bytes 294920 | tf_op jit(solution)/shard_map/ppermute | solution.py:45
  45.6 19.7 %collective-permute-start.7 = (bf16[2,192,128]{2,1,0:T(8,128)(2,1)S(1)}, bf16[2,192,128]{2,1,0:T(8,128)(2,1)S(1)}, u32[]{:S(2)}, u32[]{:S(2)}) collective-permute-start(bf16[2,192,128]{2,1,0:T(8,128)(2,1)S(1)} %get-tuple-element.24), channel_id=1, source_target_pairs={{0,112},{8,120},{16,0},{24,8},{32,16},{40,24},{48,32},{56,40},{64,... | collective-permute-start | bytes 294920 | tf_op jit(solution)/shard_map/ppermute | solution.py:45
  50.8 12.1 %collective-permute-start.4 = (bf16[4,192,128]{2,1,0:T(8,128)(2,1)S(1)}, bf16[4,192,128]{2,1,0:T(8,128)(2,1)S(1)}, u32[]{:S(2)}, u32[]{:S(2)}) collective-permute-start(bf16[4,192,128]{2,1,0:T(8,128)(2,1)S(1)} %pad_maximum_fusion.1), channel_id=1, source_target_pairs={{0,8},{8,16},{16,24},{24,32},{32,40},{40,48},{48,56},{56,64},{64,7... | collective-permute-start | bytes 589832 | tf_op jit(solution)/shard_map/ppermute | solution.py:45
  53.4 11.8 %collective-permute-start.5 = (bf16[4,192,128]{2,1,0:T(8,128)(2,1)S(1)}, bf16[4,192,128]{2,1,0:T(8,128)(2,1)S(1)}, u32[]{:S(2)}, u32[]{:S(2)}) collective-permute-start(bf16[4,192,128]{2,1,0:T(8,128)(2,1)S(1)} %pad_maximum_fusion.1), channel_id=1, source_target_pairs={{0,120},{8,0},{16,8},{24,16},{32,24},{40,32},{48,40},{56,48},{64,5... | collective-permute-start | bytes 589832 | tf_op jit(solution)/shard_map/ppermute | solution.py:45
  65.4 9.1 %copy-start.2 = (bf16[16,192,128]{2,1,0:T(8,128)(2,1)}, bf16[16,192,128]{2,1,0:T(8,128)(2,1)S(1)}, u32[]{:S(2)}) copy-start(bf16[16,192,128]{2,1,0:T(8,128)(2,1)S(1)} %constant_dynamic-update-slice_fusion.refs_2_) | copy-start | bytes 2359300
  65.4 24.4 %collective-permute-start.10 = (bf16[16,192,128]{2,1,0:T(8,128)(2,1)S(1)}, bf16[16,192,128]{2,1,0:T(8,128)(2,1)S(1)}, u32[]{:S(2)}, u32[]{:S(2)}) collective-permute-start(bf16[16,192,128]{2,1,0:T(8,128)(2,1)S(1)} %constant_dynamic-update-slice_fusion.refs_2_), channel_id=1, source_target_pairs={{0,384},{8,392},{16,400},{24,408},{32,416},{40,424},{48,432},{56,4... | collective-permute-start | bytes 2359304 | tf_op jit(solution)/shard_map/ppermute | solution.py:45
  67.3 17.1 %collective-permute-start.8 = (bf16[16,192,128]{2,1,0:T(8,128)(2,1)S(1)}, bf16[16,192,128]{2,1,0:T(8,128)(2,1)S(1)}, u32[]{:S(2)}, u32[]{:S(2)}) collective-permute-start(bf16[16,192,128]{2,1,0:T(8,128)(2,1)S(1)} %constant_dynamic-update-slice_fusion.refs_2_), channel_id=1, source_target_pairs={{0,128},{8,136},{16,144},{24,152},{32,160},{40,168},{48,176},{56,1... | collective-permute-start | bytes 2359304 | tf_op jit(solution)/shard_map/ppermute | solution.py:45
  84.4 7.3 %copy-start.1 = (bf16[16,192,128]{2,1,0:T(8,128)(2,1)}, bf16[16,192,128]{2,1,0:T(8,128)(2,1)S(1)}, u32[]{:S(2)}) copy-start(bf16[16,192,128]{2,1,0:T(8,128)(2,1)S(1)} %collective-permute-done.8.refs_2_) | copy-start | bytes 2359300
  84.5 21.3 %collective-permute-start.9 = (bf16[8,192,128]{2,1,0:T(8,128)(2,1)S(1)}, bf16[8,192,128]{2,1,0:T(8,128)(2,1)S(1)}, u32[]{:S(2)}, u32[]{:S(2)}) collective-permute-start(bf16[8,192,128]{2,1,0:T(8,128)(2,1)S(1)} %slice.38), channel_id=1, source_target_pairs={{0,128},{8,136},{16,144},{24,152},{32,160},{40,168},{48,176},{56,1... | collective-permute-start | bytes 1179656 | tf_op jit(solution)/shard_map/ppermute | solution.py:45
  89.8 2.0 %copy-start = (bf16[16,192,128]{2,1,0:T(8,128)(2,1)}, bf16[16,192,128]{2,1,0:T(8,128)(2,1)S(1)}, u32[]{:S(2)}) copy-start(bf16[16,192,128]{2,1,0:T(8,128)(2,1)S(1)} %collective-permute-done.10.refs_3_) | copy-start | bytes 2359300
  89.9 16.0 %collective-permute-start.11 = (bf16[8,192,128]{2,1,0:T(8,128)(2,1)S(1)}, bf16[8,192,128]{2,1,0:T(8,128)(2,1)S(1)}, u32[]{:S(2)}, u32[]{:S(2)}) collective-permute-start(bf16[8,192,128]{2,1,0:T(8,128)(2,1)S(1)} %slice.39), channel_id=1, source_target_pairs={{0,384},{8,392},{16,400},{24,408},{32,416},{40,424},{48,432},{56,4... | collective-permute-start | bytes 1179656 | tf_op jit(solution)/shard_map/ppermute | solution.py:45
  105.8 0.7 copy-start.3
  105.8 0.9 copy-start.4
  112.0 69.5 %all-to-all-start = ((bf16[128,2,1,256]{3,1,2,0:T(2,128)(2,1)}), bf16[128,2,1,256]{3,1,2,0:T(2,128)(2,1)S(1)}, u32[]{:S(2)}, u32[]{:S(2)}) async-start(bf16[128,2,1,256]{3,1,2,0:T(2,128)(2,1)} %bitcast.46), calls=%async_computation | async-start | bytes 262144 | tf_op jit(solution)/shard_map/all_to_all | solution.py:424
Sparse Core Ops, SparseCore 0:
  22.3 72.3 all-gather.2

commit v7 on v6

--- a/solution.py
+++ b/solution.py
@@ -74,21 +74,6 @@
     return lax.broadcasted_iota(jnp.int32, (rows, HD), 1)
 
 
-def reference_columns(m):
-    rows = m.shape[0]
-    m = jnp.broadcast_to(m, (rows, HD))
-    high = m.astype(jnp.bfloat16).astype(jnp.float32)
-    rest = m - high
-    middle = rest.astype(jnp.bfloat16).astype(jnp.float32)
-    low = rest - middle
-    lane = lanes(rows)
-    out = jnp.where(lane == 0, 1.0, 0.0)
-    out = jnp.where(lane == 1, -high, out)
-    out = jnp.where(lane == 2, -middle, out)
-    out = jnp.where(lane == 3, -low, out)
-    return out.astype(jnp.bfloat16)
-
-
 def dot_t(a, b):
     return lax.dot_general(a, b, (((1,), (1,)), ((), ())), preferred_element_type=jnp.float32)
 
@@ -108,13 +93,13 @@
     if first:
         (q_ref, k_ref, v_ref), refs = refs[:3], refs[3:]
     else:
-        (q0, acc0), refs = refs[:2], refs[2:]
+        (q_ref, m0, acc0), refs = refs[:3], refs[3:]
     if last:
         out_ref, refs = refs[0], refs[1:]
-    q1, acc1, kbuf, vbuf, sems = refs[:5]
-    stages, refs = refs[5 : 5 + n_src], refs[5 + n_src :]
+    m1, acc1, qs, kbuf, vbuf, sems = refs[:6]
+    stages, refs = refs[6 : 6 + n_src], refs[6 + n_src :]
     if first:
-        q0, acc0 = refs
+        m0, acc0 = refs
     live = live_ref[0]
 
     copies = [
@@ -122,6 +107,9 @@
     ]
     for copy in copies:
         copy.start()
+
+    for h in range(GROUP):
+        qs[h * CAP : (h + 1) * CAP, :] = q_ref[:, h * HD : (h + 1) * HD]
 
     if first:
         row = lax.broadcasted_iota(jnp.int32, (CAP, CAP), 0)
@@ -129,12 +117,10 @@
         bias = jnp.where((col <= row) & (col < live), 0.0, DEAD).astype(jnp.float32)
         for h in range(GROUP):
             at = slice(h * CAP, (h + 1) * CAP)
-            q = q_ref[:, h * HD : (h + 1) * HD]
-            s = dot_t(q, k_ref[...]) + bias
+            s = dot_t(qs[at, :], k_ref[...]) * SCALE + bias
             top = jnp.max(s, axis=1, keepdims=True)
-            p = jnp.exp2((s - top) * SCALE)
-            q0[at, 0:HD] = q
-            q0[at, HD : 2 * HD] = reference_columns(top)
+            p = jnp.exp2(s - top)
+            m0[at, :] = jnp.broadcast_to(top, (CAP, HD))
             acc0[at, 0:HD] = jnp.dot(
                 p.astype(jnp.bfloat16), v_ref[...], preferred_element_type=jnp.float32
             )
@@ -142,22 +128,15 @@
                 lanes(CAP) == 0, jnp.sum(p, axis=1, keepdims=True), 0.0
             )
 
-    q1[...] = q0[...]
+    m1[...] = m0[...]
     acc1[...] = acc0[...]
 
     height = kbuf.shape[0]
-    lane = lanes(16)
-    alive = jnp.where((lane >= 1) & (lane <= 3), 1.0, 0.0).astype(jnp.float32)
-    dead = jnp.where(lane == 0, DEAD, 0.0).astype(jnp.float32)
     step = lax.broadcasted_iota(jnp.int32, (16, HD), 0)
-    fill = lanes(WIDTH)
-    fill_alive = jnp.where((fill >= 1) & (fill <= 3), 1.0, 0.0).astype(jnp.bfloat16)
-    fill_dead = jnp.where(fill == 0, DEAD, 0.0).astype(jnp.bfloat16)
-    fill_ones = jnp.where(fill == 0, 1.0, 0.0).astype(jnp.bfloat16)
+    lead = jnp.where(lanes(16) == 0, 1.0, 0.0).astype(jnp.float32)
+    ones = jnp.where(lanes(WIDTH) == 0, 1.0, 0.0).astype(jnp.bfloat16)
     for i in range(height // WIDTH):
-        at = slice(i * WIDTH, (i + 1) * WIDTH)
-        kbuf[at, HD : 2 * HD] = fill_alive
-        vbuf[at, HD : 2 * HD] = fill_ones
+        vbuf[i * WIDTH : (i + 1) * WIDTH, HD : 2 * HD] = ones
 
     for copy in copies:
         copy.wait()
@@ -169,7 +148,7 @@
         def pack(j, off, base=base, tall=talls[i], stage=stages[i]):
             count = count_ref[base + j]
             at = pl.ds(pl.multiple_of(off, 16), tall)
-            kbuf[at, 0:HD] = stage[j, 0:tall, :]
+            kbuf[at, :] = stage[j, 0:tall, :]
             vbuf[at, 0:HD] = stage[j, tall : 2 * tall, :]
             whole = (count // 16) * 16
             part = count - whole
@@ -177,23 +156,30 @@
             @pl.when(part > 0)
             def _():
                 edge = pl.ds(pl.multiple_of(off + whole, 16), 16)
-                kbuf[edge, HD : 2 * HD] = jnp.where(step < part, alive, dead).astype(jnp.bfloat16)
+                keep = step < part
+                k = kbuf[edge, :].astype(jnp.float32)
+                k = jnp.where(keep, k, jnp.broadcast_to(k[0:1, :], (16, HD)))
+                kbuf[edge, :] = k.astype(jnp.bfloat16)
+                v = jnp.where(keep, vbuf[edge, 0:HD].astype(jnp.float32), 0.0)
+                vbuf[edge, 0:HD] = v.astype(jnp.bfloat16)
+                vbuf[edge, HD : 2 * HD] = jnp.where(keep, lead, 0.0).astype(jnp.bfloat16)
 
             return off + ((count + 15) // 16) * 16
 
         off = lax.fori_loop(0, counts[i], pack, off)
         base += counts[i]
     at = pl.ds(pl.multiple_of(off, 16), WIDTH)
-    kbuf[at, 0:HD] = jnp.zeros((WIDTH, HD), jnp.bfloat16)
-    kbuf[at, HD : 2 * HD] = fill_dead
-    vbuf[at, 0:HD] = jnp.zeros((WIDTH, HD), jnp.bfloat16)
+    k = kbuf[0:16, :].astype(jnp.float32)
+    kbuf[at, :] = jnp.broadcast_to(k[0:1, :], (WIDTH, HD)).astype(jnp.bfloat16)
+    vbuf[at, :] = jnp.zeros((WIDTH, 2 * HD), jnp.bfloat16)
     blocks = (off + WIDTH - 1) // WIDTH
 
     def block(i, track):
         at = pl.ds(pl.multiple_of(i * WIDTH, WIDTH), WIDTH)
         for t in range(TILES):
             rows = slice(t * TILE, (t + 1) * TILE)
-            p = jnp.exp2(dot_t(q1[rows, :], kbuf[at, :]) * SCALE).astype(jnp.bfloat16)
+            m = jnp.concatenate([m1[rows, :]] * (WIDTH // HD), axis=1)
+            p = jnp.exp2(dot_t(qs[rows, :], kbuf[at, :]) * SCALE - m).astype(jnp.bfloat16)
             track = jnp.maximum(
                 track, jnp.max(by_lanes(jnp.maximum, p).reshape(TILE // 16, 16, HD), axis=0)
             )
@@ -210,17 +196,14 @@
 
             def highest(i, top, rows=rows):
                 at = pl.ds(pl.multiple_of(i * WIDTH, WIDTH), WIDTH)
-                return jnp.maximum(top, by_lanes(jnp.maximum, dot_t(q0[rows, :], kbuf[at, :])))
-
-            top = lax.fori_loop(0, blocks, highest, jnp.zeros((TILE, HD), jnp.float32))
-            rise = jnp.max(top, axis=1, keepdims=True)
-            columns = q0[rows, HD : 2 * HD].astype(jnp.float32)
-            lane = lanes(TILE)
-            m = -jnp.sum(
-                jnp.where((lane >= 1) & (lane <= 3), columns, 0.0), axis=1, keepdims=True
-            )
-            q1[rows, HD : 2 * HD] = reference_columns(m + rise)
-            acc1[rows, :] = acc0[rows, :] * jnp.exp2(-rise * SCALE)
+                return jnp.maximum(top, by_lanes(jnp.maximum, dot_t(qs[rows, :], kbuf[at, :])))
+
+            top = lax.fori_loop(0, blocks, highest, jnp.full((TILE, HD), DEAD, jnp.float32))
+            old = m0[rows, :]
+            m = jnp.maximum(old, jnp.max(top, axis=1, keepdims=True) * SCALE)
+            factor = jnp.exp2(old - m)
+            m1[rows, :] = m
+            acc1[rows, :] = acc0[rows, :] * jnp.concatenate([factor, factor], axis=1)
         lax.fori_loop(0, blocks, block, none)
 
     if last:
@@ -240,7 +223,7 @@
     vmem = pl.BlockSpec(memory_space=pltpu.VMEM)
     smem = pl.BlockSpec(memory_space=pltpu.SMEM)
     state_shapes = [
-        ((ROWS, 2 * HD), jnp.bfloat16),
+        ((ROWS, HD), jnp.float32),
         ((ROWS, 2 * HD), jnp.float32),
     ]
     scratch_state = [pltpu.VMEM(*s) for s in state_shapes]
@@ -253,7 +236,8 @@
     scratch = (
         (scratch_state if last else [])
         + [
-            pltpu.VMEM((height, 2 * HD), jnp.bfloat16),
+            pltpu.VMEM((ROWS, HD), jnp.bfloat16),
+            pltpu.VMEM((height, HD), jnp.bfloat16),
             pltpu.VMEM((height, 2 * HD), jnp.bfloat16),
             pltpu.SemaphoreType.DMA((len(sources),)),
         ]
@@ -281,7 +265,9 @@
 
 def early_attention(own, beside, count_b, live, arrays, interpret=False):
     state = attention(True, False, count_b[:16], live, own, arrays, interpret)
-    return attention(False, False, count_b[16:48], live, beside, state, interpret)
+    state = (arrays[0], *state)
+    state = attention(False, False, count_b[16:48], live, beside, state, interpret)
+    return (arrays[0], *state)
 
 
 def late_attention(gathered, across, count_a, count_b, live, state, interpret=False):

time: 190 us -> 177 us (0.932)
  the two profiles are of different devices: /device:TPU:471 before, /device:TPU:486 now
where the time goes in v7:
time: 177 us; the launch traced here: 176 us
  Pallas kernels  72.5 us (41%)
  starting transfers between devices  60.5 us (34%)
  waiting for transfers between devices  16.5 us (9%)
  between operations  14.5 us (8%)
  other arithmetic  6.89 us (4%)
  local copies, waits for them, and re-layouts  5.19 us (3%)
    pallas_call x3, Pallas kernels, attention(): pl.pallas_call(kernel, out_shape=out_shape, in_specs=[smem, smem] + [pl.B...  65.7 us
    ppermute x15, starting transfers between devices, shift(): return lax.ppermute(value, 'ctx', pairs)  55.8 us
    ppermute x15, waiting for transfers between devices, shift(): return lax.ppermute(value, 'ctx', pairs)  16.5 us
    pallas_call x1, Pallas kernels, select_pages(): pl.pallas_call(kernel, out_shape=jax.ShapeDtypeStruct((2 * N, PAGE, 2 * H...  5.25 us
    all_to_all x1, starting transfers between devices, body(): lax.all_to_all(outgoing.reshape(2 * N, PAGE, 1, 2 * HD), 'tp', split_axis...  4.65 us
  transfers between devices with their start and end apart: 17, of which 5 were waited for; matrix products, arithmetic and copies ran while one was open for 5% of the time, Pallas kernels for 37%

profile of v7, /device:TPU:486, one launch (start us, length us, event | category | flops | bytes accessed | tf_op | source)
XLA Modules:
  0.0 176.0 jit_solution(719106737303791302)
XLA Ops:
  7.2 1.5 shard_map.95
  8.7 2.4 %collective-permute-start.12 = (bf16[208,128]{1,0:T(8,128)(2,1)}, bf16[208,128]{1,0:T(8,128)(2,1)S(1)}, u32[]{:S(2)}, u32[]{:S(2)}) collective-permute-start(bf16[208,128]{1,0:T(8,128)(2,1)} %get-tuple-element.12), channel_id=1, source_target_pairs={{0,128},{8,136},{16,144},{24,152},{32,160},{40,168},{48,176},{56,1... | collective-permute-start | bytes 159752 | tf_op jit(solution)/shard_map/ppermute | solution.py:45
  11.1 3.5 %collective-permute-start.13 = (bf16[208,128]{1,0:T(8,128)(2,1)}, bf16[208,128]{1,0:T(8,128)(2,1)S(1)}, u32[]{:S(2)}, u32[]{:S(2)}) collective-permute-start(bf16[208,128]{1,0:T(8,128)(2,1)} %get-tuple-element.12), channel_id=1, source_target_pairs={{0,384},{8,392},{16,400},{24,408},{32,416},{40,424},{48,432},{56,4... | collective-permute-start | bytes 159752 | tf_op jit(solution)/shard_map/ppermute | solution.py:45
  14.5 3.3 %collective-permute-start.14 = (bf16[208,128]{1,0:T(8,128)(2,1)}, bf16[208,128]{1,0:T(8,128)(2,1)S(1)}, u32[]{:S(2)}, u32[]{:S(2)}) collective-permute-start(bf16[208,128]{1,0:T(8,128)(2,1)} %get-tuple-element.12), channel_id=1, source_target_pairs={{0,256},{8,264},{16,272},{24,280},{32,288},{40,296},{48,304},{56,3... | collective-permute-start | bytes 159752 | tf_op jit(solution)/shard_map/ppermute | solution.py:45
  18.5 3.8 %collective-permute-done.14 = bf16[208,128]{1,0:T(8,128)(2,1)S(1)} collective-permute-done((bf16[208,128]{1,0:T(8,128)(2,1)}, bf16[208,128]{1,0:T(8,128)(2,1)S(1)}, u32[]{:S(2)}, u32[]{:S(2)}) %collective-permute-start.14) | collective-permute-done | bytes 53280 | tf_op jit(solution)/shard_map/ppermute | solution.py:45
  22.3 1.5 pad_maximum_fusion
  23.8 1.9 %collective-permute-start.1 = (bf16[192,128]{1,0:T(8,128)(2,1)}, bf16[192,128]{1,0:T(8,128)(2,1)S(1)}, u32[]{:S(2)}, u32[]{:S(2)}) collective-permute-start(bf16[192,128]{1,0:T(8,128)(2,1)} %get-tuple-element.10), channel_id=1, source_target_pairs={{0,32},{8,40},{16,48},{24,56},{32,64},{40,72},{48,80},{56,88},{64,... | collective-permute-start | bytes 147464 | tf_op jit(solution)/shard_map/ppermute | solution.py:45
  25.8 7.8 %collective-permute-start = (bf16[192,128]{1,0:T(8,128)(2,1)}, bf16[192,128]{1,0:T(8,128)(2,1)S(1)}, u32[]{:S(2)}, u32[]{:S(2)}) collective-permute-start(bf16[192,128]{1,0:T(8,128)(2,1)} %get-tuple-element.10), channel_id=1, source_target_pairs={{0,96},{8,104},{16,112},{24,120},{32,0},{40,8},{48,16},{56,24},{64... | collective-permute-start | bytes 147464 | tf_op jit(solution)/shard_map/ppermute | solution.py:45
  35.0 2.4 %collective-permute-start.2 = (bf16[96,128]{1,0:T(8,128)(2,1)S(1)}, bf16[96,128]{1,0:T(8,128)(2,1)S(1)}, u32[]{:S(2)}, u32[]{:S(2)}) collective-permute-start(bf16[96,128]{1,0:T(8,128)(2,1)S(1)} %slice.36), channel_id=1, source_target_pairs={{0,32},{8,40},{16,48},{24,56},{32,64},{40,72},{48,80},{56,88},{64,... | collective-permute-start | bytes 73736 | tf_op jit(solution)/shard_map/ppermute | solution.py:45
  37.5 7.3 %collective-permute-start.3 = (bf16[96,128]{1,0:T(8,128)(2,1)S(1)}, bf16[96,128]{1,0:T(8,128)(2,1)S(1)}, u32[]{:S(2)}, u32[]{:S(2)}) collective-permute-start(bf16[96,128]{1,0:T(8,128)(2,1)S(1)} %slice.37), channel_id=1, source_target_pairs={{0,96},{8,104},{16,112},{24,120},{32,0},{40,8},{48,16},{56,24},{64... | collective-permute-start | bytes 73736 | tf_op jit(solution)/shard_map/ppermute | solution.py:45
  44.8 0.8 constant_dynamic-update-slice_fusion.6
  45.6 0.9 pad_maximum_fusion.3
  46.5 1.9 %collective-permute-start.6 = (bf16[2,192,128]{2,1,0:T(8,128)(2,1)S(1)}, bf16[2,192,128]{2,1,0:T(8,128)(2,1)S(1)}, u32[]{:S(2)}, u32[]{:S(2)}) collective-permute-start(bf16[2,192,128]{2,1,0:T(8,128)(2,1)S(1)} %get-tuple-element.25), channel_id=1, source_target_pairs={{0,16},{8,24},{16,32},{24,40},{32,48},{40,56},{48,64},{56,72},{64,... | collective-permute-start | bytes 294920 | tf_op jit(solution)/shard_map/ppermute | solution.py:45
  48.5 4.8 %collective-permute-start.7 = (bf16[2,192,128]{2,1,0:T(8,128)(2,1)S(1)}, bf16[2,192,128]{2,1,0:T(8,128)(2,1)S(1)}, u32[]{:S(2)}, u32[]{:S(2)}) collective-permute-start(bf16[2,192,128]{2,1,0:T(8,128)(2,1)S(1)} %get-tuple-element.24), channel_id=1, source_target_pairs={{0,112},{8,120},{16,0},{24,8},{32,16},{40,24},{48,32},{56,40},{64,... | collective-permute-start | bytes 294920 | tf_op jit(solution)/shard_map/ppermute | solution.py:45
  53.3 0.8 pad_maximum_fusion.1
  54.2 2.7 %collective-permute-start.4 = (bf16[4,192,128]{2,1,0:T(8,128)(2,1)S(1)}, bf16[4,192,128]{2,1,0:T(8,128)(2,1)S(1)}, u32[]{:S(2)}, u32[]{:S(2)}) collective-permute-start(bf16[4,192,128]{2,1,0:T(8,128)(2,1)S(1)} %pad_maximum_fusion.1), channel_id=1, source_target_pairs={{0,8},{8,16},{16,24},{24,32},{32,40},{40,48},{48,56},{56,64},{64,7... | collective-permute-start | bytes 589832 | tf_op jit(solution)/shard_map/ppermute | solution.py:45
  56.9 3.2 %collective-permute-start.5 = (bf16[4,192,128]{2,1,0:T(8,128)(2,1)S(1)}, bf16[4,192,128]{2,1,0:T(8,128)(2,1)S(1)}, u32[]{:S(2)}, u32[]{:S(2)}) collective-permute-start(bf16[4,192,128]{2,1,0:T(8,128)(2,1)S(1)} %pad_maximum_fusion.1), channel_id=1, source_target_pairs={{0,120},{8,0},{16,8},{24,16},{32,24},{40,32},{48,40},{56,48},{64,5... | collective-permute-start | bytes 589832 | tf_op jit(solution)/shard_map/ppermute | solution.py:45
  60.1 4.6 %collective-permute-done.4 = bf16[4,192,128]{2,1,0:T(8,128)(2,1)S(1)} collective-permute-done((bf16[4,192,128]{2,1,0:T(8,128)(2,1)S(1)}, bf16[4,192,128]{2,1,0:T(8,128)(2,1)S(1)}, u32[]{:S(2)}, u32[]{:S(2)}) %collective-permute-start.4) | collective-permute-done | bytes 196640 | tf_op jit(solution)/shard_map/ppermute | solution.py:45
  64.7 3.8 %collective-permute-done.5 = bf16[4,192,128]{2,1,0:T(8,128)(2,1)S(1)} collective-permute-done((bf16[4,192,128]{2,1,0:T(8,128)(2,1)S(1)}, bf16[4,192,128]{2,1,0:T(8,128)(2,1)S(1)}, u32[]{:S(2)}, u32[]{:S(2)}) %collective-permute-start.5) | collective-permute-done | bytes 196640 | tf_op jit(solution)/shard_map/ppermute | solution.py:45
  68.7 2.7 %collective-permute-start.10 = (bf16[16,192,128]{2,1,0:T(8,128)(2,1)S(1)}, bf16[16,192,128]{2,1,0:T(8,128)(2,1)S(1)}, u32[]{:S(2)}, u32[]{:S(2)}) collective-permute-start(bf16[16,192,128]{2,1,0:T(8,128)(2,1)S(1)} %constant_dynamic-update-slice_fusion.refs_2_), channel_id=1, source_target_pairs={{0,384},{8,392},{16,400},{24,408},{32,416},{40,424},{48,432},{56,4... | collective-permute-start | bytes 2359304 | tf_op jit(solution)/shard_map/ppermute | solution.py:45
  71.4 4.3 %collective-permute-start.8 = (bf16[16,192,128]{2,1,0:T(8,128)(2,1)S(1)}, bf16[16,192,128]{2,1,0:T(8,128)(2,1)S(1)}, u32[]{:S(2)}, u32[]{:S(2)}) collective-permute-start(bf16[16,192,128]{2,1,0:T(8,128)(2,1)S(1)} %constant_dynamic-update-slice_fusion.refs_2_), channel_id=1, source_target_pairs={{0,128},{8,136},{16,144},{24,152},{32,160},{40,168},{48,176},{56,1... | collective-permute-start | bytes 2359304 | tf_op jit(solution)/shard_map/ppermute | solution.py:45
  78.3 7.0 %shard_map.96 = (f32[1536,128]{1,0:T(8,128)}, f32[1536,256]{1,0:T(8,128)}) custom-call(s32[16]{0:T(128)} %get-tuple-element.28.refs_0_, s32[1]{0:T(128)} %bitcast.5.refs_1_, bf16[16,192,128]{2,1,0:T(8,128)(2,1)} %copy-done.2, bf16[192,1024]{1,0:T(8,128)(2,1)} %refs_5_.3, bf16[192,128]{1,0:T(8,128)(2,1)} %refs_4_.2, bf16[192,128]{1,0:T(8,128)(2,1)} %refs_5_.2), custom_call_target="tpu_custom_call" | custom-call | flops 2415919104 | bytes 8388608 | tf_op jit(solution)/shard_map/pallas_call | solution.py:251
  85.3 3.6 %collective-permute-done.8.refs_2_ = bf16[16,192,128]{2,1,0:T(8,128)(2,1)S(1)} collective-permute-done((bf16[16,192,128]{2,1,0:T(8,128)(2,1)S(1)}, bf16[16,192,128]{2,1,0:T(8,128)(2,1)S(1)}, u32[]{:S(2)}, u32[]{:S(2)}) %collective-permute-start.8) | collective-permute-done | bytes 786464 | tf_op jit(solution)/shard_map/ppermute | solution.py:45
  88.9 5.6 %collective-permute-start.9 = (bf16[8,192,128]{2,1,0:T(8,128)(2,1)S(1)}, bf16[8,192,128]{2,1,0:T(8,128)(2,1)S(1)}, u32[]{:S(2)}, u32[]{:S(2)}) collective-permute-start(bf16[8,192,128]{2,1,0:T(8,128)(2,1)S(1)} %slice.38), channel_id=1, source_target_pairs={{0,128},{8,136},{16,144},{24,152},{32,160},{40,168},{48,176},{56,1... | collective-permute-start | bytes 1179656 | tf_op jit(solution)/shard_map/ppermute | solution.py:45
  94.6 1.9 %collective-permute-start.11 = (bf16[8,192,128]{2,1,0:T(8,128)(2,1)S(1)}, bf16[8,192,128]{2,1,0:T(8,128)(2,1)S(1)}, u32[]{:S(2)}, u32[]{:S(2)}) collective-permute-start(bf16[8,192,128]{2,1,0:T(8,128)(2,1)S(1)} %slice.39), channel_id=1, source_target_pairs={{0,384},{8,392},{16,400},{24,408},{32,416},{40,424},{48,432},{56,4... | collective-permute-start | bytes 1179656 | tf_op jit(solution)/shard_map/ppermute | solution.py:45
  96.5 11.7 %shard_map.97 = (f32[1536,128]{1,0:T(8,128)}, f32[1536,256]{1,0:T(8,128)}) custom-call(s32[32]{0:T(128)} %slice.33.refs_0_, s32[1]{0:T(128)} %bitcast.5.refs_1_, bf16[16,192,128]{2,1,0:T(8,128)(2,1)} %copy-done.1, bf16[16,192,128]{2,1,0:T(8,128)(2,1)} %copy-done, bf16[192,1024]{1,0:T(8,128)(2,1)} %refs_5_.3, f32[1536,128]{1,0:T(8,128)} %get-tuple-element.14.refs_5_, ...), custom_call_target="tpu_custom_call" | custom-call | flops 4831838208 | bytes 8388608 | tf_op jit(solution)/shard_map/pallas_call | solution.py:251
  108.2 0.9 slice.40
  110.5 0.7 copy-done.3
  111.4 5.2 %shard_map.99 = bf16[128,2,256]{2,1,0:T(2,128)(2,1)} custom-call(s32[128]{0:T(128)} %get-tuple-element.27.refs_0_, s32[128]{0:T(128)} %get-tuple-element.26.refs_1_, f32[1536,128]{1,0:T(8,128)} %get-tuple-element.16.refs_6_.refs_2_, bf16[1536,2,128]{2,1,0:T(2,128)(2,1)} %bitcast.41, bf16[1536,2,128]{2,1,0:T(2,128)(2,1)} %bitcast.40, ...), custom_call_target="tpu_custom_call" | custom-call | bytes 8388608 | tf_op jit(solution)/shard_map/pallas_call | solution.py:312
  116.6 4.7 %all-to-all-start = ((bf16[128,2,1,256]{3,1,2,0:T(2,128)(2,1)}), bf16[128,2,1,256]{3,1,2,0:T(2,128)(2,1)S(1)}, u32[]{:S(2)}, u32[]{:S(2)}) async-start(bf16[128,2,1,256]{3,1,2,0:T(2,128)(2,1)} %bitcast.46), calls=%async_computation | async-start | bytes 262144 | tf_op jit(solution)/shard_map/all_to_all | solution.py:410
  121.3 47.1 %shard_map.98 = bf16[192,1024]{1,0:T(8,128)(2,1)} custom-call(s32[80]{0:T(128)} %pad_add_fusion.1.refs_0_, s32[1]{0:T(128)} %bitcast.5.refs_1_, bf16[8,192,128]{2,1,0:T(8,128)(2,1)} %copy-done.3, bf16[8,192,128]{2,1,0:T(8,128)(2,1)} %copy-done.4, bf16[64,208,128]{2,1,0:T(8,128)(2,1)} %all-gather.3.cloned.1.call-done.refs_4_, bf16[192,1024]{1,0:T(8,128)(2,1)} %refs_5_.3, ...), custom_call_target="tpu_custom_call" | custom-call | flops 12079595520 | bytes 8388608 | tf_op jit(solution)/shard_map/pallas_call | solution.py:251
  168.5 0.7 copy.26
  (61 shorter events, 6.4 us)
Async XLA Ops:
  7.2 101.0 %all-gather.3.cloned.1.call-start = ((), (), s32[]{:S(2)}) async-start(), calls=%async_computation.1 | async-start | bytes 3620864 | tf_op jit(solution)/shard_map/all_gather | solution.py:49
  8.7 9.2 %collective-permute-start.12 = (bf16[208,128]{1,0:T(8,128)(2,1)}, bf16[208,128]{1,0:T(8,128)(2,1)S(1)}, u32[]{:S(2)}, u32[]{:S(2)}) collective-permute-start(bf16[208,128]{1,0:T(8,128)(2,1)} %get-tuple-element.12), channel_id=1, source_target_pairs={{0,128},{8,136},{16,144},{24,152},{32,160},{40,168},{48,176},{56,1... | collective-permute-start | bytes 159752 | tf_op jit(solution)/shard_map/ppermute | solution.py:45
  11.1 7.4 %collective-permute-start.13 = (bf16[208,128]{1,0:T(8,128)(2,1)}, bf16[208,128]{1,0:T(8,128)(2,1)S(1)}, u32[]{:S(2)}, u32[]{:S(2)}) collective-permute-start(bf16[208,128]{1,0:T(8,128)(2,1)} %get-tuple-element.12), channel_id=1, source_target_pairs={{0,384},{8,392},{16,400},{24,408},{32,416},{40,424},{48,432},{56,4... | collective-permute-start | bytes 159752 | tf_op jit(solution)/shard_map/ppermute | solution.py:45
  14.5 7.7 %collective-permute-start.14 = (bf16[208,128]{1,0:T(8,128)(2,1)}, bf16[208,128]{1,0:T(8,128)(2,1)S(1)}, u32[]{:S(2)}, u32[]{:S(2)}) collective-permute-start(bf16[208,128]{1,0:T(8,128)(2,1)} %get-tuple-element.12), channel_id=1, source_target_pairs={{0,256},{8,264},{16,272},{24,280},{32,288},{40,296},{48,304},{56,3... | collective-permute-start | bytes 159752 | tf_op jit(solution)/shard_map/ppermute | solution.py:45
  22.3 53.5 %copy-start.5 = (s32[64]{0:T(128)S(1)}, s32[64]{0:T(128)}, u32[]{:S(2)}) copy-start(s32[64]{0:T(128)} %param.11) | copy-start | bytes 772
  22.3 54.3 %copy-start.6 = (s32[64]{0:T(128)S(1)}, s32[64]{0:T(128)}, u32[]{:S(2)}) copy-start(s32[64]{0:T(128)} %constant.103.clone) | copy-start | bytes 772
  23.8 11.2 %collective-permute-start.1 = (bf16[192,128]{1,0:T(8,128)(2,1)}, bf16[192,128]{1,0:T(8,128)(2,1)S(1)}, u32[]{:S(2)}, u32[]{:S(2)}) collective-permute-start(bf16[192,128]{1,0:T(8,128)(2,1)} %get-tuple-element.10), channel_id=1, source_target_pairs={{0,32},{8,40},{16,48},{24,56},{32,64},{40,72},{48,80},{56,88},{64,... | collective-permute-start | bytes 147464 | tf_op jit(solution)/shard_map/ppermute | solution.py:45
  25.8 11.7 %collective-permute-start = (bf16[192,128]{1,0:T(8,128)(2,1)}, bf16[192,128]{1,0:T(8,128)(2,1)S(1)}, u32[]{:S(2)}, u32[]{:S(2)}) collective-permute-start(bf16[192,128]{1,0:T(8,128)(2,1)} %get-tuple-element.10), channel_id=1, source_target_pairs={{0,96},{8,104},{16,112},{24,120},{32,0},{40,8},{48,16},{56,24},{64... | collective-permute-start | bytes 147464 | tf_op jit(solution)/shard_map/ppermute | solution.py:45
  35.0 18.3 %collective-permute-start.2 = (bf16[96,128]{1,0:T(8,128)(2,1)S(1)}, bf16[96,128]{1,0:T(8,128)(2,1)S(1)}, u32[]{:S(2)}, u32[]{:S(2)}) collective-permute-start(bf16[96,128]{1,0:T(8,128)(2,1)S(1)} %slice.36), channel_id=1, source_target_pairs={{0,32},{8,40},{16,48},{24,56},{32,64},{40,72},{48,80},{56,88},{64,... | collective-permute-start | bytes 73736 | tf_op jit(solution)/shard_map/ppermute | solution.py:45
  37.5 15.8 %collective-permute-start.3 = (bf16[96,128]{1,0:T(8,128)(2,1)S(1)}, bf16[96,128]{1,0:T(8,128)(2,1)S(1)}, u32[]{:S(2)}, u32[]{:S(2)}) collective-permute-start(bf16[96,128]{1,0:T(8,128)(2,1)S(1)} %slice.37), channel_id=1, source_target_pairs={{0,96},{8,104},{16,112},{24,120},{32,0},{40,8},{48,16},{56,24},{64... | collective-permute-start | bytes 73736 | tf_op jit(solution)/shard_map/ppermute | solution.py:45
  46.5 22.1 %collective-permute-start.6 = (bf16[2,192,128]{2,1,0:T(8,128)(2,1)S(1)}, bf16[2,192,128]{2,1,0:T(8,128)(2,1)S(1)}, u32[]{:S(2)}, u32[]{:S(2)}) collective-permute-start(bf16[2,192,128]{2,1,0:T(8,128)(2,1)S(1)} %get-tuple-element.25), channel_id=1, source_target_pairs={{0,16},{8,24},{16,32},{24,40},{32,48},{40,56},{48,64},{56,72},{64,... | collective-permute-start | bytes 294920 | tf_op jit(solution)/shard_map/ppermute | solution.py:45
  48.5 20.2 %collective-permute-start.7 = (bf16[2,192,128]{2,1,0:T(8,128)(2,1)S(1)}, bf16[2,192,128]{2,1,0:T(8,128)(2,1)S(1)}, u32[]{:S(2)}, u32[]{:S(2)}) collective-permute-start(bf16[2,192,128]{2,1,0:T(8,128)(2,1)S(1)} %get-tuple-element.24), channel_id=1, source_target_pairs={{0,112},{8,120},{16,0},{24,8},{32,16},{40,24},{48,32},{56,40},{64,... | collective-permute-start | bytes 294920 | tf_op jit(solution)/shard_map/ppermute | solution.py:45
  54.2 10.5 %collective-permute-start.4 = (bf16[4,192,128]{2,1,0:T(8,128)(2,1)S(1)}, bf16[4,192,128]{2,1,0:T(8,128)(2,1)S(1)}, u32[]{:S(2)}, u32[]{:S(2)}) collective-permute-start(bf16[4,192,128]{2,1,0:T(8,128)(2,1)S(1)} %pad_maximum_fusion.1), channel_id=1, source_target_pairs={{0,8},{8,16},{16,24},{24,32},{32,40},{40,48},{48,56},{56,64},{64,7... | collective-permute-start | bytes 589832 | tf_op jit(solution)/shard_map/ppermute | solution.py:45
  56.9 11.7 %collective-permute-start.5 = (bf16[4,192,128]{2,1,0:T(8,128)(2,1)S(1)}, bf16[4,192,128]{2,1,0:T(8,128)(2,1)S(1)}, u32[]{:S(2)}, u32[]{:S(2)}) collective-permute-start(bf16[4,192,128]{2,1,0:T(8,128)(2,1)S(1)} %pad_maximum_fusion.1), channel_id=1, source_target_pairs={{0,120},{8,0},{16,8},{24,16},{32,24},{40,32},{48,40},{56,48},{64,5... | collective-permute-start | bytes 589832 | tf_op jit(solution)/shard_map/ppermute | solution.py:45
  68.7 9.7 %copy-start.2 = (bf16[16,192,128]{2,1,0:T(8,128)(2,1)}, bf16[16,192,128]{2,1,0:T(8,128)(2,1)S(1)}, u32[]{:S(2)}) copy-start(bf16[16,192,128]{2,1,0:T(8,128)(2,1)S(1)} %constant_dynamic-update-slice_fusion.refs_2_) | copy-start | bytes 2359300
  68.7 25.9 %collective-permute-start.10 = (bf16[16,192,128]{2,1,0:T(8,128)(2,1)S(1)}, bf16[16,192,128]{2,1,0:T(8,128)(2,1)S(1)}, u32[]{:S(2)}, u32[]{:S(2)}) collective-permute-start(bf16[16,192,128]{2,1,0:T(8,128)(2,1)S(1)} %constant_dynamic-update-slice_fusion.refs_2_), channel_id=1, source_target_pairs={{0,384},{8,392},{16,400},{24,408},{32,416},{40,424},{48,432},{56,4... | collective-permute-start | bytes 2359304 | tf_op jit(solution)/shard_map/ppermute | solution.py:45
  71.4 17.5 %collective-permute-start.8 = (bf16[16,192,128]{2,1,0:T(8,128)(2,1)S(1)}, bf16[16,192,128]{2,1,0:T(8,128)(2,1)S(1)}, u32[]{:S(2)}, u32[]{:S(2)}) collective-permute-start(bf16[16,192,128]{2,1,0:T(8,128)(2,1)S(1)} %constant_dynamic-update-slice_fusion.refs_2_), channel_id=1, source_target_pairs={{0,128},{8,136},{16,144},{24,152},{32,160},{40,168},{48,176},{56,1... | collective-permute-start | bytes 2359304 | tf_op jit(solution)/shard_map/ppermute | solution.py:45
  88.9 7.6 %copy-start.1 = (bf16[16,192,128]{2,1,0:T(8,128)(2,1)}, bf16[16,192,128]{2,1,0:T(8,128)(2,1)S(1)}, u32[]{:S(2)}) copy-start(bf16[16,192,128]{2,1,0:T(8,128)(2,1)S(1)} %collective-permute-done.8.refs_2_) | copy-start | bytes 2359300
  88.9 21.6 %collective-permute-start.9 = (bf16[8,192,128]{2,1,0:T(8,128)(2,1)S(1)}, bf16[8,192,128]{2,1,0:T(8,128)(2,1)S(1)}, u32[]{:S(2)}, u32[]{:S(2)}) collective-permute-start(bf16[8,192,128]{2,1,0:T(8,128)(2,1)S(1)} %slice.38), channel_id=1, source_target_pairs={{0,128},{8,136},{16,144},{24,152},{32,160},{40,168},{48,176},{56,1... | collective-permute-start | bytes 1179656 | tf_op jit(solution)/shard_map/ppermute | solution.py:45
  94.5 2.0 %copy-start = (bf16[16,192,128]{2,1,0:T(8,128)(2,1)}, bf16[16,192,128]{2,1,0:T(8,128)(2,1)S(1)}, u32[]{:S(2)}) copy-start(bf16[16,192,128]{2,1,0:T(8,128)(2,1)S(1)} %collective-permute-done.10.refs_3_) | copy-start | bytes 2359300
  94.6 15.9 %collective-permute-start.11 = (bf16[8,192,128]{2,1,0:T(8,128)(2,1)S(1)}, bf16[8,192,128]{2,1,0:T(8,128)(2,1)S(1)}, u32[]{:S(2)}, u32[]{:S(2)}) collective-permute-start(bf16[8,192,128]{2,1,0:T(8,128)(2,1)S(1)} %slice.39), channel_id=1, source_target_pairs={{0,384},{8,392},{16,400},{24,408},{32,416},{40,424},{48,432},{56,4... | collective-permute-start | bytes 1179656 | tf_op jit(solution)/shard_map/ppermute | solution.py:45
  110.5 0.7 copy-start.3
  110.5 0.9 copy-start.4
  116.6 51.8 %all-to-all-start = ((bf16[128,2,1,256]{3,1,2,0:T(2,128)(2,1)}), bf16[128,2,1,256]{3,1,2,0:T(2,128)(2,1)S(1)}, u32[]{:S(2)}, u32[]{:S(2)}) async-start(bf16[128,2,1,256]{3,1,2,0:T(2,128)(2,1)} %bitcast.46), calls=%async_computation | async-start | bytes 262144 | tf_op jit(solution)/shard_map/all_to_all | solution.py:410
Sparse Core Ops, SparseCore 0:
  24.0 77.9 all-gather.2
